TPU v7x, 128 devices: a whole 4x4x4 slice. The times are simulated.
128 devices in a mesh: outer: 16 (over x, y), inner: 8 (over z, core).
Axes of the slice: x: 4, y: 4, z: 4, core: 2. Of those that a mesh axis runs over, the one named last changes fastest.
Arguments:
- tokens: bfloat16 [2048, 4096], P(('outer', 'inner')), may hold values from -6 to 6
- out_grad: bfloat16 [2048, 4096], P(('outer', 'inner')), may hold values from -2 to 2
- combine: float32 [2048, 4], P(('outer', 'inner')), may hold values from 0.1 to 1
- expert_ids: int32 [2048, 4], P(('outer', 'inner')), may hold values from 0 to 31, all different within a row; in each aligned block of 16 rows (0 to 15, 16 to 31, ...) at most 4 rows name the same one
- gate_weight: bfloat16 [128, 4096, 384], P(('outer', 'inner')), may hold values from -0.09375 to 0.09375
- up_weight: bfloat16 [128, 4096, 384], P(('outer', 'inner')), may hold values from -0.09375 to 0.09375
- down_weight: bfloat16 [128, 384, 4096], P(('outer', 'inner')), may hold values from -0.15625 to 0.15625
Outputs:
- token_grad: bfloat16 [2048, 4096], P(('outer', 'inner'))
- combine_grad: float32 [2048, 4], P(('outer', 'inner'))
- gate_grad: bfloat16 [128, 4096, 384], P(('outer', 'inner'))
- up_grad: bfloat16 [128, 4096, 384], P(('outer', 'inner'))
- down_grad: bfloat16 [128, 384, 4096], P(('outer', 'inner'))
Inputs may be any that keep to these rules, and one draw needn't show every extreme that they name: `expert_ids`: each row names 4 different experts. In the rows of one device no expert is named by more than 4 rows, a bound that some block reaches.
All inputs are finite; a program needn't handle non-finite values.
Results may differ from a plain program's by a relative error of at most 0.018.
Values may be sent and summed in bfloat16 or wider, within the bound.
No kernel may reach another device: no remote copies, remote signals or barrier semaphores. Data moves between devices by JAX's collectives and lax.ppermute only.
A program may use at most 128 MiB of HBM per device.

v0:
```python
import functools

import jax
import jax.numpy as jnp
from jax import lax
from jax.experimental import pallas as pl
from jax.experimental.pallas import tpu as pltpu
from jax.sharding import Mesh
from jax.sharding import PartitionSpec as P

CORES = 2
CAP = 4
SLOTS = CORES * CAP
META = 128
CHIPS = ("outer", "z")
ALL = ("outer", "z", "core")
F32 = jnp.float32
BF16 = jnp.bfloat16
TN = (((0,), (0,)), ((), ()))
NT = (((1,), (1,)), ((), ()))
SMEM = pl.BlockSpec(memory_space=pltpu.SMEM)
HBM = pl.BlockSpec(memory_space=pltpu.HBM)


def dot(a, b, dims=(((1,), (0,)), ((), ()))):
    return lax.dot_general(a, b, dims, preferred_element_type=F32)


def after(x, *others):
    return lax.optimization_barrier((x, *others))


class Loaded:
    def __init__(self, source, target, semaphore):
        self.copy = pltpu.make_async_copy(source, target, semaphore)
        self.target = target
        self.shape = target.shape
        self.waiting = True
        self.copy.start()

    def wait(self):
        if self.waiting:
            self.copy.wait()
            self.waiting = False

    def __getitem__(self, index):
        self.wait()
        return self.target[index]


def call(kernel, name, outs, place, *args, raw=0, direct=0, scratch=(), limit=63 << 20):
    count, given = len(outs) - direct, len(args) - raw

    def body(place_ref, *refs):
        raw_refs, ins, refs = refs[:raw], refs[raw : raw + given], refs[raw + given :]
        out_refs, direct_refs, refs = refs[:count], refs[count : count + direct], refs[count + direct :]
        held, made, refs = refs[:given], refs[given : given + count], refs[given + count :]
        in_sems, out_sems, own = refs[0], refs[1], refs[2:]
        loaded = [Loaded(ins[n], held[n], in_sems.at[n]) for n in range(given)]
        kernel(place_ref, *raw_refs, *loaded, *made, *direct_refs, *own)
        for held_ref in loaded:
            held_ref.wait()
        copies = [pltpu.make_async_copy(made[n], out_refs[n], out_sems.at[n]) for n in range(count)]
        for copy in copies:
            copy.start()
        for copy in copies:
            copy.wait()

    return pl.pallas_call(
        body,
        in_specs=[SMEM] + [HBM] * len(args),
        out_specs=[HBM] * len(outs),
        out_shape=[jax.ShapeDtypeStruct(shape, kind) for shape, kind in outs],
        scratch_shapes=[pltpu.VMEM(x.shape, x.dtype) for x in args[raw:]]
        + [pltpu.VMEM(shape, kind) for shape, kind in outs[:count]]
        + [pltpu.SemaphoreType.DMA((max(given, 1),)), pltpu.SemaphoreType.DMA((max(count, 1),)), *scratch],
        compiler_params=pltpu.CompilerParams(vmem_limit_bytes=limit),
        name=name,
    )(place, *args)


def column(row):
    n = row.shape[1]
    here = lax.broadcasted_iota(jnp.int32, (n, n), 0) == lax.broadcasted_iota(jnp.int32, (n, n), 1)
    return jnp.sum(jnp.where(here, row, 0.0), axis=1, keepdims=True)


def row(column):
    n = column.shape[0]
    here = lax.broadcasted_iota(jnp.int32, (n, n), 0) == lax.broadcasted_iota(jnp.int32, (n, n), 1)
    return jnp.sum(jnp.where(here, column, 0.0), axis=0, keepdims=True)


def columns(start, size):
    return pl.ds(pl.multiple_of(start, size), size)


def pack_kernel(place_ref, tok_ref, grad_ref, ids_ref, comb_ref, *out_refs):
    tok, width = tok_ref.shape
    me = place_ref[0]
    lane = lax.broadcasted_iota(jnp.int32, (tok, META), 1)
    ids, comb = ids_ref[...].astype(F32), comb_ref[...]
    high = comb.astype(BF16).astype(F32)
    low = comb - high
    meta = jnp.zeros((tok, META), F32)
    topk = ids.shape[0]
    for part, value in enumerate((ids, high, low)):
        for k in range(topk):
            meta = jnp.where(lane == part * topk + k, column(value[k : k + 1, :]), meta)
    meta = meta.astype(BF16)
    for j, out_ref in enumerate(out_refs):
        piece = out_ref.shape[1] - META
        which = (me % CORES) ^ j
        out_ref[:tok, :piece] = tok_ref[:, columns(which * piece, piece)]
        out_ref[tok:, :piece] = grad_ref[:, columns(which * piece, piece)]
        out_ref[:tok, piece:] = meta
        out_ref[tok:, piece:] = jnp.zeros_like(meta)


def slot_mask(core, meta, lines):
    tokens = meta.shape[0]
    own = tokens // CORES
    line = lax.broadcasted_iota(jnp.int32, (tokens, lines), 1)
    expert = (line // (2 * SLOTS)).astype(F32)
    named = [jnp.where(meta[:, k : k + 1] == expert, 1.0, 0.0) for k in range(4)]
    total = named[0] + named[1] + named[2] + named[3]
    after = lax.broadcasted_iota(jnp.int32, (tokens, tokens), 0)
    before = lax.broadcasted_iota(jnp.int32, (tokens, tokens), 1)
    earlier = jnp.where((before < after) & (before // own == after // own), 1.0, 0.0)
    rank = dot(earlier.astype(BF16), total.astype(BF16)).astype(jnp.int32)
    token = lax.broadcasted_iota(jnp.int32, (tokens, lines), 0)
    place = rank + ((token // own) ^ core) * CAP
    mask = jnp.where((total > 0.0) & (place == line % SLOTS), 1.0, 0.0)
    return mask, named


def meta_of(refs, tok):
    width = refs[0].shape[1] - META
    return jnp.concatenate([ref[:tok, width:] for ref in refs], axis=0).astype(F32)


def build_kernel(scaled, place_ref, own_ref, other_ref, out_ref):
    refs = (own_ref, other_ref)
    lines, half = out_ref.shape
    tok = own_ref.shape[0] // 2
    meta = meta_of(refs, tok)
    mask, named = slot_mask(place_ref[0], meta, lines)
    pick = mask.astype(BF16)
    if scaled:
        ones = jnp.ones((mask.shape[0], META), BF16)
        weight = jnp.zeros((lines, META), F32)
        for part in (1, 2):
            chosen = sum(named[k] * meta[:, part * 4 + k : part * 4 + k + 1] for k in range(4)) * mask
            weight += dot(chosen.astype(BF16), ones, TN)
        weight = weight[:, :1]
    first = tok if scaled else 0
    step = 512
    for at in range(0, half, step):
        found = dot(pick, jnp.concatenate([ref[first : first + tok, at : at + step] for ref in refs], axis=0), TN)
        out_ref[:, at : at + step] = (found * weight if scaled else found).astype(BF16)


def gate_up_kernel(place_ref, gate_hbm, up_hbm, own_ref, other_ref, out_ref, first_ref, sems):
    core = place_ref[0]
    half = own_ref.shape[1]
    parts, _, both = first_ref.shape
    ff, quarter = both // 2, CORES * half // parts
    copies = []
    for n in range(parts):
        at = columns(((core ^ (n * CORES // parts)) * half) + (n * quarter) % half, quarter)
        copies += [
            pltpu.make_async_copy(gate_hbm.at[0, at, :], first_ref.at[n, :, pl.ds(0, ff)], sems.at[2 * n]),
            pltpu.make_async_copy(up_hbm.at[0, at, :], first_ref.at[n, :, pl.ds(ff, ff)], sems.at[2 * n + 1]),
        ]
    for copy in copies:
        copy.start()
    pre = 0.0
    for n in range(parts):
        ref, at = (own_ref, other_ref)[n * CORES // parts], (n * quarter) % half
        rows = ref[:, at : at + quarter]
        copies[2 * n].wait()
        copies[2 * n + 1].wait()
        pre += dot(rows, first_ref[n])
    out_ref[...] = pre


def back_product(down_hbm, which, grads_ref, down_ref, sems):
    half = grads_ref.shape[1]
    step = half // CORES
    copies = []
    for n in range(CORES):
        at = columns(which * half + n * step, step)
        copies.append(pltpu.make_async_copy(down_hbm.at[0, :, at], down_ref.at[n], sems.at[n]))
    for copy in copies:
        copy.start()
    scaled = 0.0
    for n, copy in enumerate(copies):
        grads = grads_ref[:, n * step : (n + 1) * step]
        copy.wait()
        scaled += dot(grads, down_ref[n], NT)
    return scaled


def back_early_kernel(place_ref, down_hbm, own_ref, out_ref, down_ref, sems):
    out_ref[...] = back_product(down_hbm, place_ref[0], own_ref, down_ref, sems)


def back_late_kernel(place_ref, down_hbm, other_ref, sum_ref, pre_ref, deltas_ref, hidden_ref, score_ref, down_ref, sems):
    scaled = back_product(down_hbm, 1 - place_ref[0], other_ref, down_ref, sems) + sum_ref[...]
    ff = hidden_ref.shape[1]
    gate_pre, up_pre = pre_ref[:, :ff], pre_ref[:, ff:]
    sigmoid_gate = jax.nn.sigmoid(gate_pre)
    active = gate_pre * sigmoid_gate
    hidden = (active * up_pre).astype(BF16)
    score = jnp.sum(scaled * hidden.astype(F32), axis=1, keepdims=True)
    deltas_ref[:, :ff] = (scaled * up_pre * sigmoid_gate * (1.0 + gate_pre * (1.0 - sigmoid_gate))).astype(BF16)
    deltas_ref[:, ff:] = (scaled * active).astype(BF16)
    hidden_ref[...] = hidden
    score_ref[...] = jnp.broadcast_to(score, score_ref.shape).astype(BF16)


def lend_kernel(place_ref, gate_hbm, up_hbm, out_ref, sems):
    half, both = out_ref.shape
    ff = both // 2
    at = columns((1 - place_ref[0]) * half, half)
    copies = [
        pltpu.make_async_copy(gate_hbm.at[0, at, :], out_ref.at[:, pl.ds(0, ff)], sems.at[0]),
        pltpu.make_async_copy(up_hbm.at[0, at, :], out_ref.at[:, pl.ds(ff, ff)], sems.at[1]),
    ]
    for copy in copies:
        copy.start()
    for copy in copies:
        copy.wait()


def parts_kernel(place_ref, gate_hbm, up_hbm, lent_hbm, own_ref, other_ref, score_ref, out_ref, weight_ref, sems):
    steps, _, step, both = weight_ref.shape
    half, ff = steps * step, both // 2
    start = place_ref[0] * half
    copies = []
    for n in range(steps):
        at = columns(start + n * step, step)
        pairs = (
            (gate_hbm.at[0, at, :], weight_ref.at[n, 0, :, pl.ds(0, ff)]),
            (up_hbm.at[0, at, :], weight_ref.at[n, 0, :, pl.ds(ff, ff)]),
            (lent_hbm.at[pl.ds(n * step, step), :], weight_ref.at[n, 1]),
        )
        copies.append([pltpu.make_async_copy(*pair, sems.at[3 * n + k]) for k, pair in enumerate(pairs)])
    for some in copies:
        for copy in some:
            copy.start()
    out_ref[:, half:] = score_ref[...]
    own, other = own_ref[...], other_ref[...]
    for n, some in enumerate(copies):
        for copy in some:
            copy.wait()
        part = dot(own, weight_ref[n, 0], NT) + dot(other, weight_ref[n, 1], NT)
        out_ref[:, n * step : (n + 1) * step] = part.astype(BF16)


def gather_kernel(place_ref, own_ref, other_ref, back_ref, mark_ref, mine_ref, send_ref):
    lines, total = back_ref.shape
    width = total - META
    tok = own_ref.shape[0] // 2
    mask, named = slot_mask(place_ref[0], meta_of((own_ref, other_ref), tok), lines)
    pick = mask.astype(BF16)
    step = 512
    for at in range(0, width, step):
        part = dot(pick, back_ref[:, at : at + step]).astype(BF16)
        mine_ref[:, at : at + step] = part[:tok]
        send_ref[:, at : at + step] = part[tok:]
    scores = back_ref[:, width:]
    lane = lax.broadcasted_iota(jnp.int32, (mask.shape[0], META), 1)
    found = jnp.zeros((mask.shape[0], META), F32)
    for k in range(4):
        found = jnp.where(lane == k, dot((mask * named[k]).astype(BF16), scores), found)
    mine_ref[:, width:] = found[:tok].astype(BF16)
    send_ref[:, width:] = found[tok:].astype(BF16)


def final_kernel(place_ref, comb_ref, own_ref, other_ref, out_ref, score_ref):
    core = place_ref[0]
    width = own_ref.shape[1] - META
    out_ref[:, columns(core * width, width)] = own_ref[:, :width]
    out_ref[:, columns((1 - core) * width, width)] = other_ref[:, :width]
    score = own_ref[:, width:].astype(F32) + other_ref[:, width:].astype(F32)
    for k in range(comb_ref.shape[0]):
        score_ref[k : k + 1, :] = row(score[:, k : k + 1]) / comb_ref[k : k + 1, :]


def weights_kernel(place_ref, *refs):
    rows_refs, grads_refs = refs[0:2], refs[2:4]
    deltas_ref, hidden_ref, mark_ref, gate_hbm, up_hbm, down_hbm, gate_ref, up_ref, down_ref, sems = refs[4:]
    mark_ref[...] = jnp.zeros_like(mark_ref)
    core = place_ref[0]
    half, step = rows_refs[0].shape[1], gate_ref.shape[1]
    ff = hidden_ref.shape[1]
    deltas = deltas_ref[...]
    copies = []
    for j in range(CORES):
        for at in range(0, half, step):
            n = (j * half + at) // step
            grad = dot(rows_refs[j][:, at : at + step], deltas, TN)
            gate_ref[n] = grad[:, :ff].astype(BF16)
            up_ref[n] = grad[:, ff:].astype(BF16)
            cols = columns((core ^ j) * half + at, step)
            copies += [
                pltpu.make_async_copy(gate_ref.at[n], gate_hbm.at[0, cols, :], sems.at[3 * n]),
                pltpu.make_async_copy(up_ref.at[n], up_hbm.at[0, cols, :], sems.at[3 * n + 1]),
            ]
            for copy in copies[-2:]:
                copy.start()
    hidden = hidden_ref[...].T
    for j in range(CORES):
        for at in range(0, half, step):
            n = (j * half + at) // step
            down_ref[n] = dot(hidden, grads_refs[j][:, at : at + step]).astype(BF16)
            cols = columns((core ^ j) * half + at, step)
            copies.append(pltpu.make_async_copy(down_ref.at[n], down_hbm.at[0, :, cols], sems.at[3 * n + 2]))
            copies[-1].start()
    for copy in copies:
        copy.wait()


def local(tokens, out_grad, combine, expert_ids, gate_weight, up_weight, down_weight):
    tok, width = tokens.shape
    chips = lax.axis_size(CHIPS)
    lines = chips * SLOTS
    ff = gate_weight.shape[2]
    half, quarter = width // CORES, width // CORES // 2
    step = 512
    place = lax.axis_index("core").astype(jnp.int32).reshape(1)

    def swap(x):
        return lax.ppermute(x, "core", [(0, 1), (1, 0)])

    def deliver(x):
        found = lax.all_to_all(x.reshape(chips, SLOTS, x.shape[1]), CHIPS, split_axis=0, concat_axis=0, tiled=True)
        return found.reshape(x.shape)

    own, send = call(
        pack_kernel, "pack", [((2 * tok, half + META), BF16)] * CORES,
        place, tokens, out_grad, expert_ids.T, combine.T,
    )
    messages = (own, swap(send))

    def build(scaled):
        kernel = functools.partial(build_kernel, scaled)
        return call(kernel, "build", [((lines, half), BF16)], place, *messages)[0]

    rows_out = build(False)
    grads_out = build(True)
    lend = call(
        lend_kernel, "lend", [((half, 2 * ff), BF16)], place, gate_weight, up_weight,
        raw=2, scratch=[pltpu.SemaphoreType.DMA((2,))],
    )[0]
    rows, grads_out, lend = after(deliver(rows_out), grads_out, lend)
    lent = swap(lend)
    rows_pair = (rows, swap(rows))
    pre = call(
        gate_up_kernel, "gate_up", [((lines, 2 * ff), F32)], place, gate_weight, up_weight, *rows_pair,
        raw=2, scratch=[pltpu.VMEM((4, quarter, 2 * ff), BF16), pltpu.SemaphoreType.DMA((8,))],
    )[0]
    grads, pre, lent = after(deliver(grads_out), pre, lent)
    grads_pair = (grads, swap(grads))
    scratch = [pltpu.VMEM((CORES, ff, quarter), BF16), pltpu.SemaphoreType.DMA((CORES,))]
    scaled = call(
        back_early_kernel, "back_early", [((lines, ff), F32)], place, down_weight, grads_pair[0], raw=1, scratch=scratch
    )[0]
    other, scaled = after(grads_pair[1], scaled)
    deltas, hidden, score = call(
        back_late_kernel,
        "back_late",
        [((lines, 2 * ff), BF16), ((lines, ff), BF16), ((lines, META), BF16)],
        place, down_weight, other, scaled, pre, raw=1, scratch=scratch,
    )
    parts = call(
        parts_kernel,
        "row_parts",
        [((lines, half + META), BF16)],
        place, gate_weight, up_weight, lent, deltas, swap(deltas), score,
        raw=3,
        scratch=[
            pltpu.VMEM((half // step, 2, step, 2 * ff), BF16),
            pltpu.SemaphoreType.DMA((3 * half // step,)),
        ],
    )[0]
    mark, gate_grad, up_grad, down_grad = call(
        weights_kernel,
        "weight_grads",
        [((8, META), F32), (gate_weight.shape, BF16), (up_weight.shape, BF16), (down_weight.shape, BF16)],
        place, *rows_pair, *grads_pair, deltas, hidden,
        direct=3,
        scratch=[
            pltpu.VMEM((width // step, step, ff), BF16),
            pltpu.VMEM((width // step, step, ff), BF16),
            pltpu.VMEM((width // step, ff, step), BF16),
            pltpu.SemaphoreType.DMA((3 * width // step,)),
        ],
    )
    mine, send = call(
        gather_kernel, "gather_rows", [((tok, half + META), BF16)] * CORES, place, *messages, deliver(parts), mark
    )
    token_grad, combine_grad = call(
        final_kernel, "total", [(tokens.shape, BF16), (combine.shape[::-1], F32)], place, combine.T, mine, swap(send)
    )
    return token_grad, combine_grad.T, gate_grad, up_grad, down_grad


def solution(mesh):
    outer, inner = mesh.devices.shape
    split = Mesh(mesh.devices.reshape(outer, inner // CORES, CORES), ALL)
    flat, deep = P(ALL, None), P(ALL, None, None)
    return jax.shard_map(
        local,
        mesh=split,
        in_specs=(flat, flat, flat, flat, deep, deep, deep),
        out_specs=(flat, flat, deep, deep, deep),
        check_vma=False,
    )
```

profile of v0, /device:TPU:1, one launch (start us, length us, event | category | flops | bytes accessed | tf_op | source)
XLA Modules:
  0.0 153.0 jit_solution(9135701227545269805)
XLA Ops:
  0.6 1.7 %pack.1 = (bf16[32,2176]{1,0:T(8,128)(2,1)}, bf16[32,2176]{1,0:T(8,128)(2,1)}) custom-call(s32[1]{0:T(128)} %bitcast.place_ref, bf16[16,4096]{1,0:T(8,128)(2,1)} %refs_0_.6, bf16[16,4096]{1,0:T(8,128)(2,1)} %refs_1_.4, s32[4,16]{1,0:T(4,128)} %bitcast.15, f32[4,16]{1,0:T(4,128)} %bitcast.13), custom_call_target="tpu_custom_call" | custom-call | tf_op jit(solution)/shard_map/pack/pallas_call | solution.py:69
  2.4 1.5 collective-permute-start
  3.9 1.2 collective-permute-done.refs_1_
  5.1 0.6 copy-done
  5.7 3.3 %build.2 = bf16[512,2048]{1,0:T(8,128)(2,1)} custom-call(s32[1]{0:T(128)} %bitcast.place_ref, bf16[32,2176]{1,0:T(8,128)(2,1)} %get-tuple-element.26.refs_0_, bf16[32,2176]{1,0:T(8,128)(2,1)} %copy-done), custom_call_target="tpu_custom_call" | custom-call | tf_op jit(solution)/shard_map/build/pallas_call | solution.py:69
  9.0 11.5 %all-to-all-start = ((bf16[64,8,2048]{2,1,0:T(8,128)(2,1)}), bf16[64,8,2048]{2,1,0:T(8,128)(2,1)}, u32[]{:S(2)}, u32[]{:S(2)}) async-start(bf16[64,8,2048]{2,1,0:T(8,128)(2,1)} %bitcast.12), calls=%async_computation | async-start | bytes 4194304 | tf_op jit(solution)/shard_map/all_to_all | solution.py:338
  20.5 3.6 %lend.1 = bf16[2048,768]{1,0:T(8,128)(2,1)} custom-call(s32[1]{0:T(128)} %bitcast.place_ref, bf16[1,4096,384]{2,1,0:T(8,128)(2,1)} %refs_0_.11, bf16[1,4096,384]{2,1,0:T(8,128)(2,1)} %refs_1_.7), custom_call_target="tpu_custom_call" | custom-call | tf_op jit(solution)/shard_map/lend/pallas_call | solution.py:69
  24.1 3.4 %build.3 = bf16[512,2048]{1,0:T(8,128)(2,1)} custom-call(s32[1]{0:T(128)} %bitcast.place_ref, bf16[32,2176]{1,0:T(8,128)(2,1)} %get-tuple-element.26.refs_0_, bf16[32,2176]{1,0:T(8,128)(2,1)} %copy-done), custom_call_target="tpu_custom_call" | custom-call | tf_op jit(solution)/shard_map/build/pallas_call | solution.py:69
  27.5 20.4 %all-to-all-done = bf16[64,8,2048]{2,1,0:T(8,128)(2,1)} async-done(((bf16[64,8,2048]{2,1,0:T(8,128)(2,1)}), bf16[64,8,2048]{2,1,0:T(8,128)(2,1)}, u32[]{:S(2)}, u32[]{:S(2)}) %all-to-all-start) | async-done | bytes 2097184 | tf_op jit(solution)/shard_map/all_to_all | solution.py:338
  47.9 3.0 %collective-permute-start.2 = (bf16[2048,768]{1,0:T(8,128)(2,1)}, bf16[2048,768]{1,0:T(8,128)(2,1)}, u32[]{:S(2)}, u32[]{:S(2)}) collective-permute-start(bf16[2048,768]{1,0:T(8,128)(2,1)} %lend.1), channel_id=1, source_target_pairs={{0,1},{1,0},{2,3},{3,2},{4,5},{5,4},{6,7},{7,6},{8,9},{9,8},{10,11... | collective-permute-start | bytes 9437192 | tf_op jit(solution)/shard_map/ppermute | solution.py:335
  51.0 0.0 collective-permute-start.1
  51.0 5.6 %all-to-all-start.1 = ((bf16[64,8,2048]{2,1,0:T(8,128)(2,1)}), bf16[64,8,2048]{2,1,0:T(8,128)(2,1)}, u32[]{:S(2)}, u32[]{:S(2)}) async-start(bf16[64,8,2048]{2,1,0:T(8,128)(2,1)} %bitcast.11), calls=%async_computation.1 | async-start | bytes 4194304 | tf_op jit(solution)/shard_map/all_to_all | solution.py:338
  56.6 3.1 %collective-permute-done.1.refs_3_.refs_1_ = bf16[512,2048]{1,0:T(8,128)(2,1)} collective-permute-done((bf16[512,2048]{1,0:T(8,128)(2,1)}, bf16[512,2048]{1,0:T(8,128)(2,1)}, u32[]{:S(2)}, u32[]{:S(2)}) %collective-permute-start.1) | collective-permute-done | bytes 2097184 | tf_op jit(solution)/shard_map/ppermute | solution.py:335
  59.6 9.2 %gate_up.1.refs_3_ = f32[512,768]{1,0:T(8,128)} custom-call(s32[1]{0:T(128)} %bitcast.place_ref, bf16[1,4096,384]{2,1,0:T(8,128)(2,1)} %refs_0_.11, bf16[1,4096,384]{2,1,0:T(8,128)(2,1)} %refs_1_.7, bf16[512,2048]{1,0:T(8,128)(2,1)} %bitcast.4.refs_2_.refs_0_, bf16[512,2048]{1,0:T(8,128)(2,1)} %collective-permute-done.1.refs_3_.refs_1_), custom_call_target="tpu_custom_call" | custom-call | tf_op jit(solution)/shard_map/gate_up/pallas_call | solution.py:69
  68.8 15.2 %all-to-all-done.1 = bf16[64,8,2048]{2,1,0:T(8,128)(2,1)} async-done(((bf16[64,8,2048]{2,1,0:T(8,128)(2,1)}), bf16[64,8,2048]{2,1,0:T(8,128)(2,1)}, u32[]{:S(2)}, u32[]{:S(2)}) %all-to-all-start.1) | async-done | bytes 2097184 | tf_op jit(solution)/shard_map/all_to_all | solution.py:338
  84.0 0.0 collective-permute-done.2.refs_2_
  84.0 3.0 %collective-permute-start.3 = (bf16[512,2048]{1,0:T(8,128)(2,1)}, bf16[512,2048]{1,0:T(8,128)(2,1)}, u32[]{:S(2)}, u32[]{:S(2)}) collective-permute-start(bf16[512,2048]{1,0:T(8,128)(2,1)} %bitcast.6.refs_1_.refs_2_), channel_id=1, source_target_pairs={{0,1},{1,0},{2,3},{3,2},{4,5},{5,4},{6,7},{7,6},{8,9},{9,8},{10,11... | collective-permute-start | bytes 6291464 | tf_op jit(solution)/shard_map/ppermute | solution.py:335
  87.0 4.2 %back_early.1.refs_2_ = f32[512,384]{1,0:T(8,128)} custom-call(s32[1]{0:T(128)} %bitcast.place_ref, bf16[1,384,4096]{2,1,0:T(8,128)(2,1)} %refs_0_.10, bf16[512,2048]{1,0:T(8,128)(2,1)} %bitcast.6.refs_1_.refs_2_), custom_call_target="tpu_custom_call" | custom-call | tf_op jit(solution)/shard_map/back_early/pallas_call | solution.py:69
  91.2 0.0 collective-permute-done.3.refs_1_.refs_3_
  91.3 5.6 %back_late.1 = (bf16[512,768]{1,0:T(8,128)(2,1)}, bf16[512,384]{1,0:T(8,128)(2,1)}, bf16[512,128]{1,0:T(8,128)(2,1)}) custom-call(s32[1]{0:T(128)} %bitcast.place_ref, bf16[1,384,4096]{2,1,0:T(8,128)(2,1)} %refs_0_.10, bf16[512,2048]{1,0:T(8,128)(2,1)} %collective-permute-done.3.refs_1_.refs_3_, f32[512,384]{1,0:T(8,128)} %back_early.1.refs_2_, ...), custom_call_target="tpu_custom_call" | custom-call | tf_op jit(solution)/shard_map/back_late/pallas_call | solution.py:69
  96.9 0.5 collective-permute-start.4
  97.4 2.2 %collective-permute-done.4.refs_4_ = bf16[512,768]{1,0:T(8,128)(2,1)S(1)} collective-permute-done((bf16[512,768]{1,0:T(8,128)(2,1)}, bf16[512,768]{1,0:T(8,128)(2,1)S(1)}, u32[]{:S(2)}, u32[]{:S(2)}) %collective-permute-start.4) | collective-permute-done | bytes 786464 | tf_op jit(solution)/shard_map/ppermute | solution.py:335
  99.6 0.9 copy-done.1
  100.5 8.8 %row_parts.1 = bf16[512,2176]{1,0:T(8,128)(2,1)} custom-call(s32[1]{0:T(128)} %bitcast.place_ref, bf16[1,4096,384]{2,1,0:T(8,128)(2,1)} %refs_0_.11, bf16[1,4096,384]{2,1,0:T(8,128)(2,1)} %refs_1_.7, bf16[2048,768]{1,0:T(8,128)(2,1)} %collective-permute-done.2.refs_2_, bf16[512,768]{1,0:T(8,128)(2,1)} %get-tuple-element.36.refs_3_.refs_4_, ...), custom_call_target="tpu_custom_call" | custom-call | tf_op jit(solution)/shard_map/row_parts/pallas_call | solution.py:69
  109.3 5.6 %all-to-all-start.2 = ((bf16[64,8,2176]{2,1,0:T(8,128)(2,1)}), bf16[64,8,2176]{2,1,0:T(8,128)(2,1)}, u32[]{:S(2)}, u32[]{:S(2)}) async-start(bf16[64,8,2176]{2,1,0:T(8,128)(2,1)} %bitcast.10), calls=%async_computation.2 | async-start | bytes 4456448 | tf_op jit(solution)/shard_map/all_to_all | solution.py:338
  114.8 11.1 %weight_grads.1 = (f32[8,128]{1,0:T(8,128)}, bf16[1,4096,384]{2,1,0:T(8,128)(2,1)}, bf16[1,4096,384]{2,1,0:T(8,128)(2,1)}, bf16[1,384,4096]{2,1,0:T(8,128)(2,1)}) custom-call(s32[1]{0:T(128)} %bitcast.place_ref, bf16[512,2048]{1,0:T(8,128)(2,1)} %bitcast.4.refs_2_.refs_0_, bf16[512,2048]{1,0:T(8,128)(2,1)} %collective-permute-done.1.refs_3_.refs_1_, ...), custom_call_target="tpu_custom_call" | custom-call | tf_op jit(solution)/shard_map/weight_grads/pallas_call | solution.py:69
  125.9 18.5 %all-to-all-done.2 = bf16[64,8,2176]{2,1,0:T(8,128)(2,1)} async-done(((bf16[64,8,2176]{2,1,0:T(8,128)(2,1)}), bf16[64,8,2176]{2,1,0:T(8,128)(2,1)}, u32[]{:S(2)}, u32[]{:S(2)}) %all-to-all-start.2) | async-done | bytes 2228256 | tf_op jit(solution)/shard_map/all_to_all | solution.py:338
  144.5 3.1 %gather_rows.1 = (bf16[16,2176]{1,0:T(8,128)(2,1)}, bf16[16,2176]{1,0:T(8,128)(2,1)}) custom-call(s32[1]{0:T(128)} %bitcast.place_ref, bf16[32,2176]{1,0:T(8,128)(2,1)} %get-tuple-element.26.refs_0_, bf16[32,2176]{1,0:T(8,128)(2,1)} %copy-done, bf16[512,2176]{1,0:T(8,128)(2,1)} %bitcast.8.refs_2_, f32[8,128]{1,0:T(8,128)} %get-tuple-element.39.refs_3_), custom_call_target="tpu_custom_call" | custom-call | tf_op jit(solution)/shard_map/gather_rows/pallas_call | solution.py:69
  147.5 1.9 %collective-permute-start.5 = (bf16[16,2176]{1,0:T(8,128)(2,1)}, bf16[16,2176]{1,0:T(8,128)(2,1)S(1)}, u32[]{:S(2)}, u32[]{:S(2)}) collective-permute-start(bf16[16,2176]{1,0:T(8,128)(2,1)} %get-tuple-element.41), channel_id=1, source_target_pairs={{0,1},{1,0},{2,3},{3,2},{4,5},{5,4},{6,7},{7,6},{8,9},{9,8},{10,11... | collective-permute-start | bytes 208904 | tf_op jit(solution)/shard_map/ppermute | solution.py:335
  149.4 1.1 collective-permute-done.5.refs_2_
  150.5 0.6 copy-done.2
  151.1 1.7 %total.1 = (bf16[16,4096]{1,0:T(8,128)(2,1)}, f32[4,16]{1,0:T(4,128)}) custom-call(s32[1]{0:T(128)} %bitcast.place_ref, f32[4,16]{1,0:T(4,128)} %bitcast.14, bf16[16,2176]{1,0:T(8,128)(2,1)} %get-tuple-element.40.refs_1_, bf16[16,2176]{1,0:T(8,128)(2,1)} %copy-done.2), custom_call_target="tpu_custom_call" | custom-call | tf_op jit(solution)/shard_map/total/pallas_call | solution.py:69
  (3 shorter events, 0.0 us)
Async XLA Ops:
  2.4 2.7 %collective-permute-start = (bf16[32,2176]{1,0:T(8,128)(2,1)}, bf16[32,2176]{1,0:T(8,128)(2,1)S(1)}, u32[]{:S(2)}, u32[]{:S(2)}) collective-permute-start(bf16[32,2176]{1,0:T(8,128)(2,1)} %get-tuple-element.27), channel_id=1, source_target_pairs={{0,1},{1,0},{2,3},{3,2},{4,5},{5,4},{6,7},{7,6},{8,9},{9,8},{10,11... | collective-permute-start | bytes 417800 | tf_op jit(solution)/shard_map/ppermute | solution.py:335
  5.1 0.7 copy-start
  9.0 38.9 %all-to-all-start = ((bf16[64,8,2048]{2,1,0:T(8,128)(2,1)}), bf16[64,8,2048]{2,1,0:T(8,128)(2,1)}, u32[]{:S(2)}, u32[]{:S(2)}) async-start(bf16[64,8,2048]{2,1,0:T(8,128)(2,1)} %bitcast.12), calls=%async_computation | async-start | bytes 4194304 | tf_op jit(solution)/shard_map/all_to_all | solution.py:338
  47.9 36.1 %collective-permute-start.2 = (bf16[2048,768]{1,0:T(8,128)(2,1)}, bf16[2048,768]{1,0:T(8,128)(2,1)}, u32[]{:S(2)}, u32[]{:S(2)}) collective-permute-start(bf16[2048,768]{1,0:T(8,128)(2,1)} %lend.1), channel_id=1, source_target_pairs={{0,1},{1,0},{2,3},{3,2},{4,5},{5,4},{6,7},{7,6},{8,9},{9,8},{10,11... | collective-permute-start | bytes 9437192 | tf_op jit(solution)/shard_map/ppermute | solution.py:335
  51.0 8.6 %collective-permute-start.1 = (bf16[512,2048]{1,0:T(8,128)(2,1)}, bf16[512,2048]{1,0:T(8,128)(2,1)}, u32[]{:S(2)}, u32[]{:S(2)}) collective-permute-start(bf16[512,2048]{1,0:T(8,128)(2,1)} %bitcast.4.refs_2_.refs_0_), channel_id=1, source_target_pairs={{0,1},{1,0},{2,3},{3,2},{4,5},{5,4},{6,7},{7,6},{8,9},{9,8},{10,11... | collective-permute-start | bytes 6291464 | tf_op jit(solution)/shard_map/ppermute | solution.py:335
  51.0 33.0 %all-to-all-start.1 = ((bf16[64,8,2048]{2,1,0:T(8,128)(2,1)}), bf16[64,8,2048]{2,1,0:T(8,128)(2,1)}, u32[]{:S(2)}, u32[]{:S(2)}) async-start(bf16[64,8,2048]{2,1,0:T(8,128)(2,1)} %bitcast.11), calls=%async_computation.1 | async-start | bytes 4194304 | tf_op jit(solution)/shard_map/all_to_all | solution.py:338
  84.0 7.3 %collective-permute-start.3 = (bf16[512,2048]{1,0:T(8,128)(2,1)}, bf16[512,2048]{1,0:T(8,128)(2,1)}, u32[]{:S(2)}, u32[]{:S(2)}) collective-permute-start(bf16[512,2048]{1,0:T(8,128)(2,1)} %bitcast.6.refs_1_.refs_2_), channel_id=1, source_target_pairs={{0,1},{1,0},{2,3},{3,2},{4,5},{5,4},{6,7},{7,6},{8,9},{9,8},{10,11... | collective-permute-start | bytes 6291464 | tf_op jit(solution)/shard_map/ppermute | solution.py:335
  96.9 2.8 %collective-permute-start.4 = (bf16[512,768]{1,0:T(8,128)(2,1)}, bf16[512,768]{1,0:T(8,128)(2,1)S(1)}, u32[]{:S(2)}, u32[]{:S(2)}) collective-permute-start(bf16[512,768]{1,0:T(8,128)(2,1)} %get-tuple-element.36.refs_3_.refs_4_), channel_id=1, source_target_pairs={{0,1},{1,0},{2,3},{3,2},{4,5},{5,4},{6,7},{7,6},{8,9},{9,8},{10,11... | collective-permute-start | bytes 2359304 | tf_op jit(solution)/shard_map/ppermute | solution.py:335
  99.6 0.9 copy-start.1
  109.3 35.2 %all-to-all-start.2 = ((bf16[64,8,2176]{2,1,0:T(8,128)(2,1)}), bf16[64,8,2176]{2,1,0:T(8,128)(2,1)}, u32[]{:S(2)}, u32[]{:S(2)}) async-start(bf16[64,8,2176]{2,1,0:T(8,128)(2,1)} %bitcast.10), calls=%async_computation.2 | async-start | bytes 4456448 | tf_op jit(solution)/shard_map/all_to_all | solution.py:338
  147.5 3.0 %collective-permute-start.5 = (bf16[16,2176]{1,0:T(8,128)(2,1)}, bf16[16,2176]{1,0:T(8,128)(2,1)S(1)}, u32[]{:S(2)}, u32[]{:S(2)}) collective-permute-start(bf16[16,2176]{1,0:T(8,128)(2,1)} %get-tuple-element.41), channel_id=1, source_target_pairs={{0,1},{1,0},{2,3},{3,2},{4,5},{5,4},{6,7},{7,6},{8,9},{9,8},{10,11... | collective-permute-start | bytes 208904 | tf_op jit(solution)/shard_map/ppermute | solution.py:335
  150.5 0.6 copy-start.2
where the time goes:
time: 154 us; the launch traced here: 153 us
  waiting for transfers between devices  61.8 us (40%)
  Pallas kernels  55.6 us (36%)
  starting transfers between devices  32.6 us (21%)
  local copies, waits for them, and re-layouts  2.16 us (1%)
    pallas_call x11, Pallas kernels, call(): pl.pallas_call(body, in_specs=[SMEM] + [HBM] * len(args), out_specs=[HBM]...  55.6 us
    all_to_all x3, waiting for transfers between devices, deliver(): lax.all_to_all(x.reshape(chips, SLOTS, x.shape[1]), CHIPS, split_axis=0,...  54.1 us
    all_to_all x3, starting transfers between devices, deliver(): lax.all_to_all(x.reshape(chips, SLOTS, x.shape[1]), CHIPS, split_axis=0,...  22.6 us
    ppermute x6, starting transfers between devices, swap(): return lax.ppermute(x, 'core', [(0, 1), (1, 0)])  9.99 us
    ppermute x6, waiting for transfers between devices, swap(): return lax.ppermute(x, 'core', [(0, 1), (1, 0)])  7.61 us
  transfers between devices with their start and end apart: 9, of which 7 were waited for; matrix products, arithmetic and copies ran while one was open for 0% of the time, Pallas kernels for 21%

commit v1 on v0

v1 whole, which is shorter than its diff:
```python
import functools

import jax
import jax.numpy as jnp
from jax import lax
from jax.experimental import pallas as pl
from jax.experimental.pallas import tpu as pltpu
from jax.sharding import Mesh
from jax.sharding import PartitionSpec as P

CORES = 2
TOPK = 4
CAP = 4
SLOTS = CORES * CAP
META = 128
CHIPS = ("outer", "z")
ALL = ("outer", "z", "core")
F32 = jnp.float32
BF16 = jnp.bfloat16
TN = (((0,), (0,)), ((), ()))
NT = (((1,), (1,)), ((), ()))
SMEM = pl.BlockSpec(memory_space=pltpu.SMEM)
HBM = pl.BlockSpec(memory_space=pltpu.HBM)


def dot(a, b, dims=(((1,), (0,)), ((), ()))):
    return lax.dot_general(a, b, dims, preferred_element_type=F32)


def after(x, *others):
    return lax.optimization_barrier((x, *others))


class Loaded:
    def __init__(self, source, target, semaphore):
        self.copy = pltpu.make_async_copy(source, target, semaphore)
        self.target = target
        self.shape = target.shape
        self.waiting = True
        self.copy.start()

    def wait(self):
        if self.waiting:
            self.copy.wait()
            self.waiting = False

    def __getitem__(self, index):
        self.wait()
        return self.target[index]


class Stages:
    def __init__(self, groups, depth):
        self.groups, self.depth = groups, depth
        for copy in sum(groups[:depth], []):
            copy.start()

    def wait(self, n):
        for copy in self.groups[n]:
            copy.wait()
        for copy in sum(self.groups[n + self.depth : n + self.depth + 1], []):
            copy.start()


def call(kernel, name, outs, place, *args, raw=0, direct=0, scratch=(), limit=28 << 20, far=False):
    count, given = len(outs) - direct, len(args) - raw

    def body(place_ref, *refs):
        raw_refs, ins, refs = refs[:raw], refs[raw : raw + given], refs[raw + given :]
        out_refs, direct_refs, refs = refs[:count], refs[count : count + direct], refs[count + direct :]
        held, made, refs = refs[:given], refs[given : given + count], refs[given + count :]
        in_sems, out_sems, own = refs[0], refs[1], refs[2:]
        loaded = [Loaded(ins[n], held[n], in_sems.at[n]) for n in range(given)]
        kernel(place_ref, *raw_refs, *loaded, *made, *direct_refs, *own)
        for held_ref in loaded:
            held_ref.wait()
        copies = [pltpu.make_async_copy(made[n], out_refs[n], out_sems.at[n]) for n in range(count)]
        for copy in copies:
            copy.start()
        for copy in copies:
            copy.wait()

    return pl.pallas_call(
        body,
        in_specs=[SMEM] + [HBM] * len(args),
        out_specs=[HBM] * len(outs),
        out_shape=[pltpu.HBM(*out) if far else jax.ShapeDtypeStruct(*out) for out in outs],
        scratch_shapes=[pltpu.VMEM(x.shape, x.dtype) for x in args[raw:]]
        + [pltpu.VMEM(shape, kind) for shape, kind in outs[:count]]
        + [pltpu.SemaphoreType.DMA((max(given, 1),)), pltpu.SemaphoreType.DMA((max(count, 1),)), *scratch],
        compiler_params=pltpu.CompilerParams(vmem_limit_bytes=limit),
        name=name,
    )(place, *args)


def column(row):
    n = row.shape[1]
    here = lax.broadcasted_iota(jnp.int32, (n, n), 0) == lax.broadcasted_iota(jnp.int32, (n, n), 1)
    return jnp.sum(jnp.where(here, row, 0.0), axis=1, keepdims=True)


def row(column):
    n = column.shape[0]
    here = lax.broadcasted_iota(jnp.int32, (n, n), 0) == lax.broadcasted_iota(jnp.int32, (n, n), 1)
    return jnp.sum(jnp.where(here, column, 0.0), axis=0, keepdims=True)


def columns(start, size):
    return pl.ds(pl.multiple_of(start, size), size)


def slot_mask(core, ids, lines):
    tokens = ids[0].shape[0]
    own = tokens // CORES
    line = lax.broadcasted_iota(jnp.int32, (tokens, lines), 1)
    expert = (line // (2 * SLOTS)).astype(F32)
    named = [jnp.where(some == expert, 1.0, 0.0) for some in ids]
    total = named[0] + named[1] + named[2] + named[3]
    after = lax.broadcasted_iota(jnp.int32, (tokens, tokens), 0)
    before = lax.broadcasted_iota(jnp.int32, (tokens, tokens), 1)
    earlier = jnp.where((before < after) & (before // own == after // own), 1.0, 0.0)
    rank = dot(earlier.astype(BF16), total.astype(BF16)).astype(jnp.int32)
    token = lax.broadcasted_iota(jnp.int32, (tokens, lines), 0)
    place = rank + ((token // own) ^ core) * CAP
    mask = jnp.where((total > 0.0) & (place == line % SLOTS), 1.0, 0.0)
    return mask, named


def both_of(refs, k):
    return jnp.concatenate([column(ref[k : k + 1, :].astype(F32)) for ref in refs], axis=0)


def build_kernel(place_ref, ids_ref, other_ids_ref, *refs):
    scaled = len(refs) > 5
    if scaled:
        comb_refs, rows_refs, (picks_ref, out_hbm, out_ref, sems) = refs[0:2], refs[2:4], refs[4:]
    else:
        rows_refs, (out_hbm, out_ref, sems) = refs[0:2], refs[2:]
    core = place_ref[0]
    steps, lines, step = out_ref.shape
    tok, width = rows_refs[0].shape
    half = width // CORES
    ids_refs = (ids_ref, other_ids_ref)
    mask, named = slot_mask(core, [both_of(ids_refs, k) for k in range(TOPK)], lines)
    pick = mask.astype(BF16)
    if scaled:
        picks_ref[: CORES * tok, :] = pick
        for k in range(TOPK):
            picks_ref[(k + 1) * CORES * tok : (k + 2) * CORES * tok, :] = (mask * named[k]).astype(BF16)
        chosen = sum(named[k] * both_of(comb_refs, k) for k in range(TOPK)) * mask
        high = chosen.astype(BF16)
        ones = jnp.ones((mask.shape[0], META), BF16)
        weight = dot(high, ones, TN) + dot((chosen - high.astype(F32)).astype(BF16), ones, TN)
        weight = weight[:, :1]
    copies = []
    for n in range(steps):
        cols = columns(core * half + n * step, step)
        found = dot(pick, jnp.concatenate([ref[:, cols] for ref in rows_refs], axis=0), TN)
        out_ref[n] = (found * weight if scaled else found).astype(BF16)
        copies.append(pltpu.make_async_copy(out_ref.at[n], out_hbm.at[:, pl.ds(n * step, step)], sems.at[n]))
        copies[-1].start()
    for copy in copies:
        copy.wait()


def lend_kernel(place_ref, gate_hbm, up_hbm, order_hbm, first_ref, sems):
    half, both = first_ref.shape
    ff = both // 2
    at = columns((1 - place_ref[0]) * half, half)
    copies = [
        pltpu.make_async_copy(gate_hbm.at[0, at, :], first_ref.at[:, pl.ds(0, ff)], sems.at[0]),
        pltpu.make_async_copy(up_hbm.at[0, at, :], first_ref.at[:, pl.ds(ff, ff)], sems.at[1]),
    ]
    for copy in copies:
        copy.start()
    for copy in copies:
        copy.wait()


def turn_kernel(place_ref, gate_hbm, up_hbm, down_hbm, order_hbm, back_ref, parts_ref, first_ref, down_ref, sems):
    half, both = first_ref.shape
    ff = both // 2
    at = columns(place_ref[0] * half, half)
    copies = [
        pltpu.make_async_copy(down_hbm.at[0], down_ref, sems.at[0]),
        pltpu.make_async_copy(gate_hbm.at[0, at, :], first_ref.at[:, pl.ds(0, ff)], sems.at[1]),
        pltpu.make_async_copy(up_hbm.at[0, at, :], first_ref.at[:, pl.ds(ff, ff)], sems.at[2]),
    ]
    for copy in copies:
        copy.start()
    for copy in copies:
        copy.wait()
    step = 256
    for n in range(0, CORES * half, step):
        back_ref[n : n + step, :] = down_ref[:, n : n + step].T
    for n in range(0, half, step):
        parts_ref[:, n : n + step] = first_ref[n : n + step, :].T


def turn_lent_kernel(place_ref, lent_ref, parts_ref):
    step = 256
    for n in range(0, lent_ref.shape[0], step):
        parts_ref[:, n : n + step] = lent_ref[n : n + step, :].T


def gate_up_kernel(place_ref, gate_hbm, up_hbm, own_hbm, other_hbm, factors_ref, hidden_ref, rows_ref, first_ref, sems):
    core = place_ref[0]
    parts, step, both = first_ref.shape
    ff = both // 2
    half = parts * step // CORES
    groups = []
    for n in range(parts):
        j, at = divmod(n * step, half)
        cols = columns((core ^ j) * half + at, step)
        pairs = (
            ((own_hbm, other_hbm)[j].at[:, pl.ds(at, step)], rows_ref.at[n]),
            (gate_hbm.at[0, cols, :], first_ref.at[n, :, pl.ds(0, ff)]),
            (up_hbm.at[0, cols, :], first_ref.at[n, :, pl.ds(ff, ff)]),
        )
        groups.append([pltpu.make_async_copy(*pair, sems.at[3 * n + k]) for k, pair in enumerate(pairs)])
    stages = Stages(groups, 2)
    pre = 0.0
    for n in range(parts):
        stages.wait(n)
        pre += dot(rows_ref[n], first_ref[n])
    gate_pre, up_pre = pre[:, :ff], pre[:, ff:]
    sigmoid_gate = jax.nn.sigmoid(gate_pre)
    active = gate_pre * sigmoid_gate
    hidden_ref[...] = (active * up_pre).astype(BF16)
    factors_ref[:, :ff] = up_pre * sigmoid_gate * (1.0 + gate_pre * (1.0 - sigmoid_gate))
    factors_ref[:, ff:] = active


def back_product(which, back_hbm, grads_hbm, rows_ref, back_ref, sems):
    parts, _, step = rows_ref.shape
    groups = []
    for n in range(parts):
        at = columns((which * parts + n) * step, step)
        pairs = ((grads_hbm.at[:, pl.ds(n * step, step)], rows_ref.at[n]), (back_hbm.at[at, :], back_ref.at[n]))
        groups.append([pltpu.make_async_copy(*pair, sems.at[2 * n + k]) for k, pair in enumerate(pairs)])
    stages = Stages(groups, parts)
    scaled = 0.0
    for n in range(parts):
        stages.wait(n)
        scaled += dot(rows_ref[n], back_ref[n])
    return scaled


def back_early_kernel(place_ref, back_hbm, own_hbm, out_ref, *own):
    out_ref[...] = back_product(place_ref[0], back_hbm, own_hbm, *own)


def back_late_kernel(place_ref, back_hbm, other_hbm, sum_ref, factors_ref, hidden_ref, deltas_ref, score_ref, *own):
    scaled = back_product(1 - place_ref[0], back_hbm, other_hbm, *own) + sum_ref[...]
    ff = scaled.shape[1]
    score = jnp.sum(scaled * hidden_ref[...].astype(F32), axis=1, keepdims=True)
    deltas_ref[:, :ff] = (scaled * factors_ref[:, :ff]).astype(BF16)
    deltas_ref[:, ff:] = (scaled * factors_ref[:, ff:]).astype(BF16)
    score_ref[...] = jnp.broadcast_to(score, score_ref.shape).astype(BF16)


def parts_kernel(last, place_ref, turned_hbm, deltas_ref, *refs):
    if last:
        before_ref, score_ref, *refs = refs
    out_hbm, weight_ref, part_ref, sems, out_sems = refs
    steps, _, step = weight_ref.shape
    half = steps * step
    stages = Stages([
        [pltpu.make_async_copy(turned_hbm.at[:, pl.ds(n * step, step)], weight_ref.at[n], sems.at[n])]
        for n in range(steps)
    ], 2)
    deltas = deltas_ref[...]
    outs = []
    for n in range(steps):
        stages.wait(n)
        part = dot(deltas, weight_ref[n])
        if last:
            part += before_ref[:, n * step : (n + 1) * step].astype(F32)
        part_ref[n] = part.astype(BF16)
        outs.append(pltpu.make_async_copy(part_ref.at[n], out_hbm.at[:, pl.ds(n * step, step)], out_sems.at[n]))
        outs[-1].start()
    if last:
        score_ref.wait()
        outs.append(pltpu.make_async_copy(score_ref.target, out_hbm.at[:, pl.ds(half, META)], out_sems.at[steps]))
        outs[-1].start()
    for copy in outs:
        copy.wait()


def gather_kernel(place_ref, back_hbm, picks_ref, mark_ref, mine_ref, send_ref, mine_score_ref, send_score_ref, back_ref, sems):
    tok, width = mine_ref.shape
    tokens = CORES * tok
    steps, _, step = back_ref.shape
    copies = [pltpu.make_async_copy(back_hbm.at[:, pl.ds(width, META)], back_ref.at[steps - 1, :, pl.ds(0, META)], sems.at[0])]
    for n in range(steps - 1):
        copies.append(pltpu.make_async_copy(back_hbm.at[:, pl.ds(n * step, step)], back_ref.at[n], sems.at[n + 1]))
    for copy in copies:
        copy.start()
    pick = picks_ref[:tokens, :]
    copies[0].wait()
    scores = dot(picks_ref[tokens:, :], back_ref[steps - 1, :, :META])
    for k in range(TOPK):
        mine_score_ref[k : k + 1, :] = row(scores[k * tokens : k * tokens + tok, :1])
        send_score_ref[k : k + 1, :] = row(scores[k * tokens + tok : (k + 1) * tokens, :1])
    for n in range(steps - 1):
        copies[n + 1].wait()
        part = dot(pick, back_ref[n]).astype(BF16)
        mine_ref[:, n * step : (n + 1) * step] = part[:tok]
        send_ref[:, n * step : (n + 1) * step] = part[tok:]


def weights_kernel(place_ref, *refs):
    rows_refs, grads_refs = refs[0:2], refs[2:4]
    deltas_ref, hidden_ref, mark_ref, gate_hbm, up_hbm, down_hbm, gate_ref, up_ref, down_ref, sems = refs[4:]
    mark_ref[...] = jnp.zeros_like(mark_ref)
    core = place_ref[0]
    half, step = rows_refs[0].shape[1], gate_ref.shape[1]
    ff = hidden_ref.shape[1]
    deltas = deltas_ref[...]
    copies = []
    for j in range(CORES):
        for at in range(0, half, step):
            n = (j * half + at) // step
            grad = dot(rows_refs[j][:, at : at + step], deltas, TN)
            gate_ref[n] = grad[:, :ff].astype(BF16)
            up_ref[n] = grad[:, ff:].astype(BF16)
            cols = columns((core ^ j) * half + at, step)
            copies += [
                pltpu.make_async_copy(gate_ref.at[n], gate_hbm.at[0, cols, :], sems.at[3 * n]),
                pltpu.make_async_copy(up_ref.at[n], up_hbm.at[0, cols, :], sems.at[3 * n + 1]),
            ]
            for copy in copies[-2:]:
                copy.start()
    hidden = hidden_ref[...].T
    for j in range(CORES):
        for at in range(0, half, step):
            n = (j * half + at) // step
            down_ref[n] = dot(hidden, grads_refs[j][:, at : at + step]).astype(BF16)
            cols = columns((core ^ j) * half + at, step)
            copies.append(pltpu.make_async_copy(down_ref.at[n], down_hbm.at[0, :, cols], sems.at[3 * n + 2]))
            copies[-1].start()
    for copy in copies:
        copy.wait()


def local(tokens, out_grad, combine, expert_ids, gate_weight, up_weight, down_weight):
    tok, width = tokens.shape
    chips = lax.axis_size(CHIPS)
    lines = chips * SLOTS
    ff = gate_weight.shape[2]
    half, quarter = width // CORES, width // CORES // 2
    step = 512
    place = lax.axis_index("core").astype(jnp.int32).reshape(1)

    def swap(x):
        return lax.ppermute(x, "core", [(0, 1), (1, 0)])

    def deliver(x):
        found = lax.all_to_all(x.reshape(chips, SLOTS, x.shape[1]), CHIPS, split_axis=0, concat_axis=0, tiled=True)
        return found.reshape(x.shape)

    ids, comb = expert_ids.T, combine.T
    ids_pair = (ids, swap(ids))
    tokens_pair = (tokens, swap(tokens))
    scratch = [pltpu.VMEM((half // step, lines, step), BF16), pltpu.SemaphoreType.DMA((half // step,))]
    out = ((lines, half), BF16)
    rows_out = call(
        build_kernel, "build_rows", [out], place, *ids_pair, *tokens_pair, direct=1, scratch=scratch, limit=63 << 20
    )[0]
    later = after(comb, out_grad, rows_out)[:2]
    comb_pair, out_grad_pair = [(x, swap(x)) for x in later]
    picks, grads_out = call(
        build_kernel, "build_grads", [(((TOPK + 1) * CORES * tok, lines), BF16), out],
        place, *ids_pair, *comb_pair, *out_grad_pair, direct=1, scratch=scratch, far=True,
    )
    lend = call(
        lend_kernel, "lend", [((half, 2 * ff), BF16)], place, gate_weight, up_weight, out_grad_pair[1],
        raw=3, scratch=[pltpu.SemaphoreType.DMA((2,))],
    )[0]
    back, parts_own = call(
        turn_kernel,
        "turn",
        [((width, ff), BF16), ((2 * ff, half), BF16)],
        place, gate_weight, up_weight, down_weight, out_grad_pair[1],
        raw=4,
        scratch=[pltpu.VMEM((half, 2 * ff), BF16), pltpu.VMEM((ff, width), BF16), pltpu.SemaphoreType.DMA((3,))],
    )
    rows, grads_out, back, parts_own, lend = after(deliver(rows_out), grads_out, back, parts_own, lend)
    parts_other = call(turn_lent_kernel, "turn_lent", [((2 * ff, half), BF16)], place, swap(lend))[0]
    rows_pair = (rows, swap(rows))
    factors, hidden = call(
        gate_up_kernel,
        "gate_up",
        [((lines, 2 * ff), F32), ((lines, ff), BF16)],
        place, gate_weight, up_weight, *rows_pair,
        raw=4,
        scratch=[
            pltpu.VMEM((4, lines, quarter), BF16),
            pltpu.VMEM((4, quarter, 2 * ff), BF16),
            pltpu.SemaphoreType.DMA((12,)),
        ],
    )
    grads, factors, hidden, parts_other = after(deliver(grads_out), factors, hidden, parts_other)
    grads_pair = (grads, swap(grads))
    scratch = [
        pltpu.VMEM((half // step, lines, step), BF16),
        pltpu.VMEM((half // step, step, ff), BF16),
        pltpu.SemaphoreType.DMA((2 * half // step,)),
    ]
    scaled = call(
        back_early_kernel, "back_early", [((lines, ff), F32)], place, back, grads, raw=2, scratch=scratch
    )[0]
    other, scaled = after(grads_pair[1], scaled)
    deltas, score = call(
        back_late_kernel,
        "back_late",
        [((lines, 2 * ff), BF16), ((lines, META), BF16)],
        place, back, other, scaled, factors, hidden, raw=2, scratch=scratch,
    )

    def parts(last, size, *args):
        return call(
            functools.partial(parts_kernel, last),
            "row_parts",
            [((lines, size), BF16)],
            place, *args,
            raw=1,
            direct=1,
            far=last,
            scratch=[
                pltpu.VMEM((half // step, 2 * ff, step), BF16),
                pltpu.VMEM((half // step, lines, step), BF16),
                pltpu.SemaphoreType.DMA((half // step,)),
                pltpu.SemaphoreType.DMA((half // step + 1,)),
            ],
        )[0]

    part = parts(False, half, parts_own, deltas)
    deltas_other, part = after(swap(deltas), part)
    parts_sum = parts(True, half + META, parts_other, deltas_other, part, score)
    mark, gate_grad, up_grad, down_grad = call(
        weights_kernel,
        "weight_grads",
        [((8, META), F32), (gate_weight.shape, BF16), (up_weight.shape, BF16), (down_weight.shape, BF16)],
        place, *rows_pair, *grads_pair, deltas, hidden,
        direct=3,
        scratch=[
            pltpu.VMEM((width // step, step, ff), BF16),
            pltpu.VMEM((width // step, step, ff), BF16),
            pltpu.VMEM((width // step, ff, step), BF16),
            pltpu.SemaphoreType.DMA((3 * width // step,)),
        ],
    )
    mine, send, mine_score, send_score = call(
        gather_kernel,
        "gather_rows",
        [((tok, half), BF16)] * CORES + [((TOPK, tok), F32)] * CORES,
        place, deliver(parts_sum), pltpu.with_memory_space_constraint(picks, pltpu.HBM), mark,
        raw=1,
        scratch=[pltpu.VMEM((half // step + 1, lines, step), BF16), pltpu.SemaphoreType.DMA((half // step + 1,))],
    )
    combine_grad = ((mine_score + swap(send_score)) / comb).T
    other = swap(send)
    token_grad = jnp.where(
        place[0] == 0, jnp.concatenate([mine, other], axis=1), jnp.concatenate([other, mine], axis=1)
    )
    return token_grad, combine_grad, gate_grad, up_grad, down_grad


def solution(mesh):
    outer, inner = mesh.devices.shape
    split = Mesh(mesh.devices.reshape(outer, inner // CORES, CORES), ALL)
    flat, deep = P(ALL, None), P(ALL, None, None)
    return jax.shard_map(
        local,
        mesh=split,
        in_specs=(flat, flat, flat, flat, deep, deep, deep),
        out_specs=(flat, flat, deep, deep, deep),
        check_vma=False,
    )
```

time: 154 us -> 144 us (0.935)
  waiting for transfers between devices: 61.8 us -> 47.5 us
  local copies, waits for them, and re-layouts: 2.16 us -> 14.7 us
  Pallas kernels: 55.6 us -> 44.8 us
  starting transfers between devices: 32.6 us -> 34.2 us
    all_to_all x3, waiting for transfers between devices: 54.1 us -> 41.5 us  [deliver(): lax.all_to_all(x.reshape(chips, SLOTS, x.shape[1]), CHIPS, split_axis=0,...]
    unnamed x6 -> x42, local copies, waits for them, and re-layouts: 2.16 us -> 14.7 us
    pallas_call x11 -> x12, Pallas kernels: 55.6 us -> 44.8 us  [call(): pl.pallas_call(body, in_specs=[SMEM] + [HBM] * len(args), out_specs=[HBM]...]
    ppermute x6 -> x10, waiting for transfers between devices: 7.61 us -> 5.94 us  [swap(): return lax.ppermute(x, 'core', [(0, 1), (1, 0)])]
    ppermute x6 -> x10, starting transfers between devices: 9.99 us -> 11.5 us  [swap(): return lax.ppermute(x, 'core', [(0, 1), (1, 0)])]
  transfers between devices with their start and end apart: 9 -> 13, of which waited for: 7 -> 7; matrix products, arithmetic and copies ran while one was open for 0% -> 0% of each run, Pallas kernels for 21% -> 22%
where the time goes in v1:
time: 144 us; the launch traced here: 143 us
  waiting for transfers between devices  47.5 us (33%)
  Pallas kernels  44.8 us (31%)
  starting transfers between devices  34.2 us (24%)
  local copies, waits for them, and re-layouts  14.7 us (10%)
    pallas_call x12, Pallas kernels, call(): pl.pallas_call(body, in_specs=[SMEM] + [HBM] * len(args), out_specs=[HBM]...  44.8 us
    all_to_all x3, waiting for transfers between devices, deliver(): lax.all_to_all(x.reshape(chips, SLOTS, x.shape[1]), CHIPS, split_axis=0,...  41.5 us
    all_to_all x3, starting transfers between devices, deliver(): lax.all_to_all(x.reshape(chips, SLOTS, x.shape[1]), CHIPS, split_axis=0,...  22.7 us
    unnamed x42, local copies, waits for them, and re-layouts  14.7 us
    ppermute x10, starting transfers between devices, swap(): return lax.ppermute(x, 'core', [(0, 1), (1, 0)])  11.5 us
    ppermute x10, waiting for transfers between devices, swap(): return lax.ppermute(x, 'core', [(0, 1), (1, 0)])  5.94 us
  transfers between devices with their start and end apart: 13, of which 7 were waited for; matrix products, arithmetic and copies ran while one was open for 0% of the time, Pallas kernels for 22%

profile of v1, /device:TPU:1, one launch (start us, length us, event | category | flops | bytes accessed | tf_op | source)
XLA Modules:
  0.0 143.4 jit_solution(15651741663432879584)
XLA Ops:
  0.6 1.5 %collective-permute-start.1 = (bf16[16,4096]{1,0:T(8,128)(2,1)}, bf16[16,4096]{1,0:T(8,128)(2,1)S(1)}, u32[]{:S(2)}, u32[]{:S(2)}) collective-permute-start(bf16[16,4096]{1,0:T(8,128)(2,1)} %refs_2_.2), channel_id=1, source_target_pairs={{0,1},{1,0},{2,3},{3,2},{4,5},{5,4},{6,7},{7,6},{8,9},{9,8},{10,11... | collective-permute-start | bytes 393224 | tf_op jit(solution)/shard_map/ppermute | solution.py:356
  2.2 1.3 collective-permute-done.refs_1_
  4.2 2.9 %build_rows.1 = bf16[512,2048]{1,0:T(8,128)(2,1)} custom-call(s32[1]{0:T(128)} %bitcast.place_ref, s32[4,16]{1,0:T(4,128)} %bitcast.16, s32[4,16]{1,0:T(4,128)} %copy-done.18, bf16[16,4096]{1,0:T(8,128)(2,1)} %refs_2_.2, bf16[16,4096]{1,0:T(8,128)(2,1)} %copy-done.20), custom_call_target="tpu_custom_call" | custom-call | tf_op jit(solution)/shard_map/build_rows/pallas_call | solution.py:83
  7.1 11.8 %all-to-all-start = ((bf16[64,8,2048]{2,1,0:T(8,128)(2,1)}), bf16[64,8,2048]{2,1,0:T(8,128)(2,1)}, u32[]{:S(2)}, u32[]{:S(2)}) async-start(bf16[64,8,2048]{2,1,0:T(8,128)(2,1)} %bitcast.19), calls=%async_computation | async-start | bytes 4194304 | tf_op jit(solution)/shard_map/all_to_all | solution.py:359
  19.6 1.1 collective-permute-done.2.refs_3_
  20.6 3.8 %build_grads.1 = (bf16[160,512]{1,0:T(8,128)(2,1)}, bf16[512,2048]{1,0:T(8,128)(2,1)}) custom-call(s32[1]{0:T(128)} %bitcast.place_ref, s32[4,16]{1,0:T(4,128)S(1)} %bitcast.17, s32[4,16]{1,0:T(4,128)S(1)} %copy-done.19, f32[4,16]{1,0:T(4,128)S(1)} %bitcast.14, f32[4,16]{1,0:T(4,128)S(1)} %collective-permute-done.2.refs_3_, bf16[16,4096]{1,0:T(8,128)(2,1)S(1)} %copy-done.15, ...), custom_call_target="tpu_custom_call" | custom-call | tf_op jit(solution)/shard_map/build_grads/pallas_call | solution.py:83
  24.5 1.9 %copy-done.1 = bf16[1,4096,384]{2,1,0:T(8,128)(2,1)S(1)} copy-done((bf16[1,4096,384]{2,1,0:T(8,128)(2,1)S(1)}, bf16[1,4096,384]{2,1,0:T(8,128)(2,1)}, u32[]{:S(2)}) %copy-start.1) | copy-done | bytes 3145752
  26.9 1.7 %copy-done.12 = bf16[2048,768]{1,0:T(8,128)(2,1)} copy-done((bf16[2048,768]{1,0:T(8,128)(2,1)}, bf16[2048,768]{1,0:T(8,128)(2,1)S(1)}, u32[]{:S(2)}) %copy-start.12) | copy-done | bytes 3145752
  29.1 2.8 %turn.1 = (bf16[4096,384]{1,0:T(8,128)(2,1)S(1)}, bf16[768,2048]{1,0:T(8,128)(2,1)S(1)}) custom-call(s32[1]{0:T(128)} %bitcast.place_ref, bf16[1,4096,384]{2,1,0:T(8,128)(2,1)S(1)} %copy-done, bf16[1,4096,384]{2,1,0:T(8,128)(2,1)S(1)} %copy-done.1, bf16[1,384,4096]{2,1,0:T(8,128)(2,1)S(1)} %copy-done.11, ...), custom_call_target="tpu_custom_call" | custom-call | tf_op jit(solution)/shard_map/turn/pallas_call | solution.py:83
  31.9 1.7 %copy-done.3 = bf16[4096,384]{1,0:T(8,128)(2,1)} copy-done((bf16[4096,384]{1,0:T(8,128)(2,1)}, bf16[4096,384]{1,0:T(8,128)(2,1)S(1)}, u32[]{:S(2)}) %copy-start.3) | copy-done | bytes 3145752
  33.5 1.7 %copy-done.9 = bf16[768,2048]{1,0:T(8,128)(2,1)} copy-done((bf16[768,2048]{1,0:T(8,128)(2,1)}, bf16[768,2048]{1,0:T(8,128)(2,1)S(1)}, u32[]{:S(2)}) %copy-start.9) | copy-done | bytes 3145752
  35.2 11.4 %all-to-all-done = bf16[64,8,2048]{2,1,0:T(8,128)(2,1)} async-done(((bf16[64,8,2048]{2,1,0:T(8,128)(2,1)}), bf16[64,8,2048]{2,1,0:T(8,128)(2,1)}, u32[]{:S(2)}, u32[]{:S(2)}) %all-to-all-start) | async-done | bytes 2097184 | tf_op jit(solution)/shard_map/all_to_all | solution.py:359
  46.6 2.8 %collective-permute-start.5 = (bf16[2048,768]{1,0:T(8,128)(2,1)}, bf16[2048,768]{1,0:T(8,128)(2,1)}, u32[]{:S(2)}, u32[]{:S(2)}) collective-permute-start(bf16[2048,768]{1,0:T(8,128)(2,1)} %copy-done.12), channel_id=1, source_target_pairs={{0,1},{1,0},{2,3},{3,2},{4,5},{5,4},{6,7},{7,6},{8,9},{9,8},{10,11... | collective-permute-start | bytes 9437192 | tf_op jit(solution)/shard_map/ppermute | solution.py:356
  49.4 5.7 %all-to-all-start.1 = ((bf16[64,8,2048]{2,1,0:T(8,128)(2,1)}), bf16[64,8,2048]{2,1,0:T(8,128)(2,1)}, u32[]{:S(2)}, u32[]{:S(2)}) async-start(bf16[64,8,2048]{2,1,0:T(8,128)(2,1)} %bitcast.20), calls=%async_computation.1 | async-start | bytes 4194304 | tf_op jit(solution)/shard_map/all_to_all | solution.py:359
  55.1 2.9 %collective-permute-done.4.refs_3_.refs_1_ = bf16[512,2048]{1,0:T(8,128)(2,1)} collective-permute-done((bf16[512,2048]{1,0:T(8,128)(2,1)}, bf16[512,2048]{1,0:T(8,128)(2,1)}, u32[]{:S(2)}, u32[]{:S(2)}) %collective-permute-start.4) | collective-permute-done | bytes 2097184 | tf_op jit(solution)/shard_map/ppermute | solution.py:356
  58.0 1.9 %copy-done.2 = bf16[1,4096,384]{2,1,0:T(8,128)(2,1)S(1)} copy-done((bf16[1,4096,384]{2,1,0:T(8,128)(2,1)S(1)}, bf16[1,4096,384]{2,1,0:T(8,128)(2,1)}, u32[]{:S(2)}) %copy-start.2) | copy-done | bytes 3145752
  59.9 6.8 %gate_up.1 = (f32[512,768]{1,0:T(8,128)S(1)}, bf16[512,384]{1,0:T(8,128)(2,1)S(1)}) custom-call(s32[1]{0:T(128)} %bitcast.place_ref, bf16[1,4096,384]{2,1,0:T(8,128)(2,1)S(1)} %copy-done, bf16[1,4096,384]{2,1,0:T(8,128)(2,1)S(1)} %copy-done.2, bf16[512,2048]{1,0:T(8,128)(2,1)} %bitcast.3.refs_2_.refs_0_, bf16[512,2048]{1,0:T(8,128)(2,1)} %collective-permute-done.4.refs_3_.refs_1_), custom_call_target="tpu_custom_call" | custom-call | tf_op jit(solution)/shard_map/gate_up/pallas_call | solution.py:83
  66.7 1.2 copy-done.13
  67.9 3.1 %turn_lent.1.refs_0_ = bf16[768,2048]{1,0:T(8,128)(2,1)S(1)} custom-call(s32[1]{0:T(128)} %bitcast.place_ref, bf16[2048,768]{1,0:T(8,128)(2,1)} %collective-permute-done.5.refs_0_), custom_call_target="tpu_custom_call" | custom-call | tf_op jit(solution)/shard_map/turn_lent/pallas_call | solution.py:83
  71.0 11.4 %all-to-all-done.1 = bf16[64,8,2048]{2,1,0:T(8,128)(2,1)} async-done(((bf16[64,8,2048]{2,1,0:T(8,128)(2,1)}), bf16[64,8,2048]{2,1,0:T(8,128)(2,1)}, u32[]{:S(2)}, u32[]{:S(2)}) %all-to-all-start.1) | async-done | bytes 2097184 | tf_op jit(solution)/shard_map/all_to_all | solution.py:359
  82.4 3.0 %collective-permute-start.6 = (bf16[512,2048]{1,0:T(8,128)(2,1)}, bf16[512,2048]{1,0:T(8,128)(2,1)S(1)}, u32[]{:S(2)}, u32[]{:S(2)}) collective-permute-start(bf16[512,2048]{1,0:T(8,128)(2,1)} %bitcast.6.refs_1_.refs_2_), channel_id=1, source_target_pairs={{0,1},{1,0},{2,3},{3,2},{4,5},{5,4},{6,7},{7,6},{8,9},{9,8},{10,11... | collective-permute-start | bytes 6291464 | tf_op jit(solution)/shard_map/ppermute | solution.py:356
  85.4 1.9 %copy-done.4 = bf16[4096,384]{1,0:T(8,128)(2,1)S(1)} copy-done((bf16[4096,384]{1,0:T(8,128)(2,1)S(1)}, bf16[4096,384]{1,0:T(8,128)(2,1)}, u32[]{:S(2)}) %copy-start.4) | copy-done | bytes 3145752
  87.3 2.8 %back_early.1.refs_2_ = f32[512,384]{1,0:T(8,128)S(1)} custom-call(s32[1]{0:T(128)} %bitcast.place_ref, bf16[4096,384]{1,0:T(8,128)(2,1)S(1)} %copy-done.4, bf16[512,2048]{1,0:T(8,128)(2,1)} %bitcast.6.refs_1_.refs_2_), custom_call_target="tpu_custom_call" | custom-call | tf_op jit(solution)/shard_map/back_early/pallas_call | solution.py:83
  90.2 3.8 %back_late.1 = (bf16[512,768]{1,0:T(8,128)(2,1)S(1)}, bf16[512,128]{1,0:T(8,128)(2,1)S(1)}) custom-call(s32[1]{0:T(128)} %bitcast.place_ref, bf16[4096,384]{1,0:T(8,128)(2,1)S(1)} %copy-done.4, bf16[512,2048]{1,0:T(8,128)(2,1)S(1)} %collective-permute-done.6.refs_1_.refs_3_, f32[512,384]{1,0:T(8,128)S(1)} %back_early.1.refs_2_, f32[512,768]{1,0:T(8,128)S(1)} %copy-done.14, ...), custom_call_target="tpu_custom_call" | custom-call | tf_op jit(solution)/shard_map/back_late/pallas_call | solution.py:83
  94.1 3.3 %row_parts.2.refs_2_ = bf16[512,2048]{1,0:T(8,128)(2,1)S(1)} custom-call(s32[1]{0:T(128)} %bitcast.place_ref, bf16[768,2048]{1,0:T(8,128)(2,1)S(1)} %copy-done.10, bf16[512,768]{1,0:T(8,128)(2,1)S(1)} %get-tuple-element.53.refs_1_.refs_4_), custom_call_target="tpu_custom_call" | custom-call | tf_op jit(solution)/shard_map/row_parts/pallas_call | solution.py:83
  97.4 4.3 %row_parts.3 = bf16[512,2176]{1,0:T(8,128)(2,1)} custom-call(s32[1]{0:T(128)} %bitcast.place_ref, bf16[768,2048]{1,0:T(8,128)(2,1)S(1)} %turn_lent.1.refs_0_, bf16[512,768]{1,0:T(8,128)(2,1)S(1)} %collective-permute-done.7.refs_1_, bf16[512,2048]{1,0:T(8,128)(2,1)S(1)} %row_parts.2.refs_2_, bf16[512,128]{1,0:T(8,128)(2,1)S(1)} %get-tuple-element.57.refs_3_), custom_call_target="tpu_custom_call" | custom-call | tf_op jit(solution)/shard_map/row_parts/pallas_call | solution.py:83
  101.7 5.2 %all-to-all-start.2 = ((bf16[64,8,2176]{2,1,0:T(8,128)(2,1)}), bf16[64,8,2176]{2,1,0:T(8,128)(2,1)S(1)}, u32[]{:S(2)}, u32[]{:S(2)}) async-start(bf16[64,8,2176]{2,1,0:T(8,128)(2,1)} %bitcast.18), calls=%async_computation.2 | async-start | bytes 4456448 | tf_op jit(solution)/shard_map/all_to_all | solution.py:359
  107.0 1.6 %copy-done.6 = bf16[512,2048]{1,0:T(8,128)(2,1)S(1)} copy-done((bf16[512,2048]{1,0:T(8,128)(2,1)S(1)}, bf16[512,2048]{1,0:T(8,128)(2,1)}, u32[]{:S(2)}) %copy-start.6) | copy-done | bytes 2097176
  108.5 8.4 %weight_grads.1 = (f32[8,128]{1,0:T(8,128)S(1)}, bf16[1,4096,384]{2,1,0:T(8,128)(2,1)}, bf16[1,4096,384]{2,1,0:T(8,128)(2,1)}, bf16[1,384,4096]{2,1,0:T(8,128)(2,1)}) custom-call(s32[1]{0:T(128)} %bitcast.place_ref, bf16[512,2048]{1,0:T(8,128)(2,1)} %bitcast.3.refs_2_.refs_0_, bf16[512,2048]{1,0:T(8,128)(2,1)} %collective-permute-done.4.refs_3_.refs_1_, ...), custom_call_target="tpu_custom_call" | custom-call | tf_op jit(solution)/shard_map/weight_grads/pallas_call | solution.py:83
  117.0 18.8 %all-to-all-done.2 = bf16[64,8,2176]{2,1,0:T(8,128)(2,1)S(1)} async-done(((bf16[64,8,2176]{2,1,0:T(8,128)(2,1)}), bf16[64,8,2176]{2,1,0:T(8,128)(2,1)S(1)}, u32[]{:S(2)}, u32[]{:S(2)}) %all-to-all-start.2) | async-done | bytes 2228256 | tf_op jit(solution)/shard_map/all_to_all | solution.py:359
  135.8 2.2 %gather_rows.1 = (bf16[16,2048]{1,0:T(8,128)(2,1)S(1)}, bf16[16,2048]{1,0:T(8,128)(2,1)S(1)}, f32[4,16]{1,0:T(4,128)S(1)}, f32[4,16]{1,0:T(4,128)S(1)}) custom-call(s32[1]{0:T(128)} %bitcast.place_ref, bf16[512,2176]{1,0:T(8,128)(2,1)S(1)} %bitcast.12, bf16[160,512]{1,0:T(8,128)(2,1)} %get-tuple-element.58.refs_1_, f32[8,128]{1,0:T(8,128)S(1)} %get-tuple-element.59.refs_2_), custom_call_target="tpu_custom_call" | custom-call | tf_op jit(solution)/shard_map/gather_rows/pallas_call | solution.py:83
  138.0 3.2 %collective-permute-start.9 = (f32[4,16]{1,0:T(4,128)S(1)}, f32[4,16]{1,0:T(4,128)S(1)}, u32[]{:S(2)}, u32[]{:S(2)}) collective-permute-start(f32[4,16]{1,0:T(4,128)S(1)} %get-tuple-element.63), channel_id=1, source_target_pairs={{0,1},{1,0},{2,3},{3,2},{4,5},{5,4},{6,7},{7,6},{8,9},{9,8},{10,11... | collective-permute-start | bytes 776 | tf_op jit(solution)/shard_map/ppermute | solution.py:356
  (50 shorter events, 4.8 us)
Async XLA Ops:
  0.6 2.9 %collective-permute-start.1 = (bf16[16,4096]{1,0:T(8,128)(2,1)}, bf16[16,4096]{1,0:T(8,128)(2,1)S(1)}, u32[]{:S(2)}, u32[]{:S(2)}) collective-permute-start(bf16[16,4096]{1,0:T(8,128)(2,1)} %refs_2_.2), channel_id=1, source_target_pairs={{0,1},{1,0},{2,3},{3,2},{4,5},{5,4},{6,7},{7,6},{8,9},{9,8},{10,11... | collective-permute-start | bytes 393224 | tf_op jit(solution)/shard_map/ppermute | solution.py:356
  2.1 1.4 collective-permute-start
  4.2 14.7 %copy-start.15 = (bf16[16,4096]{1,0:T(8,128)(2,1)S(1)}, bf16[16,4096]{1,0:T(8,128)(2,1)}, u32[]{:S(2)}) copy-start(bf16[16,4096]{1,0:T(8,128)(2,1)} %refs_4_) | copy-start | bytes 393220
  4.2 15.3 %copy-start.16 = (f32[16,4]{0,1:T(4,128)S(1)}, f32[16,4]{0,1:T(4,128)}, u32[]{:S(2)}) copy-start(f32[16,4]{0,1:T(4,128)} %param.9) | copy-start | bytes 772
  4.2 16.5 %copy-start.17 = (s32[16,4]{0,1:T(4,128)S(1)}, s32[16,4]{0,1:T(4,128)}, u32[]{:S(2)}) copy-start(s32[16,4]{0,1:T(4,128)} %param.10) | copy-start | bytes 772
  7.1 13.5 %copy-start.19 = (s32[4,16]{1,0:T(4,128)S(1)}, s32[4,16]{1,0:T(4,128)}, u32[]{:S(2)}) copy-start(s32[4,16]{1,0:T(4,128)} %copy-done.18) | copy-start | bytes 772
  7.1 17.3 %copy-start = (bf16[1,4096,384]{2,1,0:T(8,128)(2,1)S(1)}, bf16[1,4096,384]{2,1,0:T(8,128)(2,1)}, u32[]{:S(2)}) copy-start(bf16[1,4096,384]{2,1,0:T(8,128)(2,1)} %refs_0_.5) | copy-start | bytes 9437188
  7.1 39.4 %all-to-all-start = ((bf16[64,8,2048]{2,1,0:T(8,128)(2,1)}), bf16[64,8,2048]{2,1,0:T(8,128)(2,1)}, u32[]{:S(2)}, u32[]{:S(2)}) async-start(bf16[64,8,2048]{2,1,0:T(8,128)(2,1)} %bitcast.19), calls=%async_computation | async-start | bytes 4194304 | tf_op jit(solution)/shard_map/all_to_all | solution.py:359
  18.9 1.7 %collective-permute-start.3 = (bf16[16,4096]{1,0:T(8,128)(2,1)S(1)}, bf16[16,4096]{1,0:T(8,128)(2,1)S(1)}, u32[]{:S(2)}, u32[]{:S(2)}) collective-permute-start(bf16[16,4096]{1,0:T(8,128)(2,1)S(1)} %copy-done.15), channel_id=1, source_target_pairs={{0,1},{1,0},{2,3},{3,2},{4,5},{5,4},{6,7},{7,6},{8,9},{9,8},{10,11... | collective-permute-start | bytes 393224 | tf_op jit(solution)/shard_map/ppermute | solution.py:356
  19.5 1.2 collective-permute-start.2
  24.4 1.9 %copy-start.1 = (bf16[1,4096,384]{2,1,0:T(8,128)(2,1)S(1)}, bf16[1,4096,384]{2,1,0:T(8,128)(2,1)}, u32[]{:S(2)}) copy-start(bf16[1,4096,384]{2,1,0:T(8,128)(2,1)} %refs_1_.5) | copy-start | bytes 9437188
  26.3 2.8 %copy-start.11 = (bf16[1,384,4096]{2,1,0:T(8,128)(2,1)S(1)}, bf16[1,384,4096]{2,1,0:T(8,128)(2,1)}, u32[]{:S(2)}) copy-start(bf16[1,384,4096]{2,1,0:T(8,128)(2,1)} %refs_2_.3) | copy-start | bytes 9437188
  26.9 1.7 %copy-start.12 = (bf16[2048,768]{1,0:T(8,128)(2,1)}, bf16[2048,768]{1,0:T(8,128)(2,1)S(1)}, u32[]{:S(2)}) copy-start(bf16[2048,768]{1,0:T(8,128)(2,1)S(1)} %lend.1) | copy-start | bytes 9437188
  31.9 1.7 %copy-start.3 = (bf16[4096,384]{1,0:T(8,128)(2,1)}, bf16[4096,384]{1,0:T(8,128)(2,1)S(1)}, u32[]{:S(2)}) copy-start(bf16[4096,384]{1,0:T(8,128)(2,1)S(1)} %get-tuple-element.47.refs_0_) | copy-start | bytes 9437188
  33.5 1.7 %copy-start.9 = (bf16[768,2048]{1,0:T(8,128)(2,1)}, bf16[768,2048]{1,0:T(8,128)(2,1)S(1)}, u32[]{:S(2)}) copy-start(bf16[768,2048]{1,0:T(8,128)(2,1)S(1)} %get-tuple-element.54.refs_0_) | copy-start | bytes 9437188
  46.6 21.3 %collective-permute-start.5 = (bf16[2048,768]{1,0:T(8,128)(2,1)}, bf16[2048,768]{1,0:T(8,128)(2,1)}, u32[]{:S(2)}, u32[]{:S(2)}) collective-permute-start(bf16[2048,768]{1,0:T(8,128)(2,1)} %copy-done.12), channel_id=1, source_target_pairs={{0,1},{1,0},{2,3},{3,2},{4,5},{5,4},{6,7},{7,6},{8,9},{9,8},{10,11... | collective-permute-start | bytes 9437192 | tf_op jit(solution)/shard_map/ppermute | solution.py:356
  49.4 8.6 %collective-permute-start.4 = (bf16[512,2048]{1,0:T(8,128)(2,1)}, bf16[512,2048]{1,0:T(8,128)(2,1)}, u32[]{:S(2)}, u32[]{:S(2)}) collective-permute-start(bf16[512,2048]{1,0:T(8,128)(2,1)} %bitcast.3.refs_2_.refs_0_), channel_id=1, source_target_pairs={{0,1},{1,0},{2,3},{3,2},{4,5},{5,4},{6,7},{7,6},{8,9},{9,8},{10,11... | collective-permute-start | bytes 6291464 | tf_op jit(solution)/shard_map/ppermute | solution.py:356
  49.4 33.0 %all-to-all-start.1 = ((bf16[64,8,2048]{2,1,0:T(8,128)(2,1)}), bf16[64,8,2048]{2,1,0:T(8,128)(2,1)}, u32[]{:S(2)}, u32[]{:S(2)}) async-start(bf16[64,8,2048]{2,1,0:T(8,128)(2,1)} %bitcast.20), calls=%async_computation.1 | async-start | bytes 4194304 | tf_op jit(solution)/shard_map/all_to_all | solution.py:359
  58.0 1.9 %copy-start.2 = (bf16[1,4096,384]{2,1,0:T(8,128)(2,1)S(1)}, bf16[1,4096,384]{2,1,0:T(8,128)(2,1)}, u32[]{:S(2)}) copy-start(bf16[1,4096,384]{2,1,0:T(8,128)(2,1)} %refs_1_.5) | copy-start | bytes 9437188
  66.7 1.2 copy-start.13
  82.4 7.8 %collective-permute-start.6 = (bf16[512,2048]{1,0:T(8,128)(2,1)}, bf16[512,2048]{1,0:T(8,128)(2,1)S(1)}, u32[]{:S(2)}, u32[]{:S(2)}) collective-permute-start(bf16[512,2048]{1,0:T(8,128)(2,1)} %bitcast.6.refs_1_.refs_2_), channel_id=1, source_target_pairs={{0,1},{1,0},{2,3},{3,2},{4,5},{5,4},{6,7},{7,6},{8,9},{9,8},{10,11... | collective-permute-start | bytes 6291464 | tf_op jit(solution)/shard_map/ppermute | solution.py:356
  85.4 1.9 %copy-start.4 = (bf16[4096,384]{1,0:T(8,128)(2,1)S(1)}, bf16[4096,384]{1,0:T(8,128)(2,1)}, u32[]{:S(2)}) copy-start(bf16[4096,384]{1,0:T(8,128)(2,1)} %copy-done.3) | copy-start | bytes 9437188
  87.3 2.9 %copy-start.14 = (f32[512,768]{1,0:T(8,128)S(1)}, f32[512,768]{1,0:T(8,128)}, u32[]{:S(2)}) copy-start(f32[512,768]{1,0:T(8,128)} %copy-done.13) | copy-start | bytes 4718596
  90.1 3.9 %copy-start.10 = (bf16[768,2048]{1,0:T(8,128)(2,1)S(1)}, bf16[768,2048]{1,0:T(8,128)(2,1)}, u32[]{:S(2)}) copy-start(bf16[768,2048]{1,0:T(8,128)(2,1)} %copy-done.9) | copy-start | bytes 9437188
  90.2 3.8 %copy-start.5 = (bf16[512,2048]{1,0:T(8,128)(2,1)}, bf16[512,2048]{1,0:T(8,128)(2,1)S(1)}, u32[]{:S(2)}) copy-start(bf16[512,2048]{1,0:T(8,128)(2,1)S(1)} %collective-permute-done.6.refs_1_.refs_3_) | copy-start | bytes 6291460
  94.0 7.8 %copy-start.7 = (bf16[512,768]{1,0:T(8,128)(2,1)}, bf16[512,768]{1,0:T(8,128)(2,1)S(1)}, u32[]{:S(2)}) copy-start(bf16[512,768]{1,0:T(8,128)(2,1)S(1)} %get-tuple-element.53.refs_1_.refs_4_) | copy-start | bytes 2359300
  94.0 3.4 %collective-permute-start.7 = (bf16[512,768]{1,0:T(8,128)(2,1)S(1)}, bf16[512,768]{1,0:T(8,128)(2,1)S(1)}, u32[]{:S(2)}, u32[]{:S(2)}) collective-permute-start(bf16[512,768]{1,0:T(8,128)(2,1)S(1)} %get-tuple-element.53.refs_1_.refs_4_), channel_id=1, source_target_pairs={{0,1},{1,0},{2,3},{3,2},{4,5},{5,4},{6,7},{7,6},{8,9},{9,8},{10,11... | collective-permute-start | bytes 2359304 | tf_op jit(solution)/shard_map/ppermute | solution.py:356
  101.7 5.2 %copy-start.8 = (bf16[512,768]{1,0:T(8,128)(2,1)S(1)}, bf16[512,768]{1,0:T(8,128)(2,1)}, u32[]{:S(2)}) copy-start(bf16[512,768]{1,0:T(8,128)(2,1)} %copy-done.7) | copy-start | bytes 2359300
  101.7 34.1 %all-to-all-start.2 = ((bf16[64,8,2176]{2,1,0:T(8,128)(2,1)}), bf16[64,8,2176]{2,1,0:T(8,128)(2,1)S(1)}, u32[]{:S(2)}, u32[]{:S(2)}) async-start(bf16[64,8,2176]{2,1,0:T(8,128)(2,1)} %bitcast.18), calls=%async_computation.2 | async-start | bytes 4456448 | tf_op jit(solution)/shard_map/all_to_all | solution.py:359
  107.0 1.6 %copy-start.6 = (bf16[512,2048]{1,0:T(8,128)(2,1)S(1)}, bf16[512,2048]{1,0:T(8,128)(2,1)}, u32[]{:S(2)}) copy-start(bf16[512,2048]{1,0:T(8,128)(2,1)} %copy-done.5) | copy-start | bytes 6291460
  138.0 4.1 %collective-permute-start.9 = (f32[4,16]{1,0:T(4,128)S(1)}, f32[4,16]{1,0:T(4,128)S(1)}, u32[]{:S(2)}, u32[]{:S(2)}) collective-permute-start(f32[4,16]{1,0:T(4,128)S(1)} %get-tuple-element.63), channel_id=1, source_target_pairs={{0,1},{1,0},{2,3},{3,2},{4,5},{5,4},{6,7},{7,6},{8,9},{9,8},{10,11... | collective-permute-start | bytes 776 | tf_op jit(solution)/shard_map/ppermute | solution.py:356
  141.3 1.4 collective-permute-start.8
  (2 other events, 1.2 us)

commit v2 on v1

--- a/solution.py
+++ b/solution.py
@@ -21,6 +21,7 @@
 NT = (((1,), (1,)), ((), ()))
 SMEM = pl.BlockSpec(memory_space=pltpu.SMEM)
 HBM = pl.BlockSpec(memory_space=pltpu.HBM)
+VMEM = pl.BlockSpec(memory_space=pltpu.VMEM)
 
 
 def dot(a, b, dims=(((1,), (0,)), ((), ()))):
@@ -88,6 +89,19 @@
         scratch_shapes=[pltpu.VMEM(x.shape, x.dtype) for x in args[raw:]]
         + [pltpu.VMEM(shape, kind) for shape, kind in outs[:count]]
         + [pltpu.SemaphoreType.DMA((max(given, 1),)), pltpu.SemaphoreType.DMA((max(count, 1),)), *scratch],
+        compiler_params=pltpu.CompilerParams(vmem_limit_bytes=limit),
+        name=name,
+    )(place, *args)
+
+
+def call_near(kernel, name, outs, place, *args, direct=0, scratch=(), limit=28 << 20):
+    count = len(outs) - direct
+    return pl.pallas_call(
+        kernel,
+        in_specs=[SMEM] + [VMEM] * len(args),
+        out_specs=[VMEM] * count + [HBM] * direct,
+        out_shape=[jax.ShapeDtypeStruct(*out) for out in outs[:count]] + [pltpu.HBM(*out) for out in outs[count:]],
+        scratch_shapes=list(scratch),
         compiler_params=pltpu.CompilerParams(vmem_limit_bytes=limit),
         name=name,
     )(place, *args)
@@ -231,27 +245,17 @@
     factors_ref[:, ff:] = active
 
 
-def back_product(which, back_hbm, grads_hbm, rows_ref, back_ref, sems):
-    parts, _, step = rows_ref.shape
-    groups = []
-    for n in range(parts):
-        at = columns((which * parts + n) * step, step)
-        pairs = ((grads_hbm.at[:, pl.ds(n * step, step)], rows_ref.at[n]), (back_hbm.at[at, :], back_ref.at[n]))
-        groups.append([pltpu.make_async_copy(*pair, sems.at[2 * n + k]) for k, pair in enumerate(pairs)])
-    stages = Stages(groups, parts)
-    scaled = 0.0
-    for n in range(parts):
-        stages.wait(n)
-        scaled += dot(rows_ref[n], back_ref[n])
-    return scaled
-
-
-def back_early_kernel(place_ref, back_hbm, own_hbm, out_ref, *own):
-    out_ref[...] = back_product(place_ref[0], back_hbm, own_hbm, *own)
-
-
-def back_late_kernel(place_ref, back_hbm, other_hbm, sum_ref, factors_ref, hidden_ref, deltas_ref, score_ref, *own):
-    scaled = back_product(1 - place_ref[0], back_hbm, other_hbm, *own) + sum_ref[...]
+def back_product(which, back_ref, grads_ref):
+    half = grads_ref.shape[1]
+    return dot(grads_ref[...], back_ref[columns(which * half, half), :])
+
+
+def back_early_kernel(place_ref, back_ref, own_ref, out_ref):
+    out_ref[...] = back_product(place_ref[0], back_ref, own_ref)
+
+
+def back_late_kernel(place_ref, back_ref, other_ref, sum_ref, factors_ref, hidden_ref, deltas_ref, score_ref):
+    scaled = back_product(1 - place_ref[0], back_ref, other_ref) + sum_ref[...]
     ff = scaled.shape[1]
     score = jnp.sum(scaled * hidden_ref[...].astype(F32), axis=1, keepdims=True)
     deltas_ref[:, :ff] = (scaled * factors_ref[:, :ff]).astype(BF16)
@@ -259,29 +263,24 @@
     score_ref[...] = jnp.broadcast_to(score, score_ref.shape).astype(BF16)
 
 
-def parts_kernel(last, place_ref, turned_hbm, deltas_ref, *refs):
-    if last:
-        before_ref, score_ref, *refs = refs
-    out_hbm, weight_ref, part_ref, sems, out_sems = refs
-    steps, _, step = weight_ref.shape
+def parts_own_kernel(place_ref, turned_ref, deltas_ref, out_ref):
+    step = 512
+    deltas = deltas_ref[...]
+    for at in range(0, out_ref.shape[1], step):
+        out_ref[:, at : at + step] = dot(deltas, turned_ref[:, at : at + step]).astype(BF16)
+
+
+def parts_sum_kernel(place_ref, turned_ref, deltas_ref, before_ref, score_ref, out_hbm, part_ref, sems):
+    steps, _, step = part_ref.shape
     half = steps * step
-    stages = Stages([
-        [pltpu.make_async_copy(turned_hbm.at[:, pl.ds(n * step, step)], weight_ref.at[n], sems.at[n])]
-        for n in range(steps)
-    ], 2)
+    outs = [pltpu.make_async_copy(score_ref, out_hbm.at[:, pl.ds(half, META)], sems.at[steps])]
+    outs[0].start()
     deltas = deltas_ref[...]
-    outs = []
     for n in range(steps):
-        stages.wait(n)
-        part = dot(deltas, weight_ref[n])
-        if last:
-            part += before_ref[:, n * step : (n + 1) * step].astype(F32)
+        at = n * step
+        part = dot(deltas, turned_ref[:, at : at + step]) + before_ref[:, at : at + step].astype(F32)
         part_ref[n] = part.astype(BF16)
-        outs.append(pltpu.make_async_copy(part_ref.at[n], out_hbm.at[:, pl.ds(n * step, step)], out_sems.at[n]))
-        outs[-1].start()
-    if last:
-        score_ref.wait()
-        outs.append(pltpu.make_async_copy(score_ref.target, out_hbm.at[:, pl.ds(half, META)], out_sems.at[steps]))
+        outs.append(pltpu.make_async_copy(part_ref.at[n], out_hbm.at[:, pl.ds(at, step)], sems.at[n]))
         outs[-1].start()
     for copy in outs:
         copy.wait()
@@ -365,7 +364,8 @@
     scratch = [pltpu.VMEM((half // step, lines, step), BF16), pltpu.SemaphoreType.DMA((half // step,))]
     out = ((lines, half), BF16)
     rows_out = call(
-        build_kernel, "build_rows", [out], place, *ids_pair, *tokens_pair, direct=1, scratch=scratch, limit=63 << 20
+        build_kernel, "build_rows", [out], place, *[pltpu.with_memory_space_constraint(x, pltpu.HBM) for x in ids_pair],
+        pltpu.with_memory_space_constraint(tokens, pltpu.HBM), tokens_pair[1], direct=1, scratch=scratch, far=True,
     )[0]
     later = after(comb, out_grad, rows_out)[:2]
     comb_pair, out_grad_pair = [(x, swap(x)) for x in later]
@@ -402,42 +402,24 @@
     )
     grads, factors, hidden, parts_other = after(deliver(grads_out), factors, hidden, parts_other)
     grads_pair = (grads, swap(grads))
-    scratch = [
-        pltpu.VMEM((half // step, lines, step), BF16),
-        pltpu.VMEM((half // step, step, ff), BF16),
-        pltpu.SemaphoreType.DMA((2 * half // step,)),
-    ]
-    scaled = call(
-        back_early_kernel, "back_early", [((lines, ff), F32)], place, back, grads, raw=2, scratch=scratch
-    )[0]
+    scaled = call_near(back_early_kernel, "back_early", [((lines, ff), F32)], place, back, grads)[0]
     other, scaled = after(grads_pair[1], scaled)
-    deltas, score = call(
+    deltas, score = call_near(
         back_late_kernel,
         "back_late",
         [((lines, 2 * ff), BF16), ((lines, META), BF16)],
-        place, back, other, scaled, factors, hidden, raw=2, scratch=scratch,
-    )
-
-    def parts(last, size, *args):
-        return call(
-            functools.partial(parts_kernel, last),
-            "row_parts",
-            [((lines, size), BF16)],
-            place, *args,
-            raw=1,
-            direct=1,
-            far=last,
-            scratch=[
-                pltpu.VMEM((half // step, 2 * ff, step), BF16),
-                pltpu.VMEM((half // step, lines, step), BF16),
-                pltpu.SemaphoreType.DMA((half // step,)),
-                pltpu.SemaphoreType.DMA((half // step + 1,)),
-            ],
-        )[0]
-
-    part = parts(False, half, parts_own, deltas)
+        place, back, other, scaled, factors, hidden,
+    )
+    part = call_near(parts_own_kernel, "parts_own", [((lines, half), BF16)], place, parts_own, deltas)[0]
     deltas_other, part = after(swap(deltas), part)
-    parts_sum = parts(True, half + META, parts_other, deltas_other, part, score)
+    parts_sum = call_near(
+        parts_sum_kernel,
+        "parts_sum",
+        [((lines, half + META), BF16)],
+        place, parts_other, deltas_other, part, score,
+        direct=1,
+        scratch=[pltpu.VMEM((half // step, lines, step), BF16), pltpu.SemaphoreType.DMA((half // step + 1,))],
+    )[0]
     mark, gate_grad, up_grad, down_grad = call(
         weights_kernel,
         "weight_grads",

time: 144 us -> 139 us (0.965)
  Pallas kernels: 44.8 us -> 39.5 us
  starting transfers between devices: 34.2 us -> 32.7 us
    pallas_call x12 -> x8, Pallas kernels: 44.8 us -> 30.6 us  [call(): pl.pallas_call(body, in_specs=[SMEM] + [HBM] * len(args), out_specs=[HBM]...]
    pallas_call x0 -> x4, Pallas kernels: none -> 8.86 us  [call_near(): pl.pallas_call(kernel, in_specs=[SMEM] + [VMEM] * len(args), out_specs=[V...]
    ppermute x10, starting transfers between devices: 11.5 us -> 10 us  [swap(): return lax.ppermute(x, 'core', [(0, 1), (1, 0)])]
    unnamed x42 -> x40, local copies, waits for them, and re-layouts: 14.7 us -> 16 us
where the time goes in v2:
time: 139 us
  waiting for transfers between devices  48.2 us (35%)
  Pallas kernels  39.5 us (28%)
  starting transfers between devices  32.7 us (24%)
  local copies, waits for them, and re-layouts  16 us (12%)
    all_to_all x3, waiting for transfers between devices, deliver(): lax.all_to_all(x.reshape(chips, SLOTS, x.shape[1]), CHIPS, split_axis=0,...  42.2 us
    pallas_call x8, Pallas kernels, call(): pl.pallas_call(body, in_specs=[SMEM] + [HBM] * len(args), out_specs=[HBM]...  30.6 us
    all_to_all x3, starting transfers between devices, deliver(): lax.all_to_all(x.reshape(chips, SLOTS, x.shape[1]), CHIPS, split_axis=0,...  22.7 us
    unnamed x40, local copies, waits for them, and re-layouts  16 us
    ppermute x10, starting transfers between devices, swap(): return lax.ppermute(x, 'core', [(0, 1), (1, 0)])  10 us
    pallas_call x4, Pallas kernels, call_near(): pl.pallas_call(kernel, in_specs=[SMEM] + [VMEM] * len(args), out_specs=[V...  8.86 us
    ppermute x10, waiting for transfers between devices, swap(): return lax.ppermute(x, 'core', [(0, 1), (1, 0)])  5.94 us
  transfers between devices with their start and end apart: 13, of which 7 were waited for; matrix products, arithmetic and copies ran while one was open for 0% of the time, Pallas kernels for 22%

profile of v2, /device:TPU:1, one launch (start us, length us, event | category | flops | bytes accessed | tf_op | source)
XLA Modules:
  0.0 138.5 jit_solution(9414810429205023964)
XLA Ops:
  0.6 1.5 %collective-permute-start.1 = (bf16[16,4096]{1,0:T(8,128)(2,1)}, bf16[16,4096]{1,0:T(8,128)(2,1)S(1)}, u32[]{:S(2)}, u32[]{:S(2)}) collective-permute-start(bf16[16,4096]{1,0:T(8,128)(2,1)} %refs_2_.2), channel_id=1, source_target_pairs={{0,1},{1,0},{2,3},{3,2},{4,5},{5,4},{6,7},{7,6},{8,9},{9,8},{10,11... | collective-permute-start | bytes 393224 | tf_op jit(solution)/shard_map/ppermute | solution.py:355
  2.2 1.3 collective-permute-done.refs_1_
  4.1 3.0 %build_rows.1 = bf16[512,2048]{1,0:T(8,128)(2,1)} custom-call(s32[1]{0:T(128)} %bitcast.place_ref, s32[4,16]{1,0:T(4,128)} %bitcast.16, s32[4,16]{1,0:T(4,128)} %copy-done.18, bf16[16,4096]{1,0:T(8,128)(2,1)} %refs_2_.2, bf16[16,4096]{1,0:T(8,128)(2,1)S(1)} %collective-permute-done.1.refs_3_), custom_call_target="tpu_custom_call" | custom-call | tf_op jit(solution)/shard_map/build_rows/pallas_call | solution.py:84
  7.1 11.5 %all-to-all-start = ((bf16[64,8,2048]{2,1,0:T(8,128)(2,1)}), bf16[64,8,2048]{2,1,0:T(8,128)(2,1)}, u32[]{:S(2)}, u32[]{:S(2)}) async-start(bf16[64,8,2048]{2,1,0:T(8,128)(2,1)} %bitcast.19), calls=%async_computation | async-start | bytes 4194304 | tf_op jit(solution)/shard_map/all_to_all | solution.py:358
  20.3 3.8 %build_grads.1 = (bf16[160,512]{1,0:T(8,128)(2,1)}, bf16[512,2048]{1,0:T(8,128)(2,1)}) custom-call(s32[1]{0:T(128)} %bitcast.place_ref, s32[4,16]{1,0:T(4,128)S(1)} %bitcast.17, s32[4,16]{1,0:T(4,128)S(1)} %copy-done.19, f32[4,16]{1,0:T(4,128)S(1)} %bitcast.14, f32[4,16]{1,0:T(4,128)S(1)} %collective-permute-done.2.refs_3_, bf16[16,4096]{1,0:T(8,128)(2,1)S(1)} %copy-done.15, ...), custom_call_target="tpu_custom_call" | custom-call | tf_op jit(solution)/shard_map/build_grads/pallas_call | solution.py:84
  24.1 1.9 %copy-done.1 = bf16[1,4096,384]{2,1,0:T(8,128)(2,1)S(1)} copy-done((bf16[1,4096,384]{2,1,0:T(8,128)(2,1)S(1)}, bf16[1,4096,384]{2,1,0:T(8,128)(2,1)}, u32[]{:S(2)}) %copy-start.1) | copy-done | bytes 3145752
  26.6 1.7 %copy-done.12 = bf16[2048,768]{1,0:T(8,128)(2,1)} copy-done((bf16[2048,768]{1,0:T(8,128)(2,1)}, bf16[2048,768]{1,0:T(8,128)(2,1)S(1)}, u32[]{:S(2)}) %copy-start.12) | copy-done | bytes 3145752
  28.8 2.8 %turn.1 = (bf16[4096,384]{1,0:T(8,128)(2,1)S(1)}, bf16[768,2048]{1,0:T(8,128)(2,1)S(1)}) custom-call(s32[1]{0:T(128)} %bitcast.place_ref, bf16[1,4096,384]{2,1,0:T(8,128)(2,1)S(1)} %copy-done, bf16[1,4096,384]{2,1,0:T(8,128)(2,1)S(1)} %copy-done.1, bf16[1,384,4096]{2,1,0:T(8,128)(2,1)S(1)} %copy-done.11, ...), custom_call_target="tpu_custom_call" | custom-call | tf_op jit(solution)/shard_map/turn/pallas_call | solution.py:84
  31.6 1.7 %copy-done.3 = bf16[4096,384]{1,0:T(8,128)(2,1)} copy-done((bf16[4096,384]{1,0:T(8,128)(2,1)}, bf16[4096,384]{1,0:T(8,128)(2,1)S(1)}, u32[]{:S(2)}) %copy-start.3) | copy-done | bytes 3145752
  33.2 1.7 %copy-done.9 = bf16[768,2048]{1,0:T(8,128)(2,1)} copy-done((bf16[768,2048]{1,0:T(8,128)(2,1)}, bf16[768,2048]{1,0:T(8,128)(2,1)S(1)}, u32[]{:S(2)}) %copy-start.9) | copy-done | bytes 3145752
  34.9 11.3 %all-to-all-done = bf16[64,8,2048]{2,1,0:T(8,128)(2,1)} async-done(((bf16[64,8,2048]{2,1,0:T(8,128)(2,1)}), bf16[64,8,2048]{2,1,0:T(8,128)(2,1)}, u32[]{:S(2)}, u32[]{:S(2)}) %all-to-all-start) | async-done | bytes 2097184 | tf_op jit(solution)/shard_map/all_to_all | solution.py:358
  46.2 2.8 %collective-permute-start.5 = (bf16[2048,768]{1,0:T(8,128)(2,1)}, bf16[2048,768]{1,0:T(8,128)(2,1)}, u32[]{:S(2)}, u32[]{:S(2)}) collective-permute-start(bf16[2048,768]{1,0:T(8,128)(2,1)} %copy-done.12), channel_id=1, source_target_pairs={{0,1},{1,0},{2,3},{3,2},{4,5},{5,4},{6,7},{7,6},{8,9},{9,8},{10,11... | collective-permute-start | bytes 9437192 | tf_op jit(solution)/shard_map/ppermute | solution.py:355
  49.0 5.7 %all-to-all-start.1 = ((bf16[64,8,2048]{2,1,0:T(8,128)(2,1)}), bf16[64,8,2048]{2,1,0:T(8,128)(2,1)}, u32[]{:S(2)}, u32[]{:S(2)}) async-start(bf16[64,8,2048]{2,1,0:T(8,128)(2,1)} %bitcast.20), calls=%async_computation.1 | async-start | bytes 4194304 | tf_op jit(solution)/shard_map/all_to_all | solution.py:358
  54.8 2.9 %collective-permute-done.4.refs_3_.refs_1_ = bf16[512,2048]{1,0:T(8,128)(2,1)} collective-permute-done((bf16[512,2048]{1,0:T(8,128)(2,1)}, bf16[512,2048]{1,0:T(8,128)(2,1)}, u32[]{:S(2)}, u32[]{:S(2)}) %collective-permute-start.4) | collective-permute-done | bytes 2097184 | tf_op jit(solution)/shard_map/ppermute | solution.py:355
  57.7 1.9 %copy-done.2 = bf16[1,4096,384]{2,1,0:T(8,128)(2,1)S(1)} copy-done((bf16[1,4096,384]{2,1,0:T(8,128)(2,1)S(1)}, bf16[1,4096,384]{2,1,0:T(8,128)(2,1)}, u32[]{:S(2)}) %copy-start.2) | copy-done | bytes 3145752
  59.6 6.8 %gate_up.1 = (f32[512,768]{1,0:T(8,128)S(1)}, bf16[512,384]{1,0:T(8,128)(2,1)S(1)}) custom-call(s32[1]{0:T(128)} %bitcast.place_ref, bf16[1,4096,384]{2,1,0:T(8,128)(2,1)S(1)} %copy-done, bf16[1,4096,384]{2,1,0:T(8,128)(2,1)S(1)} %copy-done.2, bf16[512,2048]{1,0:T(8,128)(2,1)} %bitcast.3.refs_2_.refs_0_, bf16[512,2048]{1,0:T(8,128)(2,1)} %collective-permute-done.4.refs_3_.refs_1_), custom_call_target="tpu_custom_call" | custom-call | tf_op jit(solution)/shard_map/gate_up/pallas_call | solution.py:84
  66.4 1.2 copy-done.13
  67.6 3.1 %turn_lent.1.turned_ref = bf16[768,2048]{1,0:T(8,128)(2,1)S(1)} custom-call(s32[1]{0:T(128)} %bitcast.place_ref, bf16[2048,768]{1,0:T(8,128)(2,1)} %collective-permute-done.5.refs_0_), custom_call_target="tpu_custom_call" | custom-call | tf_op jit(solution)/shard_map/turn_lent/pallas_call | solution.py:84
  70.7 11.4 %all-to-all-done.1 = bf16[64,8,2048]{2,1,0:T(8,128)(2,1)} async-done(((bf16[64,8,2048]{2,1,0:T(8,128)(2,1)}), bf16[64,8,2048]{2,1,0:T(8,128)(2,1)}, u32[]{:S(2)}, u32[]{:S(2)}) %all-to-all-start.1) | async-done | bytes 2097184 | tf_op jit(solution)/shard_map/all_to_all | solution.py:358
  82.1 3.0 %collective-permute-start.6 = (bf16[512,2048]{1,0:T(8,128)(2,1)}, bf16[512,2048]{1,0:T(8,128)(2,1)S(1)}, u32[]{:S(2)}, u32[]{:S(2)}) collective-permute-start(bf16[512,2048]{1,0:T(8,128)(2,1)} %bitcast.6.own_ref.refs_2_), channel_id=1, source_target_pairs={{0,1},{1,0},{2,3},{3,2},{4,5},{5,4},{6,7},{7,6},{8,9},{9,8},{10,11... | collective-permute-start | bytes 6291464 | tf_op jit(solution)/shard_map/ppermute | solution.py:355
  85.1 1.9 %copy-done.4 = bf16[4096,384]{1,0:T(8,128)(2,1)S(1)} copy-done((bf16[4096,384]{1,0:T(8,128)(2,1)S(1)}, bf16[4096,384]{1,0:T(8,128)(2,1)}, u32[]{:S(2)}) %copy-start.4) | copy-done | bytes 3145752
  87.0 3.0 %back_early.1.sum_ref = f32[512,384]{1,0:T(8,128)S(1)} custom-call(s32[1]{0:T(128)} %bitcast.place_ref, bf16[4096,384]{1,0:T(8,128)(2,1)S(1)} %copy-done.4, bf16[512,2048]{1,0:T(8,128)(2,1)} %bitcast.6.own_ref.refs_2_), custom_call_target="tpu_custom_call" | custom-call | tf_op jit(solution)/shard_map/back_early/pallas_call | solution.py:99
  90.0 1.4 back_late.1
  91.5 1.4 %copy-done.10 = bf16[768,2048]{1,0:T(8,128)(2,1)S(1)} copy-done((bf16[768,2048]{1,0:T(8,128)(2,1)S(1)}, bf16[768,2048]{1,0:T(8,128)(2,1)}, u32[]{:S(2)}) %copy-start.10) | copy-done | bytes 3145752
  92.9 1.8 %parts_own.1.before_ref = bf16[512,2048]{1,0:T(8,128)(2,1)S(1)} custom-call(s32[1]{0:T(128)} %bitcast.place_ref, bf16[768,2048]{1,0:T(8,128)(2,1)S(1)} %copy-done.10, bf16[512,768]{1,0:T(8,128)(2,1)S(1)} %get-tuple-element.53.deltas_ref.refs_4_), custom_call_target="tpu_custom_call" | custom-call | tf_op jit(solution)/shard_map/parts_own/pallas_call | solution.py:99
  94.7 2.7 %parts_sum.1 = bf16[512,2176]{1,0:T(8,128)(2,1)} custom-call(s32[1]{0:T(128)} %bitcast.place_ref, bf16[768,2048]{1,0:T(8,128)(2,1)S(1)} %turn_lent.1.turned_ref, bf16[512,768]{1,0:T(8,128)(2,1)S(1)} %collective-permute-done.7.deltas_ref, bf16[512,2048]{1,0:T(8,128)(2,1)S(1)} %parts_own.1.before_ref, bf16[512,128]{1,0:T(8,128)(2,1)S(1)} %get-tuple-element.57.score_ref), custom_call_target="tpu_custom_call" | custom-call | tf_op jit(solution)/shard_map/parts_sum/pallas_call | solution.py:99
  97.5 5.4 %all-to-all-start.2 = ((bf16[64,8,2176]{2,1,0:T(8,128)(2,1)}), bf16[64,8,2176]{2,1,0:T(8,128)(2,1)S(1)}, u32[]{:S(2)}, u32[]{:S(2)}) async-start(bf16[64,8,2176]{2,1,0:T(8,128)(2,1)} %bitcast.18), calls=%async_computation.2 | async-start | bytes 4456448 | tf_op jit(solution)/shard_map/all_to_all | solution.py:358
  102.9 1.6 %copy-done.6 = bf16[512,2048]{1,0:T(8,128)(2,1)S(1)} copy-done((bf16[512,2048]{1,0:T(8,128)(2,1)S(1)}, bf16[512,2048]{1,0:T(8,128)(2,1)}, u32[]{:S(2)}) %copy-start.6) | copy-done | bytes 2097176
  104.5 8.4 %weight_grads.1 = (f32[8,128]{1,0:T(8,128)S(1)}, bf16[1,4096,384]{2,1,0:T(8,128)(2,1)}, bf16[1,4096,384]{2,1,0:T(8,128)(2,1)}, bf16[1,384,4096]{2,1,0:T(8,128)(2,1)}) custom-call(s32[1]{0:T(128)} %bitcast.place_ref, bf16[512,2048]{1,0:T(8,128)(2,1)} %bitcast.3.refs_2_.refs_0_, bf16[512,2048]{1,0:T(8,128)(2,1)} %collective-permute-done.4.refs_3_.refs_1_, ...), custom_call_target="tpu_custom_call" | custom-call | tf_op jit(solution)/shard_map/weight_grads/pallas_call | solution.py:84
  112.9 19.6 %all-to-all-done.2 = bf16[64,8,2176]{2,1,0:T(8,128)(2,1)S(1)} async-done(((bf16[64,8,2176]{2,1,0:T(8,128)(2,1)}), bf16[64,8,2176]{2,1,0:T(8,128)(2,1)S(1)}, u32[]{:S(2)}, u32[]{:S(2)}) %all-to-all-start.2) | async-done | bytes 2228256 | tf_op jit(solution)/shard_map/all_to_all | solution.py:358
  132.5 2.2 %gather_rows.1 = (bf16[16,2048]{1,0:T(8,128)(2,1)S(1)}, bf16[16,2048]{1,0:T(8,128)(2,1)S(1)}, f32[4,16]{1,0:T(4,128)S(1)}, f32[4,16]{1,0:T(4,128)S(1)}) custom-call(s32[1]{0:T(128)} %bitcast.place_ref, bf16[512,2176]{1,0:T(8,128)(2,1)S(1)} %bitcast.12, bf16[160,512]{1,0:T(8,128)(2,1)} %get-tuple-element.58.refs_1_, f32[8,128]{1,0:T(8,128)S(1)} %get-tuple-element.59.refs_2_), custom_call_target="tpu_custom_call" | custom-call | tf_op jit(solution)/shard_map/gather_rows/pallas_call | solution.py:84
  134.7 1.7 %collective-permute-start.9 = (f32[4,16]{1,0:T(4,128)S(1)}, f32[4,16]{1,0:T(4,128)S(1)}, u32[]{:S(2)}, u32[]{:S(2)}) collective-permute-start(f32[4,16]{1,0:T(4,128)S(1)} %get-tuple-element.63), channel_id=1, source_target_pairs={{0,1},{1,0},{2,3},{3,2},{4,5},{5,4},{6,7},{7,6},{8,9},{9,8},{10,11... | collective-permute-start | bytes 776 | tf_op jit(solution)/shard_map/ppermute | solution.py:355
  (48 shorter events, 5.7 us)
Async XLA Ops:
  0.6 2.9 %collective-permute-start.1 = (bf16[16,4096]{1,0:T(8,128)(2,1)}, bf16[16,4096]{1,0:T(8,128)(2,1)S(1)}, u32[]{:S(2)}, u32[]{:S(2)}) collective-permute-start(bf16[16,4096]{1,0:T(8,128)(2,1)} %refs_2_.2), channel_id=1, source_target_pairs={{0,1},{1,0},{2,3},{3,2},{4,5},{5,4},{6,7},{7,6},{8,9},{9,8},{10,11... | collective-permute-start | bytes 393224 | tf_op jit(solution)/shard_map/ppermute | solution.py:355
  2.1 1.4 collective-permute-start
  4.1 14.5 %copy-start.15 = (bf16[16,4096]{1,0:T(8,128)(2,1)S(1)}, bf16[16,4096]{1,0:T(8,128)(2,1)}, u32[]{:S(2)}) copy-start(bf16[16,4096]{1,0:T(8,128)(2,1)} %refs_4_) | copy-start | bytes 393220
  4.1 15.1 %copy-start.16 = (f32[16,4]{0,1:T(4,128)S(1)}, f32[16,4]{0,1:T(4,128)}, u32[]{:S(2)}) copy-start(f32[16,4]{0,1:T(4,128)} %param.9) | copy-start | bytes 772
  4.1 16.2 %copy-start.17 = (s32[16,4]{0,1:T(4,128)S(1)}, s32[16,4]{0,1:T(4,128)}, u32[]{:S(2)}) copy-start(s32[16,4]{0,1:T(4,128)} %param.10) | copy-start | bytes 772
  4.1 20.0 %copy-start = (bf16[1,4096,384]{2,1,0:T(8,128)(2,1)S(1)}, bf16[1,4096,384]{2,1,0:T(8,128)(2,1)}, u32[]{:S(2)}) copy-start(bf16[1,4096,384]{2,1,0:T(8,128)(2,1)} %refs_0_.5) | copy-start | bytes 9437188
  7.1 13.2 %copy-start.19 = (s32[4,16]{1,0:T(4,128)S(1)}, s32[4,16]{1,0:T(4,128)}, u32[]{:S(2)}) copy-start(s32[4,16]{1,0:T(4,128)} %copy-done.18) | copy-start | bytes 772
  7.1 39.1 %all-to-all-start = ((bf16[64,8,2048]{2,1,0:T(8,128)(2,1)}), bf16[64,8,2048]{2,1,0:T(8,128)(2,1)}, u32[]{:S(2)}, u32[]{:S(2)}) async-start(bf16[64,8,2048]{2,1,0:T(8,128)(2,1)} %bitcast.19), calls=%async_computation | async-start | bytes 4194304 | tf_op jit(solution)/shard_map/all_to_all | solution.py:358
  18.6 1.7 %collective-permute-start.3 = (bf16[16,4096]{1,0:T(8,128)(2,1)S(1)}, bf16[16,4096]{1,0:T(8,128)(2,1)S(1)}, u32[]{:S(2)}, u32[]{:S(2)}) collective-permute-start(bf16[16,4096]{1,0:T(8,128)(2,1)S(1)} %copy-done.15), channel_id=1, source_target_pairs={{0,1},{1,0},{2,3},{3,2},{4,5},{5,4},{6,7},{7,6},{8,9},{9,8},{10,11... | collective-permute-start | bytes 393224 | tf_op jit(solution)/shard_map/ppermute | solution.py:355
  19.2 1.2 collective-permute-start.2
  24.1 1.9 %copy-start.1 = (bf16[1,4096,384]{2,1,0:T(8,128)(2,1)S(1)}, bf16[1,4096,384]{2,1,0:T(8,128)(2,1)}, u32[]{:S(2)}) copy-start(bf16[1,4096,384]{2,1,0:T(8,128)(2,1)} %refs_1_.5) | copy-start | bytes 9437188
  26.0 2.8 %copy-start.11 = (bf16[1,384,4096]{2,1,0:T(8,128)(2,1)S(1)}, bf16[1,384,4096]{2,1,0:T(8,128)(2,1)}, u32[]{:S(2)}) copy-start(bf16[1,384,4096]{2,1,0:T(8,128)(2,1)} %refs_2_.3) | copy-start | bytes 9437188
  26.6 1.7 %copy-start.12 = (bf16[2048,768]{1,0:T(8,128)(2,1)}, bf16[2048,768]{1,0:T(8,128)(2,1)S(1)}, u32[]{:S(2)}) copy-start(bf16[2048,768]{1,0:T(8,128)(2,1)S(1)} %lend.1) | copy-start | bytes 9437188
  31.6 1.7 %copy-start.3 = (bf16[4096,384]{1,0:T(8,128)(2,1)}, bf16[4096,384]{1,0:T(8,128)(2,1)S(1)}, u32[]{:S(2)}) copy-start(bf16[4096,384]{1,0:T(8,128)(2,1)S(1)} %get-tuple-element.47.back_ref) | copy-start | bytes 9437188
  33.2 1.7 %copy-start.9 = (bf16[768,2048]{1,0:T(8,128)(2,1)}, bf16[768,2048]{1,0:T(8,128)(2,1)S(1)}, u32[]{:S(2)}) copy-start(bf16[768,2048]{1,0:T(8,128)(2,1)S(1)} %get-tuple-element.54.turned_ref) | copy-start | bytes 9437188
  46.2 21.4 %collective-permute-start.5 = (bf16[2048,768]{1,0:T(8,128)(2,1)}, bf16[2048,768]{1,0:T(8,128)(2,1)}, u32[]{:S(2)}, u32[]{:S(2)}) collective-permute-start(bf16[2048,768]{1,0:T(8,128)(2,1)} %copy-done.12), channel_id=1, source_target_pairs={{0,1},{1,0},{2,3},{3,2},{4,5},{5,4},{6,7},{7,6},{8,9},{9,8},{10,11... | collective-permute-start | bytes 9437192 | tf_op jit(solution)/shard_map/ppermute | solution.py:355
  49.0 8.6 %collective-permute-start.4 = (bf16[512,2048]{1,0:T(8,128)(2,1)}, bf16[512,2048]{1,0:T(8,128)(2,1)}, u32[]{:S(2)}, u32[]{:S(2)}) collective-permute-start(bf16[512,2048]{1,0:T(8,128)(2,1)} %bitcast.3.refs_2_.refs_0_), channel_id=1, source_target_pairs={{0,1},{1,0},{2,3},{3,2},{4,5},{5,4},{6,7},{7,6},{8,9},{9,8},{10,11... | collective-permute-start | bytes 6291464 | tf_op jit(solution)/shard_map/ppermute | solution.py:355
  49.0 33.0 %all-to-all-start.1 = ((bf16[64,8,2048]{2,1,0:T(8,128)(2,1)}), bf16[64,8,2048]{2,1,0:T(8,128)(2,1)}, u32[]{:S(2)}, u32[]{:S(2)}) async-start(bf16[64,8,2048]{2,1,0:T(8,128)(2,1)} %bitcast.20), calls=%async_computation.1 | async-start | bytes 4194304 | tf_op jit(solution)/shard_map/all_to_all | solution.py:358
  57.7 1.9 %copy-start.2 = (bf16[1,4096,384]{2,1,0:T(8,128)(2,1)S(1)}, bf16[1,4096,384]{2,1,0:T(8,128)(2,1)}, u32[]{:S(2)}) copy-start(bf16[1,4096,384]{2,1,0:T(8,128)(2,1)} %refs_1_.5) | copy-start | bytes 9437188
  66.4 1.2 copy-start.13
  82.1 7.9 %collective-permute-start.6 = (bf16[512,2048]{1,0:T(8,128)(2,1)}, bf16[512,2048]{1,0:T(8,128)(2,1)S(1)}, u32[]{:S(2)}, u32[]{:S(2)}) collective-permute-start(bf16[512,2048]{1,0:T(8,128)(2,1)} %bitcast.6.own_ref.refs_2_), channel_id=1, source_target_pairs={{0,1},{1,0},{2,3},{3,2},{4,5},{5,4},{6,7},{7,6},{8,9},{9,8},{10,11... | collective-permute-start | bytes 6291464 | tf_op jit(solution)/shard_map/ppermute | solution.py:355
  85.1 1.9 %copy-start.4 = (bf16[4096,384]{1,0:T(8,128)(2,1)S(1)}, bf16[4096,384]{1,0:T(8,128)(2,1)}, u32[]{:S(2)}) copy-start(bf16[4096,384]{1,0:T(8,128)(2,1)} %copy-done.3) | copy-start | bytes 9437188
  87.0 3.0 %copy-start.14 = (f32[512,768]{1,0:T(8,128)S(1)}, f32[512,768]{1,0:T(8,128)}, u32[]{:S(2)}) copy-start(f32[512,768]{1,0:T(8,128)} %copy-done.13) | copy-start | bytes 4718596
  89.9 2.9 %copy-start.10 = (bf16[768,2048]{1,0:T(8,128)(2,1)S(1)}, bf16[768,2048]{1,0:T(8,128)(2,1)}, u32[]{:S(2)}) copy-start(bf16[768,2048]{1,0:T(8,128)(2,1)} %copy-done.9) | copy-start | bytes 9437188
  90.0 1.4 %copy-start.5 = (bf16[512,2048]{1,0:T(8,128)(2,1)}, bf16[512,2048]{1,0:T(8,128)(2,1)S(1)}, u32[]{:S(2)}) copy-start(bf16[512,2048]{1,0:T(8,128)(2,1)S(1)} %collective-permute-done.6.other_ref.refs_3_) | copy-start | bytes 6291460
  91.4 6.1 %copy-start.7 = (bf16[512,768]{1,0:T(8,128)(2,1)}, bf16[512,768]{1,0:T(8,128)(2,1)S(1)}, u32[]{:S(2)}) copy-start(bf16[512,768]{1,0:T(8,128)(2,1)S(1)} %get-tuple-element.53.deltas_ref.refs_4_) | copy-start | bytes 2359300
  91.4 3.3 %collective-permute-start.7 = (bf16[512,768]{1,0:T(8,128)(2,1)S(1)}, bf16[512,768]{1,0:T(8,128)(2,1)S(1)}, u32[]{:S(2)}, u32[]{:S(2)}) collective-permute-start(bf16[512,768]{1,0:T(8,128)(2,1)S(1)} %get-tuple-element.53.deltas_ref.refs_4_), channel_id=1, source_target_pairs={{0,1},{1,0},{2,3},{3,2},{4,5},{5,4},{6,7},{7,6},{8,9},{9,8},{10,11... | collective-permute-start | bytes 2359304 | tf_op jit(solution)/shard_map/ppermute | solution.py:355
  97.4 5.5 %copy-start.8 = (bf16[512,768]{1,0:T(8,128)(2,1)S(1)}, bf16[512,768]{1,0:T(8,128)(2,1)}, u32[]{:S(2)}) copy-start(bf16[512,768]{1,0:T(8,128)(2,1)} %copy-done.7) | copy-start | bytes 2359300
  97.5 35.0 %all-to-all-start.2 = ((bf16[64,8,2176]{2,1,0:T(8,128)(2,1)}), bf16[64,8,2176]{2,1,0:T(8,128)(2,1)S(1)}, u32[]{:S(2)}, u32[]{:S(2)}) async-start(bf16[64,8,2176]{2,1,0:T(8,128)(2,1)} %bitcast.18), calls=%async_computation.2 | async-start | bytes 4456448 | tf_op jit(solution)/shard_map/all_to_all | solution.py:358
  102.9 1.6 %copy-start.6 = (bf16[512,2048]{1,0:T(8,128)(2,1)S(1)}, bf16[512,2048]{1,0:T(8,128)(2,1)}, u32[]{:S(2)}) copy-start(bf16[512,2048]{1,0:T(8,128)(2,1)} %copy-done.5) | copy-start | bytes 6291460
  134.7 2.5 %collective-permute-start.9 = (f32[4,16]{1,0:T(4,128)S(1)}, f32[4,16]{1,0:T(4,128)S(1)}, u32[]{:S(2)}, u32[]{:S(2)}) collective-permute-start(f32[4,16]{1,0:T(4,128)S(1)} %get-tuple-element.63), channel_id=1, source_target_pairs={{0,1},{1,0},{2,3},{3,2},{4,5},{5,4},{6,7},{7,6},{8,9},{9,8},{10,11... | collective-permute-start | bytes 776 | tf_op jit(solution)/shard_map/ppermute | solution.py:355
  136.4 1.4 %collective-permute-start.8 = (bf16[16,2048]{1,0:T(8,128)(2,1)S(1)}, bf16[16,2048]{1,0:T(8,128)(2,1)S(1)}, u32[]{:S(2)}, u32[]{:S(2)}) collective-permute-start(bf16[16,2048]{1,0:T(8,128)(2,1)S(1)} %get-tuple-element.61), channel_id=1, source_target_pairs={{0,1},{1,0},{2,3},{3,2},{4,5},{5,4},{6,7},{7,6},{8,9},{9,8},{10,11... | collective-permute-start | bytes 196616 | tf_op jit(solution)/shard_map/ppermute | solution.py:355
  (1 other events, 0.6 us)

commit v3 on v2

--- a/solution.py
+++ b/solution.py
@@ -63,16 +63,17 @@
             copy.start()
 
 
-def call(kernel, name, outs, place, *args, raw=0, direct=0, scratch=(), limit=28 << 20, far=False):
-    count, given = len(outs) - direct, len(args) - raw
+def call(kernel, name, outs, place, *args, raw=0, direct=0, near=0, scratch=(), limit=28 << 20, far=False):
+    count, given = len(outs) - direct, len(args) - raw - near
 
     def body(place_ref, *refs):
         raw_refs, ins, refs = refs[:raw], refs[raw : raw + given], refs[raw + given :]
+        near_refs, refs = refs[:near], refs[near:]
         out_refs, direct_refs, refs = refs[:count], refs[count : count + direct], refs[count + direct :]
         held, made, refs = refs[:given], refs[given : given + count], refs[given + count :]
         in_sems, out_sems, own = refs[0], refs[1], refs[2:]
         loaded = [Loaded(ins[n], held[n], in_sems.at[n]) for n in range(given)]
-        kernel(place_ref, *raw_refs, *loaded, *made, *direct_refs, *own)
+        kernel(place_ref, *raw_refs, *loaded, *near_refs, *made, *direct_refs, *own)
         for held_ref in loaded:
             held_ref.wait()
         copies = [pltpu.make_async_copy(made[n], out_refs[n], out_sems.at[n]) for n in range(count)]
@@ -83,10 +84,10 @@
 
     return pl.pallas_call(
         body,
-        in_specs=[SMEM] + [HBM] * len(args),
+        in_specs=[SMEM] + [HBM] * (raw + given) + [VMEM] * near,
         out_specs=[HBM] * len(outs),
         out_shape=[pltpu.HBM(*out) if far else jax.ShapeDtypeStruct(*out) for out in outs],
-        scratch_shapes=[pltpu.VMEM(x.shape, x.dtype) for x in args[raw:]]
+        scratch_shapes=[pltpu.VMEM(x.shape, x.dtype) for x in args[raw : raw + given]]
         + [pltpu.VMEM(shape, kind) for shape, kind in outs[:count]]
         + [pltpu.SemaphoreType.DMA((max(given, 1),)), pltpu.SemaphoreType.DMA((max(count, 1),)), *scratch],
         compiler_params=pltpu.CompilerParams(vmem_limit_bytes=limit),
@@ -177,6 +178,10 @@
         copy.wait()
 
 
+def build_rows_kernel(place_ref, ids_ref, rows_ref, other_ids_ref, other_rows_ref, *refs):
+    build_kernel(place_ref, ids_ref, other_ids_ref, rows_ref, other_rows_ref, *refs)
+
+
 def lend_kernel(place_ref, gate_hbm, up_hbm, order_hbm, first_ref, sems):
     half, both = first_ref.shape
     ff = both // 2
@@ -191,30 +196,17 @@
         copy.wait()
 
 
-def turn_kernel(place_ref, gate_hbm, up_hbm, down_hbm, order_hbm, back_ref, parts_ref, first_ref, down_ref, sems):
-    half, both = first_ref.shape
-    ff = both // 2
-    at = columns(place_ref[0] * half, half)
-    copies = [
-        pltpu.make_async_copy(down_hbm.at[0], down_ref, sems.at[0]),
-        pltpu.make_async_copy(gate_hbm.at[0, at, :], first_ref.at[:, pl.ds(0, ff)], sems.at[1]),
-        pltpu.make_async_copy(up_hbm.at[0, at, :], first_ref.at[:, pl.ds(ff, ff)], sems.at[2]),
-    ]
-    for copy in copies:
-        copy.start()
-    for copy in copies:
-        copy.wait()
+def turn_kernel(place_ref, gate_ref, up_ref, down_ref, lent_ref, back_ref, own_ref, other_ref):
+    half = lent_ref.shape[0]
+    ff, width = down_ref.shape[1:]
     step = 256
-    for n in range(0, CORES * half, step):
-        back_ref[n : n + step, :] = down_ref[:, n : n + step].T
+    for n in range(0, width, step):
+        back_ref[n : n + step, :] = down_ref[0, :, n : n + step].T
     for n in range(0, half, step):
-        parts_ref[:, n : n + step] = first_ref[n : n + step, :].T
-
-
-def turn_lent_kernel(place_ref, lent_ref, parts_ref):
-    step = 256
-    for n in range(0, lent_ref.shape[0], step):
-        parts_ref[:, n : n + step] = lent_ref[n : n + step, :].T
+        at = columns(place_ref[0] * half + n, step)
+        own_ref[:ff, n : n + step] = gate_ref[0, at, :].T
+        own_ref[ff:, n : n + step] = up_ref[0, at, :].T
+        other_ref[:, n : n + step] = lent_ref[n : n + step, :].T
 
 
 def gate_up_kernel(place_ref, gate_hbm, up_hbm, own_hbm, other_hbm, factors_ref, hidden_ref, rows_ref, first_ref, sems):
@@ -286,32 +278,25 @@
         copy.wait()
 
 
-def gather_kernel(place_ref, back_hbm, picks_ref, mark_ref, mine_ref, send_ref, mine_score_ref, send_score_ref, back_ref, sems):
+def gather_kernel(place_ref, back_ref, picks_ref, mine_ref, send_ref, mine_score_ref, send_score_ref):
     tok, width = mine_ref.shape
     tokens = CORES * tok
-    steps, _, step = back_ref.shape
-    copies = [pltpu.make_async_copy(back_hbm.at[:, pl.ds(width, META)], back_ref.at[steps - 1, :, pl.ds(0, META)], sems.at[0])]
-    for n in range(steps - 1):
-        copies.append(pltpu.make_async_copy(back_hbm.at[:, pl.ds(n * step, step)], back_ref.at[n], sems.at[n + 1]))
-    for copy in copies:
-        copy.start()
+    step = 512
     pick = picks_ref[:tokens, :]
-    copies[0].wait()
-    scores = dot(picks_ref[tokens:, :], back_ref[steps - 1, :, :META])
+    for at in range(0, width, step):
+        part = dot(pick, back_ref[:, at : at + step]).astype(BF16)
+        mine_ref[:, at : at + step] = part[:tok]
+        send_ref[:, at : at + step] = part[tok:]
+    scores = dot(picks_ref[tokens:, :], back_ref[:, width:])
     for k in range(TOPK):
         mine_score_ref[k : k + 1, :] = row(scores[k * tokens : k * tokens + tok, :1])
         send_score_ref[k : k + 1, :] = row(scores[k * tokens + tok : (k + 1) * tokens, :1])
-    for n in range(steps - 1):
-        copies[n + 1].wait()
-        part = dot(pick, back_ref[n]).astype(BF16)
-        mine_ref[:, n * step : (n + 1) * step] = part[:tok]
-        send_ref[:, n * step : (n + 1) * step] = part[tok:]
 
 
 def weights_kernel(place_ref, *refs):
     rows_refs, grads_refs = refs[0:2], refs[2:4]
-    deltas_ref, hidden_ref, mark_ref, gate_hbm, up_hbm, down_hbm, gate_ref, up_ref, down_ref, sems = refs[4:]
-    mark_ref[...] = jnp.zeros_like(mark_ref)
+    deltas_ref, hidden_ref, given_ref, picks_ref, gate_hbm, up_hbm, down_hbm, gate_ref, up_ref, down_ref, sems = refs[4:]
+    picks_ref[...] = given_ref[...]
     core = place_ref[0]
     half, step = rows_refs[0].shape[1], gate_ref.shape[1]
     ff = hidden_ref.shape[1]
@@ -364,8 +349,9 @@
     scratch = [pltpu.VMEM((half // step, lines, step), BF16), pltpu.SemaphoreType.DMA((half // step,))]
     out = ((lines, half), BF16)
     rows_out = call(
-        build_kernel, "build_rows", [out], place, *[pltpu.with_memory_space_constraint(x, pltpu.HBM) for x in ids_pair],
-        pltpu.with_memory_space_constraint(tokens, pltpu.HBM), tokens_pair[1], direct=1, scratch=scratch, far=True,
+        build_rows_kernel, "build_rows", [out],
+        place, *[pltpu.with_memory_space_constraint(x, pltpu.HBM) for x in (ids, tokens)], ids_pair[1], tokens_pair[1],
+        direct=1, near=2, scratch=scratch, far=True,
     )[0]
     later = after(comb, out_grad, rows_out)[:2]
     comb_pair, out_grad_pair = [(x, swap(x)) for x in later]
@@ -377,16 +363,13 @@
         lend_kernel, "lend", [((half, 2 * ff), BF16)], place, gate_weight, up_weight, out_grad_pair[1],
         raw=3, scratch=[pltpu.SemaphoreType.DMA((2,))],
     )[0]
-    back, parts_own = call(
+    rows, grads_out, lend = after(deliver(rows_out), grads_out, lend)
+    back, parts_own, parts_other = call_near(
         turn_kernel,
         "turn",
-        [((width, ff), BF16), ((2 * ff, half), BF16)],
-        place, gate_weight, up_weight, down_weight, out_grad_pair[1],
-        raw=4,
-        scratch=[pltpu.VMEM((half, 2 * ff), BF16), pltpu.VMEM((ff, width), BF16), pltpu.SemaphoreType.DMA((3,))],
-    )
-    rows, grads_out, back, parts_own, lend = after(deliver(rows_out), grads_out, back, parts_own, lend)
-    parts_other = call(turn_lent_kernel, "turn_lent", [((2 * ff, half), BF16)], place, swap(lend))[0]
+        [((width, ff), BF16)] + [((2 * ff, half), BF16)] * CORES,
+        place, gate_weight, up_weight, down_weight, swap(lend),
+    )
     rows_pair = (rows, swap(rows))
     factors, hidden = call(
         gate_up_kernel,
@@ -400,7 +383,9 @@
             pltpu.SemaphoreType.DMA((12,)),
         ],
     )
-    grads, factors, hidden, parts_other = after(deliver(grads_out), factors, hidden, parts_other)
+    grads, factors, hidden, back, parts_own, parts_other = after(
+        deliver(grads_out), factors, hidden, back, parts_own, parts_other
+    )
     grads_pair = (grads, swap(grads))
     scaled = call_near(back_early_kernel, "back_early", [((lines, ff), F32)], place, back, grads)[0]
     other, scaled = after(grads_pair[1], scaled)
@@ -420,11 +405,11 @@
         direct=1,
         scratch=[pltpu.VMEM((half // step, lines, step), BF16), pltpu.SemaphoreType.DMA((half // step + 1,))],
     )[0]
-    mark, gate_grad, up_grad, down_grad = call(
+    picks, gate_grad, up_grad, down_grad = call(
         weights_kernel,
         "weight_grads",
-        [((8, META), F32), (gate_weight.shape, BF16), (up_weight.shape, BF16), (down_weight.shape, BF16)],
-        place, *rows_pair, *grads_pair, deltas, hidden,
+        [(picks.shape, BF16), (gate_weight.shape, BF16), (up_weight.shape, BF16), (down_weight.shape, BF16)],
+        place, *rows_pair, *grads_pair, deltas, hidden, picks,
         direct=3,
         scratch=[
             pltpu.VMEM((width // step, step, ff), BF16),
@@ -433,13 +418,11 @@
             pltpu.SemaphoreType.DMA((3 * width // step,)),
         ],
     )
-    mine, send, mine_score, send_score = call(
+    mine, send, mine_score, send_score = call_near(
         gather_kernel,
         "gather_rows",
         [((tok, half), BF16)] * CORES + [((TOPK, tok), F32)] * CORES,
-        place, deliver(parts_sum), pltpu.with_memory_space_constraint(picks, pltpu.HBM), mark,
-        raw=1,
-        scratch=[pltpu.VMEM((half // step + 1, lines, step), BF16), pltpu.SemaphoreType.DMA((half // step + 1,))],
+        place, deliver(parts_sum), picks,
     )
     combine_grad = ((mine_score + swap(send_score)) / comb).T
     other = swap(send)

time: 139 us -> 137 us (0.986)
  Pallas kernels: 39.5 us -> 36.6 us
  local copies, waits for them, and re-layouts: 16 us -> 18.8 us
  waiting for transfers between devices: 48.2 us -> 46.6 us
    pallas_call x8 -> x5, Pallas kernels: 30.6 us -> 22.7 us  [call(): pl.pallas_call(body, in_specs=[SMEM] + [HBM] * (raw + given) + [VMEM] * n...]
    pallas_call x4 -> x6, Pallas kernels: 8.86 us -> 13.9 us  [call_near(): pl.pallas_call(kernel, in_specs=[SMEM] + [VMEM] * len(args), out_specs=[V...]
    unnamed x40 -> x42, local copies, waits for them, and re-layouts: 16 us -> 18.8 us
    all_to_all x3, waiting for transfers between devices: 42.2 us -> 40.7 us  [deliver(): lax.all_to_all(x.reshape(chips, SLOTS, x.shape[1]), CHIPS, split_axis=0,...]
  transfers between devices with their start and end apart: 13 -> 13, of which waited for: 7 -> 7; matrix products, arithmetic and copies ran while one was open for 0% -> 0% of each run, Pallas kernels for 22% -> 21%
where the time goes in v3:
time: 137 us
  waiting for transfers between devices  46.6 us (34%)
  Pallas kernels  36.6 us (27%)
  starting transfers between devices  32.5 us (24%)
  local copies, waits for them, and re-layouts  18.8 us (14%)
    all_to_all x3, waiting for transfers between devices, deliver(): lax.all_to_all(x.reshape(chips, SLOTS, x.shape[1]), CHIPS, split_axis=0,...  40.7 us
    pallas_call x5, Pallas kernels, call(): pl.pallas_call(body, in_specs=[SMEM] + [HBM] * (raw + given) + [VMEM] * n...  22.7 us
    all_to_all x3, starting transfers between devices, deliver(): lax.all_to_all(x.reshape(chips, SLOTS, x.shape[1]), CHIPS, split_axis=0,...  22.5 us
    unnamed x42, local copies, waits for them, and re-layouts  18.8 us
    pallas_call x6, Pallas kernels, call_near(): pl.pallas_call(kernel, in_specs=[SMEM] + [VMEM] * len(args), out_specs=[V...  13.9 us
    ppermute x10, starting transfers between devices, swap(): return lax.ppermute(x, 'core', [(0, 1), (1, 0)])  9.98 us
    ppermute x10, waiting for transfers between devices, swap(): return lax.ppermute(x, 'core', [(0, 1), (1, 0)])  5.94 us
  transfers between devices with their start and end apart: 13, of which 7 were waited for; matrix products, arithmetic and copies ran while one was open for 0% of the time, Pallas kernels for 21%

profile of v3, /device:TPU:1, one launch (start us, length us, event | category | flops | bytes accessed | tf_op | source)
XLA Modules:
  0.0 136.6 jit_solution(15756702449727373033)
XLA Ops:
  0.6 1.5 %collective-permute-start.1 = (bf16[16,4096]{1,0:T(8,128)(2,1)}, bf16[16,4096]{1,0:T(8,128)(2,1)S(1)}, u32[]{:S(2)}, u32[]{:S(2)}) collective-permute-start(bf16[16,4096]{1,0:T(8,128)(2,1)} %refs_1_.3), channel_id=1, source_target_pairs={{0,1},{1,0},{2,3},{3,2},{4,5},{5,4},{6,7},{7,6},{8,9},{9,8},{10,11... | collective-permute-start | bytes 393224 | tf_op jit(solution)/shard_map/ppermute | solution.py:340
  2.2 1.3 collective-permute-done.refs_2_.refs_1_
  3.5 2.8 %build_rows.1 = bf16[512,2048]{1,0:T(8,128)(2,1)} custom-call(s32[1]{0:T(128)} %bitcast.place_ref, s32[4,16]{1,0:T(4,128)} %bitcast.16, bf16[16,4096]{1,0:T(8,128)(2,1)} %refs_1_.3, s32[4,16]{1,0:T(4,128)S(1)} %collective-permute-done.refs_2_.refs_1_, bf16[16,4096]{1,0:T(8,128)(2,1)S(1)} %collective-permute-done.1.refs_3_), custom_call_target="tpu_custom_call" | custom-call | tf_op jit(solution)/shard_map/build_rows/pallas_call | solution.py:85
  6.4 11.5 %all-to-all-start = ((bf16[64,8,2048]{2,1,0:T(8,128)(2,1)}), bf16[64,8,2048]{2,1,0:T(8,128)(2,1)}, u32[]{:S(2)}, u32[]{:S(2)}) async-start(bf16[64,8,2048]{2,1,0:T(8,128)(2,1)} %bitcast.19), calls=%async_computation | async-start | bytes 4194304 | tf_op jit(solution)/shard_map/all_to_all | solution.py:343
  18.5 1.1 collective-permute-done.2.refs_3_
  19.6 3.7 %build_grads.1 = (bf16[160,512]{1,0:T(8,128)(2,1)}, bf16[512,2048]{1,0:T(8,128)(2,1)}) custom-call(s32[1]{0:T(128)} %bitcast.place_ref, s32[4,16]{1,0:T(4,128)S(1)} %bitcast.17, s32[4,16]{1,0:T(4,128)S(1)} %collective-permute-done.refs_2_.refs_1_, f32[4,16]{1,0:T(4,128)S(1)} %bitcast.14, f32[4,16]{1,0:T(4,128)S(1)} %collective-permute-done.2.refs_3_, ...), custom_call_target="tpu_custom_call" | custom-call | tf_op jit(solution)/shard_map/build_grads/pallas_call | solution.py:85
  23.3 1.9 %copy-done.1 = bf16[1,4096,384]{2,1,0:T(8,128)(2,1)S(1)} copy-done((bf16[1,4096,384]{2,1,0:T(8,128)(2,1)S(1)}, bf16[1,4096,384]{2,1,0:T(8,128)(2,1)}, u32[]{:S(2)}) %copy-start.1) | copy-done | bytes 3145752
  25.8 1.7 %copy-done.12 = bf16[2048,768]{1,0:T(8,128)(2,1)} copy-done((bf16[2048,768]{1,0:T(8,128)(2,1)}, bf16[2048,768]{1,0:T(8,128)(2,1)S(1)}, u32[]{:S(2)}) %copy-start.12) | copy-done | bytes 3145752
  27.5 18.1 %all-to-all-done = bf16[64,8,2048]{2,1,0:T(8,128)(2,1)} async-done(((bf16[64,8,2048]{2,1,0:T(8,128)(2,1)}), bf16[64,8,2048]{2,1,0:T(8,128)(2,1)}, u32[]{:S(2)}, u32[]{:S(2)}) %all-to-all-start) | async-done | bytes 2097184 | tf_op jit(solution)/shard_map/all_to_all | solution.py:343
  45.5 2.8 %collective-permute-start.5 = (bf16[2048,768]{1,0:T(8,128)(2,1)}, bf16[2048,768]{1,0:T(8,128)(2,1)}, u32[]{:S(2)}, u32[]{:S(2)}) collective-permute-start(bf16[2048,768]{1,0:T(8,128)(2,1)} %copy-done.12), channel_id=1, source_target_pairs={{0,1},{1,0},{2,3},{3,2},{4,5},{5,4},{6,7},{7,6},{8,9},{9,8},{10,11... | collective-permute-start | bytes 9437192 | tf_op jit(solution)/shard_map/ppermute | solution.py:340
  48.3 5.7 %all-to-all-start.1 = ((bf16[64,8,2048]{2,1,0:T(8,128)(2,1)}), bf16[64,8,2048]{2,1,0:T(8,128)(2,1)}, u32[]{:S(2)}, u32[]{:S(2)}) async-start(bf16[64,8,2048]{2,1,0:T(8,128)(2,1)} %bitcast.20), calls=%async_computation.1 | async-start | bytes 4194304 | tf_op jit(solution)/shard_map/all_to_all | solution.py:343
  54.1 2.9 %collective-permute-done.4.refs_3_.refs_1_ = bf16[512,2048]{1,0:T(8,128)(2,1)} collective-permute-done((bf16[512,2048]{1,0:T(8,128)(2,1)}, bf16[512,2048]{1,0:T(8,128)(2,1)}, u32[]{:S(2)}, u32[]{:S(2)}) %collective-permute-start.4) | collective-permute-done | bytes 2097184 | tf_op jit(solution)/shard_map/ppermute | solution.py:340
  57.0 1.9 %copy-done.2 = bf16[1,4096,384]{2,1,0:T(8,128)(2,1)S(1)} copy-done((bf16[1,4096,384]{2,1,0:T(8,128)(2,1)S(1)}, bf16[1,4096,384]{2,1,0:T(8,128)(2,1)}, u32[]{:S(2)}) %copy-start.2) | copy-done | bytes 3145752
  58.8 6.9 %gate_up.1 = (f32[512,768]{1,0:T(8,128)S(1)}, bf16[512,384]{1,0:T(8,128)(2,1)S(1)}) custom-call(s32[1]{0:T(128)} %bitcast.place_ref, bf16[1,4096,384]{2,1,0:T(8,128)(2,1)S(1)} %copy-done, bf16[1,4096,384]{2,1,0:T(8,128)(2,1)S(1)} %copy-done.2, bf16[512,2048]{1,0:T(8,128)(2,1)} %bitcast.3.refs_2_.refs_0_, bf16[512,2048]{1,0:T(8,128)(2,1)} %collective-permute-done.4.refs_3_.refs_1_), custom_call_target="tpu_custom_call" | custom-call | tf_op jit(solution)/shard_map/gate_up/pallas_call | solution.py:85
  65.8 1.2 copy-done.13
  67.0 4.5 %turn.1 = (bf16[4096,384]{1,0:T(8,128)(2,1)S(1)}, bf16[768,2048]{1,0:T(8,128)(2,1)S(1)}, bf16[768,2048]{1,0:T(8,128)(2,1)S(1)}) custom-call(s32[1]{0:T(128)} %bitcast.place_ref, bf16[1,4096,384]{2,1,0:T(8,128)(2,1)S(1)} %copy-done, bf16[1,4096,384]{2,1,0:T(8,128)(2,1)S(1)} %copy-done.2, bf16[1,384,4096]{2,1,0:T(8,128)(2,1)S(1)} %copy-done.11, ...), custom_call_target="tpu_custom_call" | custom-call | tf_op jit(solution)/shard_map/turn/pallas_call | solution.py:100
  71.5 1.7 %copy-done.3 = bf16[4096,384]{1,0:T(8,128)(2,1)} copy-done((bf16[4096,384]{1,0:T(8,128)(2,1)}, bf16[4096,384]{1,0:T(8,128)(2,1)S(1)}, u32[]{:S(2)}) %copy-start.3) | copy-done | bytes 3145752
  73.2 1.7 %copy-done.7 = bf16[768,2048]{1,0:T(8,128)(2,1)} copy-done((bf16[768,2048]{1,0:T(8,128)(2,1)}, bf16[768,2048]{1,0:T(8,128)(2,1)S(1)}, u32[]{:S(2)}) %copy-start.7) | copy-done | bytes 3145752
  74.8 1.7 %copy-done.9 = bf16[768,2048]{1,0:T(8,128)(2,1)} copy-done((bf16[768,2048]{1,0:T(8,128)(2,1)}, bf16[768,2048]{1,0:T(8,128)(2,1)S(1)}, u32[]{:S(2)}) %copy-start.9) | copy-done | bytes 3145752
  76.5 4.8 %all-to-all-done.1 = bf16[64,8,2048]{2,1,0:T(8,128)(2,1)} async-done(((bf16[64,8,2048]{2,1,0:T(8,128)(2,1)}), bf16[64,8,2048]{2,1,0:T(8,128)(2,1)}, u32[]{:S(2)}, u32[]{:S(2)}) %all-to-all-start.1) | async-done | bytes 2097184 | tf_op jit(solution)/shard_map/all_to_all | solution.py:343
  81.3 3.0 %collective-permute-start.6 = (bf16[512,2048]{1,0:T(8,128)(2,1)}, bf16[512,2048]{1,0:T(8,128)(2,1)S(1)}, u32[]{:S(2)}, u32[]{:S(2)}) collective-permute-start(bf16[512,2048]{1,0:T(8,128)(2,1)} %bitcast.6.own_ref.refs_2_), channel_id=1, source_target_pairs={{0,1},{1,0},{2,3},{3,2},{4,5},{5,4},{6,7},{7,6},{8,9},{9,8},{10,11... | collective-permute-start | bytes 6291464 | tf_op jit(solution)/shard_map/ppermute | solution.py:340
  84.4 1.9 %copy-done.4 = bf16[4096,384]{1,0:T(8,128)(2,1)S(1)} copy-done((bf16[4096,384]{1,0:T(8,128)(2,1)S(1)}, bf16[4096,384]{1,0:T(8,128)(2,1)}, u32[]{:S(2)}) %copy-start.4) | copy-done | bytes 3145752
  86.3 3.0 %back_early.1.sum_ref = f32[512,384]{1,0:T(8,128)S(1)} custom-call(s32[1]{0:T(128)} %bitcast.place_ref, bf16[4096,384]{1,0:T(8,128)(2,1)S(1)} %copy-done.4, bf16[512,2048]{1,0:T(8,128)(2,1)} %bitcast.6.own_ref.refs_2_), custom_call_target="tpu_custom_call" | custom-call | tf_op jit(solution)/shard_map/back_early/pallas_call | solution.py:100
  89.3 1.4 %back_late.1 = (bf16[512,768]{1,0:T(8,128)(2,1)S(1)}, bf16[512,128]{1,0:T(8,128)(2,1)S(1)}) custom-call(s32[1]{0:T(128)} %bitcast.place_ref, bf16[4096,384]{1,0:T(8,128)(2,1)S(1)} %copy-done.4, bf16[512,2048]{1,0:T(8,128)(2,1)S(1)} %collective-permute-done.6.other_ref.refs_3_, f32[512,384]{1,0:T(8,128)S(1)} %back_early.1.sum_ref, f32[512,768]{1,0:T(8,128)S(1)} %copy-done.14, ...), custom_call_target="tpu_custom_call" | custom-call | tf_op jit(solution)/shard_map/back_late/pallas_call | solution.py:100
  90.8 1.1 copy-done.10
  91.9 1.8 %parts_own.1.before_ref = bf16[512,2048]{1,0:T(8,128)(2,1)S(1)} custom-call(s32[1]{0:T(128)} %bitcast.place_ref, bf16[768,2048]{1,0:T(8,128)(2,1)S(1)} %copy-done.10, bf16[512,768]{1,0:T(8,128)(2,1)S(1)} %get-tuple-element.55.deltas_ref.refs_4_), custom_call_target="tpu_custom_call" | custom-call | tf_op jit(solution)/shard_map/parts_own/pallas_call | solution.py:100
  93.7 2.7 %parts_sum.1 = bf16[512,2176]{1,0:T(8,128)(2,1)} custom-call(s32[1]{0:T(128)} %bitcast.place_ref, bf16[768,2048]{1,0:T(8,128)(2,1)S(1)} %copy-done.8, bf16[512,768]{1,0:T(8,128)(2,1)S(1)} %collective-permute-done.7.deltas_ref, bf16[512,2048]{1,0:T(8,128)(2,1)S(1)} %parts_own.1.before_ref, bf16[512,128]{1,0:T(8,128)(2,1)S(1)} %get-tuple-element.59.score_ref), custom_call_target="tpu_custom_call" | custom-call | tf_op jit(solution)/shard_map/parts_sum/pallas_call | solution.py:100
  96.4 5.3 %all-to-all-start.2 = ((bf16[64,8,2176]{2,1,0:T(8,128)(2,1)}), bf16[64,8,2176]{2,1,0:T(8,128)(2,1)S(1)}, u32[]{:S(2)}, u32[]{:S(2)}) async-start(bf16[64,8,2176]{2,1,0:T(8,128)(2,1)} %bitcast.18), calls=%async_computation.2 | async-start | bytes 4456448 | tf_op jit(solution)/shard_map/all_to_all | solution.py:343
  101.7 1.6 %copy-done.6 = bf16[512,2048]{1,0:T(8,128)(2,1)S(1)} copy-done((bf16[512,2048]{1,0:T(8,128)(2,1)S(1)}, bf16[512,2048]{1,0:T(8,128)(2,1)}, u32[]{:S(2)}) %copy-start.6) | copy-done | bytes 2097176
  104.2 8.6 %weight_grads.1 = (bf16[160,512]{1,0:T(8,128)(2,1)S(1)}, bf16[1,4096,384]{2,1,0:T(8,128)(2,1)}, bf16[1,4096,384]{2,1,0:T(8,128)(2,1)}, bf16[1,384,4096]{2,1,0:T(8,128)(2,1)}) custom-call(s32[1]{0:T(128)} %bitcast.place_ref, bf16[512,2048]{1,0:T(8,128)(2,1)} %bitcast.3.refs_2_.refs_0_, bf16[512,2048]{1,0:T(8,128)(2,1)} %collective-permute-done.4.refs_3_.refs_1_, ...), custom_call_target="tpu_custom_call" | custom-call | tf_op jit(solution)/shard_map/weight_grads/pallas_call | solution.py:85
  113.5 17.8 %all-to-all-done.2 = bf16[64,8,2176]{2,1,0:T(8,128)(2,1)S(1)} async-done(((bf16[64,8,2176]{2,1,0:T(8,128)(2,1)}), bf16[64,8,2176]{2,1,0:T(8,128)(2,1)S(1)}, u32[]{:S(2)}, u32[]{:S(2)}) %all-to-all-start.2) | async-done | bytes 2228256 | tf_op jit(solution)/shard_map/all_to_all | solution.py:343
  132.8 1.7 %collective-permute-start.9 = (f32[4,16]{1,0:T(4,128)S(1)}, f32[4,16]{1,0:T(4,128)S(1)}, u32[]{:S(2)}, u32[]{:S(2)}) collective-permute-start(f32[4,16]{1,0:T(4,128)S(1)} %get-tuple-element.65), channel_id=1, source_target_pairs={{0,1},{1,0},{2,3},{3,2},{4,5},{5,4},{6,7},{7,6},{8,9},{9,8},{10,11... | collective-permute-start | bytes 776 | tf_op jit(solution)/shard_map/ppermute | solution.py:340
  (49 shorter events, 6.7 us)
Async XLA Ops:
  0.6 2.9 %collective-permute-start.1 = (bf16[16,4096]{1,0:T(8,128)(2,1)}, bf16[16,4096]{1,0:T(8,128)(2,1)S(1)}, u32[]{:S(2)}, u32[]{:S(2)}) collective-permute-start(bf16[16,4096]{1,0:T(8,128)(2,1)} %refs_1_.3), channel_id=1, source_target_pairs={{0,1},{1,0},{2,3},{3,2},{4,5},{5,4},{6,7},{7,6},{8,9},{9,8},{10,11... | collective-permute-start | bytes 393224 | tf_op jit(solution)/shard_map/ppermute | solution.py:340
  2.1 1.4 %collective-permute-start = (s32[4,16]{1,0:T(4,128)}, s32[4,16]{1,0:T(4,128)S(1)}, u32[]{:S(2)}, u32[]{:S(2)}) collective-permute-start(s32[4,16]{1,0:T(4,128)} %bitcast.15), channel_id=1, source_target_pairs={{0,1},{1,0},{2,3},{3,2},{4,5},{5,4},{6,7},{7,6},{8,9},{9,8},{10,11... | collective-permute-start | bytes 776 | tf_op jit(solution)/shard_map/ppermute | solution.py:340
  3.5 14.4 %copy-start.18 = (bf16[16,4096]{1,0:T(8,128)(2,1)S(1)}, bf16[16,4096]{1,0:T(8,128)(2,1)}, u32[]{:S(2)}) copy-start(bf16[16,4096]{1,0:T(8,128)(2,1)} %refs_4_) | copy-start | bytes 393220
  3.5 14.9 %copy-start.19 = (f32[16,4]{0,1:T(4,128)S(1)}, f32[16,4]{0,1:T(4,128)}, u32[]{:S(2)}) copy-start(f32[16,4]{0,1:T(4,128)} %param.9) | copy-start | bytes 772
  3.5 16.1 %copy-start.20 = (s32[16,4]{0,1:T(4,128)S(1)}, s32[16,4]{0,1:T(4,128)}, u32[]{:S(2)}) copy-start(s32[16,4]{0,1:T(4,128)} %param.10) | copy-start | bytes 772
  3.5 19.8 %copy-start = (bf16[1,4096,384]{2,1,0:T(8,128)(2,1)S(1)}, bf16[1,4096,384]{2,1,0:T(8,128)(2,1)}, u32[]{:S(2)}) copy-start(bf16[1,4096,384]{2,1,0:T(8,128)(2,1)} %gate_ref.1) | copy-start | bytes 9437188
  6.4 39.2 %all-to-all-start = ((bf16[64,8,2048]{2,1,0:T(8,128)(2,1)}), bf16[64,8,2048]{2,1,0:T(8,128)(2,1)}, u32[]{:S(2)}, u32[]{:S(2)}) async-start(bf16[64,8,2048]{2,1,0:T(8,128)(2,1)} %bitcast.19), calls=%async_computation | async-start | bytes 4194304 | tf_op jit(solution)/shard_map/all_to_all | solution.py:343
  17.9 1.7 %collective-permute-start.3 = (bf16[16,4096]{1,0:T(8,128)(2,1)S(1)}, bf16[16,4096]{1,0:T(8,128)(2,1)S(1)}, u32[]{:S(2)}, u32[]{:S(2)}) collective-permute-start(bf16[16,4096]{1,0:T(8,128)(2,1)S(1)} %copy-done.18), channel_id=1, source_target_pairs={{0,1},{1,0},{2,3},{3,2},{4,5},{5,4},{6,7},{7,6},{8,9},{9,8},{10,11... | collective-permute-start | bytes 393224 | tf_op jit(solution)/shard_map/ppermute | solution.py:340
  18.4 1.2 collective-permute-start.2
  23.3 1.9 %copy-start.1 = (bf16[1,4096,384]{2,1,0:T(8,128)(2,1)S(1)}, bf16[1,4096,384]{2,1,0:T(8,128)(2,1)}, u32[]{:S(2)}) copy-start(bf16[1,4096,384]{2,1,0:T(8,128)(2,1)} %up_ref.1) | copy-start | bytes 9437188
  25.8 1.7 %copy-start.12 = (bf16[2048,768]{1,0:T(8,128)(2,1)}, bf16[2048,768]{1,0:T(8,128)(2,1)S(1)}, u32[]{:S(2)}) copy-start(bf16[2048,768]{1,0:T(8,128)(2,1)S(1)} %lend.1) | copy-start | bytes 9437188
  45.5 21.5 %collective-permute-start.5 = (bf16[2048,768]{1,0:T(8,128)(2,1)}, bf16[2048,768]{1,0:T(8,128)(2,1)}, u32[]{:S(2)}, u32[]{:S(2)}) collective-permute-start(bf16[2048,768]{1,0:T(8,128)(2,1)} %copy-done.12), channel_id=1, source_target_pairs={{0,1},{1,0},{2,3},{3,2},{4,5},{5,4},{6,7},{7,6},{8,9},{9,8},{10,11... | collective-permute-start | bytes 9437192 | tf_op jit(solution)/shard_map/ppermute | solution.py:340
  48.3 8.6 %collective-permute-start.4 = (bf16[512,2048]{1,0:T(8,128)(2,1)}, bf16[512,2048]{1,0:T(8,128)(2,1)}, u32[]{:S(2)}, u32[]{:S(2)}) collective-permute-start(bf16[512,2048]{1,0:T(8,128)(2,1)} %bitcast.3.refs_2_.refs_0_), channel_id=1, source_target_pairs={{0,1},{1,0},{2,3},{3,2},{4,5},{5,4},{6,7},{7,6},{8,9},{9,8},{10,11... | collective-permute-start | bytes 6291464 | tf_op jit(solution)/shard_map/ppermute | solution.py:340
  48.3 33.0 %all-to-all-start.1 = ((bf16[64,8,2048]{2,1,0:T(8,128)(2,1)}), bf16[64,8,2048]{2,1,0:T(8,128)(2,1)}, u32[]{:S(2)}, u32[]{:S(2)}) async-start(bf16[64,8,2048]{2,1,0:T(8,128)(2,1)} %bitcast.20), calls=%async_computation.1 | async-start | bytes 4194304 | tf_op jit(solution)/shard_map/all_to_all | solution.py:343
  57.0 1.9 %copy-start.2 = (bf16[1,4096,384]{2,1,0:T(8,128)(2,1)S(1)}, bf16[1,4096,384]{2,1,0:T(8,128)(2,1)}, u32[]{:S(2)}) copy-start(bf16[1,4096,384]{2,1,0:T(8,128)(2,1)} %up_ref.1) | copy-start | bytes 9437188
  58.8 8.2 %copy-start.11 = (bf16[1,384,4096]{2,1,0:T(8,128)(2,1)S(1)}, bf16[1,384,4096]{2,1,0:T(8,128)(2,1)}, u32[]{:S(2)}) copy-start(bf16[1,384,4096]{2,1,0:T(8,128)(2,1)} %down_ref.1) | copy-start | bytes 9437188
  65.8 1.2 copy-start.13
  71.5 1.7 %copy-start.3 = (bf16[4096,384]{1,0:T(8,128)(2,1)}, bf16[4096,384]{1,0:T(8,128)(2,1)S(1)}, u32[]{:S(2)}) copy-start(bf16[4096,384]{1,0:T(8,128)(2,1)S(1)} %get-tuple-element.49.back_ref) | copy-start | bytes 9437188
  73.2 1.7 %copy-start.7 = (bf16[768,2048]{1,0:T(8,128)(2,1)}, bf16[768,2048]{1,0:T(8,128)(2,1)S(1)}, u32[]{:S(2)}) copy-start(bf16[768,2048]{1,0:T(8,128)(2,1)S(1)} %get-tuple-element.48.turned_ref) | copy-start | bytes 9437188
  74.8 1.7 %copy-start.9 = (bf16[768,2048]{1,0:T(8,128)(2,1)}, bf16[768,2048]{1,0:T(8,128)(2,1)S(1)}, u32[]{:S(2)}) copy-start(bf16[768,2048]{1,0:T(8,128)(2,1)S(1)} %get-tuple-element.56.turned_ref) | copy-start | bytes 9437188
  81.3 7.9 %collective-permute-start.6 = (bf16[512,2048]{1,0:T(8,128)(2,1)}, bf16[512,2048]{1,0:T(8,128)(2,1)S(1)}, u32[]{:S(2)}, u32[]{:S(2)}) collective-permute-start(bf16[512,2048]{1,0:T(8,128)(2,1)} %bitcast.6.own_ref.refs_2_), channel_id=1, source_target_pairs={{0,1},{1,0},{2,3},{3,2},{4,5},{5,4},{6,7},{7,6},{8,9},{9,8},{10,11... | collective-permute-start | bytes 6291464 | tf_op jit(solution)/shard_map/ppermute | solution.py:340
  84.4 1.9 %copy-start.4 = (bf16[4096,384]{1,0:T(8,128)(2,1)S(1)}, bf16[4096,384]{1,0:T(8,128)(2,1)}, u32[]{:S(2)}) copy-start(bf16[4096,384]{1,0:T(8,128)(2,1)} %copy-done.3) | copy-start | bytes 9437188
  86.3 3.0 %copy-start.14 = (f32[512,768]{1,0:T(8,128)S(1)}, f32[512,768]{1,0:T(8,128)}, u32[]{:S(2)}) copy-start(f32[512,768]{1,0:T(8,128)} %copy-done.13) | copy-start | bytes 4718596
  89.2 2.6 %copy-start.10 = (bf16[768,2048]{1,0:T(8,128)(2,1)S(1)}, bf16[768,2048]{1,0:T(8,128)(2,1)}, u32[]{:S(2)}) copy-start(bf16[768,2048]{1,0:T(8,128)(2,1)} %copy-done.9) | copy-start | bytes 9437188
  89.3 1.4 %copy-start.5 = (bf16[512,2048]{1,0:T(8,128)(2,1)}, bf16[512,2048]{1,0:T(8,128)(2,1)S(1)}, u32[]{:S(2)}) copy-start(bf16[512,2048]{1,0:T(8,128)(2,1)S(1)} %collective-permute-done.6.other_ref.refs_3_) | copy-start | bytes 6291460
  90.7 3.0 %copy-start.8 = (bf16[768,2048]{1,0:T(8,128)(2,1)S(1)}, bf16[768,2048]{1,0:T(8,128)(2,1)}, u32[]{:S(2)}) copy-start(bf16[768,2048]{1,0:T(8,128)(2,1)} %copy-done.7) | copy-start | bytes 9437188
  90.7 3.0 %collective-permute-start.7 = (bf16[512,768]{1,0:T(8,128)(2,1)S(1)}, bf16[512,768]{1,0:T(8,128)(2,1)S(1)}, u32[]{:S(2)}, u32[]{:S(2)}) collective-permute-start(bf16[512,768]{1,0:T(8,128)(2,1)S(1)} %get-tuple-element.55.deltas_ref.refs_4_), channel_id=1, source_target_pairs={{0,1},{1,0},{2,3},{3,2},{4,5},{5,4},{6,7},{7,6},{8,9},{9,8},{10,11... | collective-permute-start | bytes 2359304 | tf_op jit(solution)/shard_map/ppermute | solution.py:340
  96.4 34.9 %all-to-all-start.2 = ((bf16[64,8,2176]{2,1,0:T(8,128)(2,1)}), bf16[64,8,2176]{2,1,0:T(8,128)(2,1)S(1)}, u32[]{:S(2)}, u32[]{:S(2)}) async-start(bf16[64,8,2176]{2,1,0:T(8,128)(2,1)} %bitcast.18), calls=%async_computation.2 | async-start | bytes 4456448 | tf_op jit(solution)/shard_map/all_to_all | solution.py:343
  101.7 1.6 %copy-start.6 = (bf16[512,2048]{1,0:T(8,128)(2,1)S(1)}, bf16[512,2048]{1,0:T(8,128)(2,1)}, u32[]{:S(2)}) copy-start(bf16[512,2048]{1,0:T(8,128)(2,1)} %copy-done.5) | copy-start | bytes 6291460
  131.3 0.9 copy-start.16
  132.8 2.5 %collective-permute-start.9 = (f32[4,16]{1,0:T(4,128)S(1)}, f32[4,16]{1,0:T(4,128)S(1)}, u32[]{:S(2)}, u32[]{:S(2)}) collective-permute-start(f32[4,16]{1,0:T(4,128)S(1)} %get-tuple-element.65), channel_id=1, source_target_pairs={{0,1},{1,0},{2,3},{3,2},{4,5},{5,4},{6,7},{7,6},{8,9},{9,8},{10,11... | collective-permute-start | bytes 776 | tf_op jit(solution)/shard_map/ppermute | solution.py:340
  134.5 1.4 %collective-permute-start.8 = (bf16[16,2048]{1,0:T(8,128)(2,1)S(1)}, bf16[16,2048]{1,0:T(8,128)(2,1)S(1)}, u32[]{:S(2)}, u32[]{:S(2)}) collective-permute-start(bf16[16,2048]{1,0:T(8,128)(2,1)S(1)} %get-tuple-element.63), channel_id=1, source_target_pairs={{0,1},{1,0},{2,3},{3,2},{4,5},{5,4},{6,7},{7,6},{8,9},{9,8},{10,11... | collective-permute-start | bytes 196616 | tf_op jit(solution)/shard_map/ppermute | solution.py:340
  (2 other events, 1.6 us)

commit v4 on v3

--- a/solution.py
+++ b/solution.py
@@ -242,8 +242,22 @@
     return dot(grads_ref[...], back_ref[columns(which * half, half), :])
 
 
-def back_early_kernel(place_ref, back_ref, own_ref, out_ref):
-    out_ref[...] = back_product(place_ref[0], back_ref, own_ref)
+def back_early_kernel(place_ref, back_hbm, own_hbm, out_ref, back_ref, own_ref, sems):
+    steps, step, _ = back_ref.shape
+    half = steps * step
+    groups = [
+        [
+            pltpu.make_async_copy(own_hbm.at[:, pl.ds(n * step, step)], own_ref.at[n], sems.at[2 * n]),
+            pltpu.make_async_copy(back_hbm.at[columns(place_ref[0] * half + n * step, step), :], back_ref.at[n], sems.at[2 * n + 1]),
+        ]
+        for n in range(steps)
+    ]
+    stages = Stages(groups, steps)
+    scaled = 0.0
+    for n in range(steps):
+        stages.wait(n)
+        scaled += dot(own_ref[n], back_ref[n])
+    out_ref[...] = scaled
 
 
 def back_late_kernel(place_ref, back_ref, other_ref, sum_ref, factors_ref, hidden_ref, deltas_ref, score_ref):
@@ -351,7 +365,8 @@
     rows_out = call(
         build_rows_kernel, "build_rows", [out],
         place, *[pltpu.with_memory_space_constraint(x, pltpu.HBM) for x in (ids, tokens)], ids_pair[1], tokens_pair[1],
-        direct=1, near=2, scratch=scratch, far=True,
+        direct=1, near=2, far=True,
+        scratch=[pltpu.VMEM((half // 256, lines, 256), BF16), pltpu.SemaphoreType.DMA((half // 256,))],
     )[0]
     later = after(comb, out_grad, rows_out)[:2]
     comb_pair, out_grad_pair = [(x, swap(x)) for x in later]
@@ -387,7 +402,18 @@
         deliver(grads_out), factors, hidden, back, parts_own, parts_other
     )
     grads_pair = (grads, swap(grads))
-    scaled = call_near(back_early_kernel, "back_early", [((lines, ff), F32)], place, back, grads)[0]
+    scaled = call(
+        back_early_kernel,
+        "back_early",
+        [((lines, ff), F32)],
+        place, pltpu.with_memory_space_constraint(back, pltpu.HBM), grads,
+        raw=2,
+        scratch=[
+            pltpu.VMEM((CORES, quarter, ff), BF16),
+            pltpu.VMEM((CORES, lines, quarter), BF16),
+            pltpu.SemaphoreType.DMA((2 * CORES,)),
+        ],
+    )[0]
     other, scaled = after(grads_pair[1], scaled)
     deltas, score = call_near(
         back_late_kernel,

time: 137 us -> 136 us (level)
  local copies, waits for them, and re-layouts: 18.8 us -> 15.9 us
  starting transfers between devices: 32.5 us -> 34.2 us
    pallas_call x5 -> x6, Pallas kernels: 22.7 us -> 26.1 us  [call(): pl.pallas_call(body, in_specs=[SMEM] + [HBM] * (raw + given) + [VMEM] * n...]
    pallas_call x6 -> x5, Pallas kernels: 13.9 us -> 10.9 us  [call_near(): pl.pallas_call(kernel, in_specs=[SMEM] + [VMEM] * len(args), out_specs=[V...]
    unnamed x42, local copies, waits for them, and re-layouts: 18.8 us -> 15.9 us
    ppermute x10, starting transfers between devices: 9.98 us -> 11.7 us  [swap(): return lax.ppermute(x, 'core', [(0, 1), (1, 0)])]
  transfers between devices with their start and end apart: 13 -> 13, of which waited for: 7 -> 8; matrix products, arithmetic and copies ran while one was open for 0% -> 0% of each run, Pallas kernels for 21% -> 22%
where the time goes in v4:
time: 136 us
  waiting for transfers between devices  46.4 us (34%)
  Pallas kernels  37 us (27%)
  starting transfers between devices  34.2 us (25%)
  local copies, waits for them, and re-layouts  15.9 us (12%)
    all_to_all x3, waiting for transfers between devices, deliver(): lax.all_to_all(x.reshape(chips, SLOTS, x.shape[1]), CHIPS, split_axis=0,...  39.8 us
    pallas_call x6, Pallas kernels, call(): pl.pallas_call(body, in_specs=[SMEM] + [HBM] * (raw + given) + [VMEM] * n...  26.1 us
    all_to_all x3, starting transfers between devices, deliver(): lax.all_to_all(x.reshape(chips, SLOTS, x.shape[1]), CHIPS, split_axis=0,...  22.5 us
    unnamed x42, local copies, waits for them, and re-layouts  15.9 us
    ppermute x10, starting transfers between devices, swap(): return lax.ppermute(x, 'core', [(0, 1), (1, 0)])  11.7 us
    pallas_call x5, Pallas kernels, call_near(): pl.pallas_call(kernel, in_specs=[SMEM] + [VMEM] * len(args), out_specs=[V...  10.9 us
    ppermute x10, waiting for transfers between devices, swap(): return lax.ppermute(x, 'core', [(0, 1), (1, 0)])  6.58 us
  transfers between devices with their start and end apart: 13, of which 8 were waited for; matrix products, arithmetic and copies ran while one was open for 0% of the time, Pallas kernels for 22%

profile of v4, /device:TPU:1, one launch (start us, length us, event | category | flops | bytes accessed | tf_op | source)
XLA Modules:
  0.0 135.6 jit_solution(6339655612506518894)
XLA Ops:
  0.6 1.5 %collective-permute-start.1 = (bf16[16,4096]{1,0:T(8,128)(2,1)}, bf16[16,4096]{1,0:T(8,128)(2,1)S(1)}, u32[]{:S(2)}, u32[]{:S(2)}) collective-permute-start(bf16[16,4096]{1,0:T(8,128)(2,1)} %refs_1_.3), channel_id=1, source_target_pairs={{0,1},{1,0},{2,3},{3,2},{4,5},{5,4},{6,7},{7,6},{8,9},{9,8},{10,11... | collective-permute-start | bytes 393224 | tf_op jit(solution)/shard_map/ppermute | solution.py:354
  2.2 1.3 collective-permute-done.refs_2_.refs_1_
  3.5 2.9 %build_rows.1 = bf16[512,2048]{1,0:T(8,128)(2,1)} custom-call(s32[1]{0:T(128)} %bitcast.place_ref, s32[4,16]{1,0:T(4,128)} %bitcast.16, bf16[16,4096]{1,0:T(8,128)(2,1)} %refs_1_.3, s32[4,16]{1,0:T(4,128)S(1)} %collective-permute-done.refs_2_.refs_1_, bf16[16,4096]{1,0:T(8,128)(2,1)S(1)} %collective-permute-done.1.refs_3_), custom_call_target="tpu_custom_call" | custom-call | tf_op jit(solution)/shard_map/build_rows/pallas_call | solution.py:85
  6.4 11.5 %all-to-all-start = ((bf16[64,8,2048]{2,1,0:T(8,128)(2,1)}), bf16[64,8,2048]{2,1,0:T(8,128)(2,1)}, u32[]{:S(2)}, u32[]{:S(2)}) async-start(bf16[64,8,2048]{2,1,0:T(8,128)(2,1)} %bitcast.19), calls=%async_computation | async-start | bytes 4194304 | tf_op jit(solution)/shard_map/all_to_all | solution.py:357
  18.6 1.1 collective-permute-done.2.refs_3_
  19.6 3.7 %build_grads.1 = (bf16[160,512]{1,0:T(8,128)(2,1)}, bf16[512,2048]{1,0:T(8,128)(2,1)}) custom-call(s32[1]{0:T(128)} %bitcast.place_ref, s32[4,16]{1,0:T(4,128)S(1)} %bitcast.17, s32[4,16]{1,0:T(4,128)S(1)} %collective-permute-done.refs_2_.refs_1_, f32[4,16]{1,0:T(4,128)S(1)} %bitcast.14, f32[4,16]{1,0:T(4,128)S(1)} %collective-permute-done.2.refs_3_, ...), custom_call_target="tpu_custom_call" | custom-call | tf_op jit(solution)/shard_map/build_grads/pallas_call | solution.py:85
  23.4 1.9 %copy-done.1 = bf16[1,4096,384]{2,1,0:T(8,128)(2,1)S(1)} copy-done((bf16[1,4096,384]{2,1,0:T(8,128)(2,1)S(1)}, bf16[1,4096,384]{2,1,0:T(8,128)(2,1)}, u32[]{:S(2)}) %copy-start.1) | copy-done | bytes 3145752
  25.8 1.7 %copy-done.12 = bf16[2048,768]{1,0:T(8,128)(2,1)} copy-done((bf16[2048,768]{1,0:T(8,128)(2,1)}, bf16[2048,768]{1,0:T(8,128)(2,1)S(1)}, u32[]{:S(2)}) %copy-start.12) | copy-done | bytes 3145752
  27.5 18.1 %all-to-all-done = bf16[64,8,2048]{2,1,0:T(8,128)(2,1)} async-done(((bf16[64,8,2048]{2,1,0:T(8,128)(2,1)}), bf16[64,8,2048]{2,1,0:T(8,128)(2,1)}, u32[]{:S(2)}, u32[]{:S(2)}) %all-to-all-start) | async-done | bytes 2097184 | tf_op jit(solution)/shard_map/all_to_all | solution.py:357
  45.6 2.8 %collective-permute-start.5 = (bf16[2048,768]{1,0:T(8,128)(2,1)}, bf16[2048,768]{1,0:T(8,128)(2,1)}, u32[]{:S(2)}, u32[]{:S(2)}) collective-permute-start(bf16[2048,768]{1,0:T(8,128)(2,1)} %copy-done.12), channel_id=1, source_target_pairs={{0,1},{1,0},{2,3},{3,2},{4,5},{5,4},{6,7},{7,6},{8,9},{9,8},{10,11... | collective-permute-start | bytes 9437192 | tf_op jit(solution)/shard_map/ppermute | solution.py:354
  48.4 5.7 %all-to-all-start.1 = ((bf16[64,8,2048]{2,1,0:T(8,128)(2,1)}), bf16[64,8,2048]{2,1,0:T(8,128)(2,1)}, u32[]{:S(2)}, u32[]{:S(2)}) async-start(bf16[64,8,2048]{2,1,0:T(8,128)(2,1)} %bitcast.20), calls=%async_computation.1 | async-start | bytes 4194304 | tf_op jit(solution)/shard_map/all_to_all | solution.py:357
  54.1 2.9 %collective-permute-done.4.refs_3_.refs_1_ = bf16[512,2048]{1,0:T(8,128)(2,1)} collective-permute-done((bf16[512,2048]{1,0:T(8,128)(2,1)}, bf16[512,2048]{1,0:T(8,128)(2,1)}, u32[]{:S(2)}, u32[]{:S(2)}) %collective-permute-start.4) | collective-permute-done | bytes 2097184 | tf_op jit(solution)/shard_map/ppermute | solution.py:354
  57.0 1.9 %copy-done.2 = bf16[1,4096,384]{2,1,0:T(8,128)(2,1)S(1)} copy-done((bf16[1,4096,384]{2,1,0:T(8,128)(2,1)S(1)}, bf16[1,4096,384]{2,1,0:T(8,128)(2,1)}, u32[]{:S(2)}) %copy-start.2) | copy-done | bytes 3145752
  58.9 6.9 %gate_up.1 = (f32[512,768]{1,0:T(8,128)S(1)}, bf16[512,384]{1,0:T(8,128)(2,1)S(1)}) custom-call(s32[1]{0:T(128)} %bitcast.place_ref, bf16[1,4096,384]{2,1,0:T(8,128)(2,1)S(1)} %copy-done, bf16[1,4096,384]{2,1,0:T(8,128)(2,1)S(1)} %copy-done.2, bf16[512,2048]{1,0:T(8,128)(2,1)} %bitcast.3.refs_2_.refs_0_, bf16[512,2048]{1,0:T(8,128)(2,1)} %collective-permute-done.4.refs_3_.refs_1_), custom_call_target="tpu_custom_call" | custom-call | tf_op jit(solution)/shard_map/gate_up/pallas_call | solution.py:85
  65.8 1.2 copy-done.13
  67.1 4.5 %turn.1 = (bf16[4096,384]{1,0:T(8,128)(2,1)S(1)}, bf16[768,2048]{1,0:T(8,128)(2,1)S(1)}, bf16[768,2048]{1,0:T(8,128)(2,1)S(1)}) custom-call(s32[1]{0:T(128)} %bitcast.place_ref, bf16[1,4096,384]{2,1,0:T(8,128)(2,1)S(1)} %copy-done, bf16[1,4096,384]{2,1,0:T(8,128)(2,1)S(1)} %copy-done.2, bf16[1,384,4096]{2,1,0:T(8,128)(2,1)S(1)} %copy-done.11, ...), custom_call_target="tpu_custom_call" | custom-call | tf_op jit(solution)/shard_map/turn/pallas_call | solution.py:100
  71.6 1.7 %copy-done.3 = bf16[4096,384]{1,0:T(8,128)(2,1)} copy-done((bf16[4096,384]{1,0:T(8,128)(2,1)}, bf16[4096,384]{1,0:T(8,128)(2,1)S(1)}, u32[]{:S(2)}) %copy-start.3) | copy-done | bytes 3145752
  73.2 1.7 %copy-done.7 = bf16[768,2048]{1,0:T(8,128)(2,1)} copy-done((bf16[768,2048]{1,0:T(8,128)(2,1)}, bf16[768,2048]{1,0:T(8,128)(2,1)S(1)}, u32[]{:S(2)}) %copy-start.7) | copy-done | bytes 3145752
  74.9 1.7 %copy-done.9 = bf16[768,2048]{1,0:T(8,128)(2,1)} copy-done((bf16[768,2048]{1,0:T(8,128)(2,1)}, bf16[768,2048]{1,0:T(8,128)(2,1)S(1)}, u32[]{:S(2)}) %copy-start.9) | copy-done | bytes 3145752
  76.5 4.8 %all-to-all-done.1 = bf16[64,8,2048]{2,1,0:T(8,128)(2,1)} async-done(((bf16[64,8,2048]{2,1,0:T(8,128)(2,1)}), bf16[64,8,2048]{2,1,0:T(8,128)(2,1)}, u32[]{:S(2)}, u32[]{:S(2)}) %all-to-all-start.1) | async-done | bytes 2097184 | tf_op jit(solution)/shard_map/all_to_all | solution.py:357
  81.4 3.0 %collective-permute-start.6 = (bf16[512,2048]{1,0:T(8,128)(2,1)}, bf16[512,2048]{1,0:T(8,128)(2,1)S(1)}, u32[]{:S(2)}, u32[]{:S(2)}) collective-permute-start(bf16[512,2048]{1,0:T(8,128)(2,1)} %bitcast.6.refs_1_.refs_2_), channel_id=1, source_target_pairs={{0,1},{1,0},{2,3},{3,2},{4,5},{5,4},{6,7},{7,6},{8,9},{9,8},{10,11... | collective-permute-start | bytes 6291464 | tf_op jit(solution)/shard_map/ppermute | solution.py:354
  84.4 3.4 %back_early.1.sum_ref = f32[512,384]{1,0:T(8,128)S(1)} custom-call(s32[1]{0:T(128)} %bitcast.place_ref, bf16[4096,384]{1,0:T(8,128)(2,1)} %copy-done.3, bf16[512,2048]{1,0:T(8,128)(2,1)} %bitcast.6.refs_1_.refs_2_), custom_call_target="tpu_custom_call" | custom-call | tf_op jit(solution)/shard_map/back_early/pallas_call | solution.py:85
  88.4 1.4 %back_late.1 = (bf16[512,768]{1,0:T(8,128)(2,1)S(1)}, bf16[512,128]{1,0:T(8,128)(2,1)S(1)}) custom-call(s32[1]{0:T(128)} %bitcast.place_ref, bf16[4096,384]{1,0:T(8,128)(2,1)S(1)} %copy-done.4, bf16[512,2048]{1,0:T(8,128)(2,1)S(1)} %collective-permute-done.6.other_ref.refs_3_, f32[512,384]{1,0:T(8,128)S(1)} %back_early.1.sum_ref, f32[512,768]{1,0:T(8,128)S(1)} %copy-done.14, ...), custom_call_target="tpu_custom_call" | custom-call | tf_op jit(solution)/shard_map/back_late/pallas_call | solution.py:100
  90.4 1.8 %parts_own.1.before_ref = bf16[512,2048]{1,0:T(8,128)(2,1)S(1)} custom-call(s32[1]{0:T(128)} %bitcast.place_ref, bf16[768,2048]{1,0:T(8,128)(2,1)S(1)} %copy-done.10, bf16[512,768]{1,0:T(8,128)(2,1)S(1)} %get-tuple-element.55.deltas_ref.refs_4_), custom_call_target="tpu_custom_call" | custom-call | tf_op jit(solution)/shard_map/parts_own/pallas_call | solution.py:100
  92.2 2.7 %parts_sum.1 = bf16[512,2176]{1,0:T(8,128)(2,1)} custom-call(s32[1]{0:T(128)} %bitcast.place_ref, bf16[768,2048]{1,0:T(8,128)(2,1)S(1)} %copy-done.8, bf16[512,768]{1,0:T(8,128)(2,1)S(1)} %collective-permute-done.7.deltas_ref, bf16[512,2048]{1,0:T(8,128)(2,1)S(1)} %parts_own.1.before_ref, bf16[512,128]{1,0:T(8,128)(2,1)S(1)} %get-tuple-element.59.score_ref), custom_call_target="tpu_custom_call" | custom-call | tf_op jit(solution)/shard_map/parts_sum/pallas_call | solution.py:100
  94.9 5.3 %all-to-all-start.2 = ((bf16[64,8,2176]{2,1,0:T(8,128)(2,1)}), bf16[64,8,2176]{2,1,0:T(8,128)(2,1)S(1)}, u32[]{:S(2)}, u32[]{:S(2)}) async-start(bf16[64,8,2176]{2,1,0:T(8,128)(2,1)} %bitcast.18), calls=%async_computation.2 | async-start | bytes 4456448 | tf_op jit(solution)/shard_map/all_to_all | solution.py:357
  100.2 1.6 %copy-done.6 = bf16[512,2048]{1,0:T(8,128)(2,1)S(1)} copy-done((bf16[512,2048]{1,0:T(8,128)(2,1)S(1)}, bf16[512,2048]{1,0:T(8,128)(2,1)}, u32[]{:S(2)}) %copy-start.6) | copy-done | bytes 2097176
  101.8 0.9 copy-done.17
  102.7 8.6 %weight_grads.1 = (bf16[160,512]{1,0:T(8,128)(2,1)S(1)}, bf16[1,4096,384]{2,1,0:T(8,128)(2,1)}, bf16[1,4096,384]{2,1,0:T(8,128)(2,1)}, bf16[1,384,4096]{2,1,0:T(8,128)(2,1)}) custom-call(s32[1]{0:T(128)} %bitcast.place_ref, bf16[512,2048]{1,0:T(8,128)(2,1)} %bitcast.3.refs_2_.refs_0_, bf16[512,2048]{1,0:T(8,128)(2,1)} %collective-permute-done.4.refs_3_.refs_1_, ...), custom_call_target="tpu_custom_call" | custom-call | tf_op jit(solution)/shard_map/weight_grads/pallas_call | solution.py:85
  112.0 17.0 %all-to-all-done.2 = bf16[64,8,2176]{2,1,0:T(8,128)(2,1)S(1)} async-done(((bf16[64,8,2176]{2,1,0:T(8,128)(2,1)}), bf16[64,8,2176]{2,1,0:T(8,128)(2,1)S(1)}, u32[]{:S(2)}, u32[]{:S(2)}) %all-to-all-start.2) | async-done | bytes 2228256 | tf_op jit(solution)/shard_map/all_to_all | solution.py:357
  128.9 0.9 copy-done.16
  130.5 3.1 %collective-permute-start.9 = (f32[4,16]{1,0:T(4,128)S(1)}, f32[4,16]{1,0:T(4,128)S(1)}, u32[]{:S(2)}, u32[]{:S(2)}) collective-permute-start(f32[4,16]{1,0:T(4,128)S(1)} %get-tuple-element.65), channel_id=1, source_target_pairs={{0,1},{1,0},{2,3},{3,2},{4,5},{5,4},{6,7},{7,6},{8,9},{9,8},{10,11... | collective-permute-start | bytes 776 | tf_op jit(solution)/shard_map/ppermute | solution.py:354
  (49 shorter events, 5.9 us)
Async XLA Ops:
  0.6 2.9 %collective-permute-start.1 = (bf16[16,4096]{1,0:T(8,128)(2,1)}, bf16[16,4096]{1,0:T(8,128)(2,1)S(1)}, u32[]{:S(2)}, u32[]{:S(2)}) collective-permute-start(bf16[16,4096]{1,0:T(8,128)(2,1)} %refs_1_.3), channel_id=1, source_target_pairs={{0,1},{1,0},{2,3},{3,2},{4,5},{5,4},{6,7},{7,6},{8,9},{9,8},{10,11... | collective-permute-start | bytes 393224 | tf_op jit(solution)/shard_map/ppermute | solution.py:354
  2.1 1.4 %collective-permute-start = (s32[4,16]{1,0:T(4,128)}, s32[4,16]{1,0:T(4,128)S(1)}, u32[]{:S(2)}, u32[]{:S(2)}) collective-permute-start(s32[4,16]{1,0:T(4,128)} %bitcast.15), channel_id=1, source_target_pairs={{0,1},{1,0},{2,3},{3,2},{4,5},{5,4},{6,7},{7,6},{8,9},{9,8},{10,11... | collective-permute-start | bytes 776 | tf_op jit(solution)/shard_map/ppermute | solution.py:354
  3.5 14.4 %copy-start.18 = (bf16[16,4096]{1,0:T(8,128)(2,1)S(1)}, bf16[16,4096]{1,0:T(8,128)(2,1)}, u32[]{:S(2)}) copy-start(bf16[16,4096]{1,0:T(8,128)(2,1)} %refs_4_) | copy-start | bytes 393220
  3.5 15.0 %copy-start.19 = (f32[16,4]{0,1:T(4,128)S(1)}, f32[16,4]{0,1:T(4,128)}, u32[]{:S(2)}) copy-start(f32[16,4]{0,1:T(4,128)} %param.9) | copy-start | bytes 772
  3.5 16.1 %copy-start.20 = (s32[16,4]{0,1:T(4,128)S(1)}, s32[16,4]{0,1:T(4,128)}, u32[]{:S(2)}) copy-start(s32[16,4]{0,1:T(4,128)} %param.10) | copy-start | bytes 772
  3.5 19.8 %copy-start = (bf16[1,4096,384]{2,1,0:T(8,128)(2,1)S(1)}, bf16[1,4096,384]{2,1,0:T(8,128)(2,1)}, u32[]{:S(2)}) copy-start(bf16[1,4096,384]{2,1,0:T(8,128)(2,1)} %gate_ref.1) | copy-start | bytes 9437188
  6.4 39.2 %all-to-all-start = ((bf16[64,8,2048]{2,1,0:T(8,128)(2,1)}), bf16[64,8,2048]{2,1,0:T(8,128)(2,1)}, u32[]{:S(2)}, u32[]{:S(2)}) async-start(bf16[64,8,2048]{2,1,0:T(8,128)(2,1)} %bitcast.19), calls=%async_computation | async-start | bytes 4194304 | tf_op jit(solution)/shard_map/all_to_all | solution.py:357
  17.9 1.7 %collective-permute-start.3 = (bf16[16,4096]{1,0:T(8,128)(2,1)S(1)}, bf16[16,4096]{1,0:T(8,128)(2,1)S(1)}, u32[]{:S(2)}, u32[]{:S(2)}) collective-permute-start(bf16[16,4096]{1,0:T(8,128)(2,1)S(1)} %copy-done.18), channel_id=1, source_target_pairs={{0,1},{1,0},{2,3},{3,2},{4,5},{5,4},{6,7},{7,6},{8,9},{9,8},{10,11... | collective-permute-start | bytes 393224 | tf_op jit(solution)/shard_map/ppermute | solution.py:354
  18.5 1.2 collective-permute-start.2
  23.4 1.9 %copy-start.1 = (bf16[1,4096,384]{2,1,0:T(8,128)(2,1)S(1)}, bf16[1,4096,384]{2,1,0:T(8,128)(2,1)}, u32[]{:S(2)}) copy-start(bf16[1,4096,384]{2,1,0:T(8,128)(2,1)} %up_ref.1) | copy-start | bytes 9437188
  25.8 1.7 %copy-start.12 = (bf16[2048,768]{1,0:T(8,128)(2,1)}, bf16[2048,768]{1,0:T(8,128)(2,1)S(1)}, u32[]{:S(2)}) copy-start(bf16[2048,768]{1,0:T(8,128)(2,1)S(1)} %lend.1) | copy-start | bytes 9437188
  45.6 21.5 %collective-permute-start.5 = (bf16[2048,768]{1,0:T(8,128)(2,1)}, bf16[2048,768]{1,0:T(8,128)(2,1)}, u32[]{:S(2)}, u32[]{:S(2)}) collective-permute-start(bf16[2048,768]{1,0:T(8,128)(2,1)} %copy-done.12), channel_id=1, source_target_pairs={{0,1},{1,0},{2,3},{3,2},{4,5},{5,4},{6,7},{7,6},{8,9},{9,8},{10,11... | collective-permute-start | bytes 9437192 | tf_op jit(solution)/shard_map/ppermute | solution.py:354
  48.4 8.6 %collective-permute-start.4 = (bf16[512,2048]{1,0:T(8,128)(2,1)}, bf16[512,2048]{1,0:T(8,128)(2,1)}, u32[]{:S(2)}, u32[]{:S(2)}) collective-permute-start(bf16[512,2048]{1,0:T(8,128)(2,1)} %bitcast.3.refs_2_.refs_0_), channel_id=1, source_target_pairs={{0,1},{1,0},{2,3},{3,2},{4,5},{5,4},{6,7},{7,6},{8,9},{9,8},{10,11... | collective-permute-start | bytes 6291464 | tf_op jit(solution)/shard_map/ppermute | solution.py:354
  48.4 33.0 %all-to-all-start.1 = ((bf16[64,8,2048]{2,1,0:T(8,128)(2,1)}), bf16[64,8,2048]{2,1,0:T(8,128)(2,1)}, u32[]{:S(2)}, u32[]{:S(2)}) async-start(bf16[64,8,2048]{2,1,0:T(8,128)(2,1)} %bitcast.20), calls=%async_computation.1 | async-start | bytes 4194304 | tf_op jit(solution)/shard_map/all_to_all | solution.py:357
  57.0 1.9 %copy-start.2 = (bf16[1,4096,384]{2,1,0:T(8,128)(2,1)S(1)}, bf16[1,4096,384]{2,1,0:T(8,128)(2,1)}, u32[]{:S(2)}) copy-start(bf16[1,4096,384]{2,1,0:T(8,128)(2,1)} %up_ref.1) | copy-start | bytes 9437188
  58.9 8.2 %copy-start.11 = (bf16[1,384,4096]{2,1,0:T(8,128)(2,1)S(1)}, bf16[1,384,4096]{2,1,0:T(8,128)(2,1)}, u32[]{:S(2)}) copy-start(bf16[1,384,4096]{2,1,0:T(8,128)(2,1)} %down_ref.1) | copy-start | bytes 9437188
  65.8 1.2 copy-start.13
  71.5 1.7 %copy-start.3 = (bf16[4096,384]{1,0:T(8,128)(2,1)}, bf16[4096,384]{1,0:T(8,128)(2,1)S(1)}, u32[]{:S(2)}) copy-start(bf16[4096,384]{1,0:T(8,128)(2,1)S(1)} %get-tuple-element.49.refs_0_.back_ref) | copy-start | bytes 9437188
  73.2 1.7 %copy-start.7 = (bf16[768,2048]{1,0:T(8,128)(2,1)}, bf16[768,2048]{1,0:T(8,128)(2,1)S(1)}, u32[]{:S(2)}) copy-start(bf16[768,2048]{1,0:T(8,128)(2,1)S(1)} %get-tuple-element.48.turned_ref) | copy-start | bytes 9437188
  74.9 1.7 %copy-start.9 = (bf16[768,2048]{1,0:T(8,128)(2,1)}, bf16[768,2048]{1,0:T(8,128)(2,1)S(1)}, u32[]{:S(2)}) copy-start(bf16[768,2048]{1,0:T(8,128)(2,1)S(1)} %get-tuple-element.56.turned_ref) | copy-start | bytes 9437188
  76.5 11.9 %copy-start.14 = (f32[512,768]{1,0:T(8,128)S(1)}, f32[512,768]{1,0:T(8,128)}, u32[]{:S(2)}) copy-start(f32[512,768]{1,0:T(8,128)} %copy-done.13) | copy-start | bytes 4718596
  81.4 7.0 %copy-start.4 = (bf16[4096,384]{1,0:T(8,128)(2,1)S(1)}, bf16[4096,384]{1,0:T(8,128)(2,1)}, u32[]{:S(2)}) copy-start(bf16[4096,384]{1,0:T(8,128)(2,1)} %copy-done.3) | copy-start | bytes 9437188
  81.4 7.0 %collective-permute-start.6 = (bf16[512,2048]{1,0:T(8,128)(2,1)}, bf16[512,2048]{1,0:T(8,128)(2,1)S(1)}, u32[]{:S(2)}, u32[]{:S(2)}) collective-permute-start(bf16[512,2048]{1,0:T(8,128)(2,1)} %bitcast.6.refs_1_.refs_2_), channel_id=1, source_target_pairs={{0,1},{1,0},{2,3},{3,2},{4,5},{5,4},{6,7},{7,6},{8,9},{9,8},{10,11... | collective-permute-start | bytes 6291464 | tf_op jit(solution)/shard_map/ppermute | solution.py:354
  87.8 2.6 %copy-start.10 = (bf16[768,2048]{1,0:T(8,128)(2,1)S(1)}, bf16[768,2048]{1,0:T(8,128)(2,1)}, u32[]{:S(2)}) copy-start(bf16[768,2048]{1,0:T(8,128)(2,1)} %copy-done.9) | copy-start | bytes 9437188
  88.4 1.4 %copy-start.5 = (bf16[512,2048]{1,0:T(8,128)(2,1)}, bf16[512,2048]{1,0:T(8,128)(2,1)S(1)}, u32[]{:S(2)}) copy-start(bf16[512,2048]{1,0:T(8,128)(2,1)S(1)} %collective-permute-done.6.other_ref.refs_3_) | copy-start | bytes 6291460
  89.8 2.4 %copy-start.8 = (bf16[768,2048]{1,0:T(8,128)(2,1)S(1)}, bf16[768,2048]{1,0:T(8,128)(2,1)}, u32[]{:S(2)}) copy-start(bf16[768,2048]{1,0:T(8,128)(2,1)} %copy-done.7) | copy-start | bytes 9437188
  89.8 2.4 %collective-permute-start.7 = (bf16[512,768]{1,0:T(8,128)(2,1)S(1)}, bf16[512,768]{1,0:T(8,128)(2,1)S(1)}, u32[]{:S(2)}, u32[]{:S(2)}) collective-permute-start(bf16[512,768]{1,0:T(8,128)(2,1)S(1)} %get-tuple-element.55.deltas_ref.refs_4_), channel_id=1, source_target_pairs={{0,1},{1,0},{2,3},{3,2},{4,5},{5,4},{6,7},{7,6},{8,9},{9,8},{10,11... | collective-permute-start | bytes 2359304 | tf_op jit(solution)/shard_map/ppermute | solution.py:354
  94.9 34.1 %all-to-all-start.2 = ((bf16[64,8,2176]{2,1,0:T(8,128)(2,1)}), bf16[64,8,2176]{2,1,0:T(8,128)(2,1)S(1)}, u32[]{:S(2)}, u32[]{:S(2)}) async-start(bf16[64,8,2176]{2,1,0:T(8,128)(2,1)} %bitcast.18), calls=%async_computation.2 | async-start | bytes 4456448 | tf_op jit(solution)/shard_map/all_to_all | solution.py:357
  100.2 1.6 %copy-start.6 = (bf16[512,2048]{1,0:T(8,128)(2,1)S(1)}, bf16[512,2048]{1,0:T(8,128)(2,1)}, u32[]{:S(2)}) copy-start(bf16[512,2048]{1,0:T(8,128)(2,1)} %copy-done.5) | copy-start | bytes 6291460
  128.9 0.9 copy-start.16
  130.5 3.9 %collective-permute-start.9 = (f32[4,16]{1,0:T(4,128)S(1)}, f32[4,16]{1,0:T(4,128)S(1)}, u32[]{:S(2)}, u32[]{:S(2)}) collective-permute-start(f32[4,16]{1,0:T(4,128)S(1)} %get-tuple-element.65), channel_id=1, source_target_pairs={{0,1},{1,0},{2,3},{3,2},{4,5},{5,4},{6,7},{7,6},{8,9},{9,8},{10,11... | collective-permute-start | bytes 776 | tf_op jit(solution)/shard_map/ppermute | solution.py:354
  133.6 1.4 %collective-permute-start.8 = (bf16[16,2048]{1,0:T(8,128)(2,1)S(1)}, bf16[16,2048]{1,0:T(8,128)(2,1)S(1)}, u32[]{:S(2)}, u32[]{:S(2)}) collective-permute-start(bf16[16,2048]{1,0:T(8,128)(2,1)S(1)} %get-tuple-element.63), channel_id=1, source_target_pairs={{0,1},{1,0},{2,3},{3,2},{4,5},{5,4},{6,7},{7,6},{8,9},{9,8},{10,11... | collective-permute-start | bytes 196616 | tf_op jit(solution)/shard_map/ppermute | solution.py:354
  (2 other events, 1.6 us)

commit v5 on v4

--- a/solution.py
+++ b/solution.py
@@ -429,7 +429,7 @@
         [((lines, half + META), BF16)],
         place, parts_other, deltas_other, part, score,
         direct=1,
-        scratch=[pltpu.VMEM((half // step, lines, step), BF16), pltpu.SemaphoreType.DMA((half // step + 1,))],
+        scratch=[pltpu.VMEM((half // quarter, lines, quarter), BF16), pltpu.SemaphoreType.DMA((half // quarter + 1,))],
     )[0]
     picks, gate_grad, up_grad, down_grad = call(
         weights_kernel,

time: 136 us -> 136 us (level)
  no operation moved by 1% of the time
where the time goes in v5:
time: 136 us
  waiting for transfers between devices  46.4 us (34%)
  Pallas kernels  37.1 us (27%)
  starting transfers between devices  34.3 us (25%)
  local copies, waits for them, and re-layouts  15.9 us (12%)
    all_to_all x3, waiting for transfers between devices, deliver(): lax.all_to_all(x.reshape(chips, SLOTS, x.shape[1]), CHIPS, split_axis=0,...  39.8 us
    pallas_call x6, Pallas kernels, call(): pl.pallas_call(body, in_specs=[SMEM] + [HBM] * (raw + given) + [VMEM] * n...  26.1 us
    all_to_all x3, starting transfers between devices, deliver(): lax.all_to_all(x.reshape(chips, SLOTS, x.shape[1]), CHIPS, split_axis=0,...  22.5 us
    unnamed x42, local copies, waits for them, and re-layouts  15.9 us
    ppermute x10, starting transfers between devices, swap(): return lax.ppermute(x, 'core', [(0, 1), (1, 0)])  11.7 us
    pallas_call x5, Pallas kernels, call_near(): pl.pallas_call(kernel, in_specs=[SMEM] + [VMEM] * len(args), out_specs=[V...  11.1 us
    ppermute x10, waiting for transfers between devices, swap(): return lax.ppermute(x, 'core', [(0, 1), (1, 0)])  6.58 us
  transfers between devices with their start and end apart: 13, of which 8 were waited for; matrix products, arithmetic and copies ran while one was open for 0% of the time, Pallas kernels for 22%

profile of v5, /device:TPU:1, one launch (start us, length us, event | category | flops | bytes accessed | tf_op | source)
XLA Modules:
  0.0 135.8 jit_solution(1899030064855518950)
XLA Ops:
  0.6 1.5 %collective-permute-start.1 = (bf16[16,4096]{1,0:T(8,128)(2,1)}, bf16[16,4096]{1,0:T(8,128)(2,1)S(1)}, u32[]{:S(2)}, u32[]{:S(2)}) collective-permute-start(bf16[16,4096]{1,0:T(8,128)(2,1)} %refs_1_.3), channel_id=1, source_target_pairs={{0,1},{1,0},{2,3},{3,2},{4,5},{5,4},{6,7},{7,6},{8,9},{9,8},{10,11... | collective-permute-start | bytes 393224 | tf_op jit(solution)/shard_map/ppermute | solution.py:354
  2.2 1.3 collective-permute-done.refs_2_.refs_1_
  3.5 2.9 %build_rows.1 = bf16[512,2048]{1,0:T(8,128)(2,1)} custom-call(s32[1]{0:T(128)} %bitcast.place_ref, s32[4,16]{1,0:T(4,128)} %bitcast.16, bf16[16,4096]{1,0:T(8,128)(2,1)} %refs_1_.3, s32[4,16]{1,0:T(4,128)S(1)} %collective-permute-done.refs_2_.refs_1_, bf16[16,4096]{1,0:T(8,128)(2,1)S(1)} %collective-permute-done.1.refs_3_), custom_call_target="tpu_custom_call" | custom-call | tf_op jit(solution)/shard_map/build_rows/pallas_call | solution.py:85
  6.4 11.5 %all-to-all-start = ((bf16[64,8,2048]{2,1,0:T(8,128)(2,1)}), bf16[64,8,2048]{2,1,0:T(8,128)(2,1)}, u32[]{:S(2)}, u32[]{:S(2)}) async-start(bf16[64,8,2048]{2,1,0:T(8,128)(2,1)} %bitcast.19), calls=%async_computation | async-start | bytes 4194304 | tf_op jit(solution)/shard_map/all_to_all | solution.py:357
  18.6 1.1 collective-permute-done.2.refs_3_
  19.6 3.7 %build_grads.1 = (bf16[160,512]{1,0:T(8,128)(2,1)}, bf16[512,2048]{1,0:T(8,128)(2,1)}) custom-call(s32[1]{0:T(128)} %bitcast.place_ref, s32[4,16]{1,0:T(4,128)S(1)} %bitcast.17, s32[4,16]{1,0:T(4,128)S(1)} %collective-permute-done.refs_2_.refs_1_, f32[4,16]{1,0:T(4,128)S(1)} %bitcast.14, f32[4,16]{1,0:T(4,128)S(1)} %collective-permute-done.2.refs_3_, ...), custom_call_target="tpu_custom_call" | custom-call | tf_op jit(solution)/shard_map/build_grads/pallas_call | solution.py:85
  23.4 1.9 %copy-done.1 = bf16[1,4096,384]{2,1,0:T(8,128)(2,1)S(1)} copy-done((bf16[1,4096,384]{2,1,0:T(8,128)(2,1)S(1)}, bf16[1,4096,384]{2,1,0:T(8,128)(2,1)}, u32[]{:S(2)}) %copy-start.1) | copy-done | bytes 3145752
  25.8 1.7 %copy-done.12 = bf16[2048,768]{1,0:T(8,128)(2,1)} copy-done((bf16[2048,768]{1,0:T(8,128)(2,1)}, bf16[2048,768]{1,0:T(8,128)(2,1)S(1)}, u32[]{:S(2)}) %copy-start.12) | copy-done | bytes 3145752
  27.5 18.1 %all-to-all-done = bf16[64,8,2048]{2,1,0:T(8,128)(2,1)} async-done(((bf16[64,8,2048]{2,1,0:T(8,128)(2,1)}), bf16[64,8,2048]{2,1,0:T(8,128)(2,1)}, u32[]{:S(2)}, u32[]{:S(2)}) %all-to-all-start) | async-done | bytes 2097184 | tf_op jit(solution)/shard_map/all_to_all | solution.py:357
  45.6 2.8 %collective-permute-start.5 = (bf16[2048,768]{1,0:T(8,128)(2,1)}, bf16[2048,768]{1,0:T(8,128)(2,1)}, u32[]{:S(2)}, u32[]{:S(2)}) collective-permute-start(bf16[2048,768]{1,0:T(8,128)(2,1)} %copy-done.12), channel_id=1, source_target_pairs={{0,1},{1,0},{2,3},{3,2},{4,5},{5,4},{6,7},{7,6},{8,9},{9,8},{10,11... | collective-permute-start | bytes 9437192 | tf_op jit(solution)/shard_map/ppermute | solution.py:354
  48.4 5.7 %all-to-all-start.1 = ((bf16[64,8,2048]{2,1,0:T(8,128)(2,1)}), bf16[64,8,2048]{2,1,0:T(8,128)(2,1)}, u32[]{:S(2)}, u32[]{:S(2)}) async-start(bf16[64,8,2048]{2,1,0:T(8,128)(2,1)} %bitcast.20), calls=%async_computation.1 | async-start | bytes 4194304 | tf_op jit(solution)/shard_map/all_to_all | solution.py:357
  54.1 2.9 %collective-permute-done.4.refs_3_.refs_1_ = bf16[512,2048]{1,0:T(8,128)(2,1)} collective-permute-done((bf16[512,2048]{1,0:T(8,128)(2,1)}, bf16[512,2048]{1,0:T(8,128)(2,1)}, u32[]{:S(2)}, u32[]{:S(2)}) %collective-permute-start.4) | collective-permute-done | bytes 2097184 | tf_op jit(solution)/shard_map/ppermute | solution.py:354
  57.0 1.9 %copy-done.2 = bf16[1,4096,384]{2,1,0:T(8,128)(2,1)S(1)} copy-done((bf16[1,4096,384]{2,1,0:T(8,128)(2,1)S(1)}, bf16[1,4096,384]{2,1,0:T(8,128)(2,1)}, u32[]{:S(2)}) %copy-start.2) | copy-done | bytes 3145752
  58.9 6.9 %gate_up.1 = (f32[512,768]{1,0:T(8,128)S(1)}, bf16[512,384]{1,0:T(8,128)(2,1)S(1)}) custom-call(s32[1]{0:T(128)} %bitcast.place_ref, bf16[1,4096,384]{2,1,0:T(8,128)(2,1)S(1)} %copy-done, bf16[1,4096,384]{2,1,0:T(8,128)(2,1)S(1)} %copy-done.2, bf16[512,2048]{1,0:T(8,128)(2,1)} %bitcast.3.refs_2_.refs_0_, bf16[512,2048]{1,0:T(8,128)(2,1)} %collective-permute-done.4.refs_3_.refs_1_), custom_call_target="tpu_custom_call" | custom-call | tf_op jit(solution)/shard_map/gate_up/pallas_call | solution.py:85
  65.8 1.2 copy-done.13
  67.1 4.5 %turn.1 = (bf16[4096,384]{1,0:T(8,128)(2,1)S(1)}, bf16[768,2048]{1,0:T(8,128)(2,1)S(1)}, bf16[768,2048]{1,0:T(8,128)(2,1)S(1)}) custom-call(s32[1]{0:T(128)} %bitcast.place_ref, bf16[1,4096,384]{2,1,0:T(8,128)(2,1)S(1)} %copy-done, bf16[1,4096,384]{2,1,0:T(8,128)(2,1)S(1)} %copy-done.2, bf16[1,384,4096]{2,1,0:T(8,128)(2,1)S(1)} %copy-done.11, ...), custom_call_target="tpu_custom_call" | custom-call | tf_op jit(solution)/shard_map/turn/pallas_call | solution.py:100
  71.6 1.7 %copy-done.3 = bf16[4096,384]{1,0:T(8,128)(2,1)} copy-done((bf16[4096,384]{1,0:T(8,128)(2,1)}, bf16[4096,384]{1,0:T(8,128)(2,1)S(1)}, u32[]{:S(2)}) %copy-start.3) | copy-done | bytes 3145752
  73.2 1.7 %copy-done.7 = bf16[768,2048]{1,0:T(8,128)(2,1)} copy-done((bf16[768,2048]{1,0:T(8,128)(2,1)}, bf16[768,2048]{1,0:T(8,128)(2,1)S(1)}, u32[]{:S(2)}) %copy-start.7) | copy-done | bytes 3145752
  74.9 1.7 %copy-done.9 = bf16[768,2048]{1,0:T(8,128)(2,1)} copy-done((bf16[768,2048]{1,0:T(8,128)(2,1)}, bf16[768,2048]{1,0:T(8,128)(2,1)S(1)}, u32[]{:S(2)}) %copy-start.9) | copy-done | bytes 3145752
  76.5 4.8 %all-to-all-done.1 = bf16[64,8,2048]{2,1,0:T(8,128)(2,1)} async-done(((bf16[64,8,2048]{2,1,0:T(8,128)(2,1)}), bf16[64,8,2048]{2,1,0:T(8,128)(2,1)}, u32[]{:S(2)}, u32[]{:S(2)}) %all-to-all-start.1) | async-done | bytes 2097184 | tf_op jit(solution)/shard_map/all_to_all | solution.py:357
  81.4 3.0 %collective-permute-start.6 = (bf16[512,2048]{1,0:T(8,128)(2,1)}, bf16[512,2048]{1,0:T(8,128)(2,1)S(1)}, u32[]{:S(2)}, u32[]{:S(2)}) collective-permute-start(bf16[512,2048]{1,0:T(8,128)(2,1)} %bitcast.6.refs_1_.refs_2_), channel_id=1, source_target_pairs={{0,1},{1,0},{2,3},{3,2},{4,5},{5,4},{6,7},{7,6},{8,9},{9,8},{10,11... | collective-permute-start | bytes 6291464 | tf_op jit(solution)/shard_map/ppermute | solution.py:354
  84.4 3.4 %back_early.1.sum_ref = f32[512,384]{1,0:T(8,128)S(1)} custom-call(s32[1]{0:T(128)} %bitcast.place_ref, bf16[4096,384]{1,0:T(8,128)(2,1)} %copy-done.3, bf16[512,2048]{1,0:T(8,128)(2,1)} %bitcast.6.refs_1_.refs_2_), custom_call_target="tpu_custom_call" | custom-call | tf_op jit(solution)/shard_map/back_early/pallas_call | solution.py:85
  88.4 1.4 %back_late.1 = (bf16[512,768]{1,0:T(8,128)(2,1)S(1)}, bf16[512,128]{1,0:T(8,128)(2,1)S(1)}) custom-call(s32[1]{0:T(128)} %bitcast.place_ref, bf16[4096,384]{1,0:T(8,128)(2,1)S(1)} %copy-done.4, bf16[512,2048]{1,0:T(8,128)(2,1)S(1)} %collective-permute-done.6.other_ref.refs_3_, f32[512,384]{1,0:T(8,128)S(1)} %back_early.1.sum_ref, f32[512,768]{1,0:T(8,128)S(1)} %copy-done.14, ...), custom_call_target="tpu_custom_call" | custom-call | tf_op jit(solution)/shard_map/back_late/pallas_call | solution.py:100
  90.4 1.8 %parts_own.1.before_ref = bf16[512,2048]{1,0:T(8,128)(2,1)S(1)} custom-call(s32[1]{0:T(128)} %bitcast.place_ref, bf16[768,2048]{1,0:T(8,128)(2,1)S(1)} %copy-done.10, bf16[512,768]{1,0:T(8,128)(2,1)S(1)} %get-tuple-element.55.deltas_ref.refs_4_), custom_call_target="tpu_custom_call" | custom-call | tf_op jit(solution)/shard_map/parts_own/pallas_call | solution.py:100
  92.2 2.8 %parts_sum.1 = bf16[512,2176]{1,0:T(8,128)(2,1)} custom-call(s32[1]{0:T(128)} %bitcast.place_ref, bf16[768,2048]{1,0:T(8,128)(2,1)S(1)} %copy-done.8, bf16[512,768]{1,0:T(8,128)(2,1)S(1)} %collective-permute-done.7.deltas_ref, bf16[512,2048]{1,0:T(8,128)(2,1)S(1)} %parts_own.1.before_ref, bf16[512,128]{1,0:T(8,128)(2,1)S(1)} %get-tuple-element.59.score_ref), custom_call_target="tpu_custom_call" | custom-call | tf_op jit(solution)/shard_map/parts_sum/pallas_call | solution.py:100
  95.0 5.3 %all-to-all-start.2 = ((bf16[64,8,2176]{2,1,0:T(8,128)(2,1)}), bf16[64,8,2176]{2,1,0:T(8,128)(2,1)S(1)}, u32[]{:S(2)}, u32[]{:S(2)}) async-start(bf16[64,8,2176]{2,1,0:T(8,128)(2,1)} %bitcast.18), calls=%async_computation.2 | async-start | bytes 4456448 | tf_op jit(solution)/shard_map/all_to_all | solution.py:357
  100.3 1.6 %copy-done.6 = bf16[512,2048]{1,0:T(8,128)(2,1)S(1)} copy-done((bf16[512,2048]{1,0:T(8,128)(2,1)S(1)}, bf16[512,2048]{1,0:T(8,128)(2,1)}, u32[]{:S(2)}) %copy-start.6) | copy-done | bytes 2097176
  101.9 0.9 copy-done.17
  102.8 8.6 %weight_grads.1 = (bf16[160,512]{1,0:T(8,128)(2,1)S(1)}, bf16[1,4096,384]{2,1,0:T(8,128)(2,1)}, bf16[1,4096,384]{2,1,0:T(8,128)(2,1)}, bf16[1,384,4096]{2,1,0:T(8,128)(2,1)}) custom-call(s32[1]{0:T(128)} %bitcast.place_ref, bf16[512,2048]{1,0:T(8,128)(2,1)} %bitcast.3.refs_2_.refs_0_, bf16[512,2048]{1,0:T(8,128)(2,1)} %collective-permute-done.4.refs_3_.refs_1_, ...), custom_call_target="tpu_custom_call" | custom-call | tf_op jit(solution)/shard_map/weight_grads/pallas_call | solution.py:85
  112.1 17.0 %all-to-all-done.2 = bf16[64,8,2176]{2,1,0:T(8,128)(2,1)S(1)} async-done(((bf16[64,8,2176]{2,1,0:T(8,128)(2,1)}), bf16[64,8,2176]{2,1,0:T(8,128)(2,1)S(1)}, u32[]{:S(2)}, u32[]{:S(2)}) %all-to-all-start.2) | async-done | bytes 2228256 | tf_op jit(solution)/shard_map/all_to_all | solution.py:357
  129.1 0.9 copy-done.16
  130.6 3.1 %collective-permute-start.9 = (f32[4,16]{1,0:T(4,128)S(1)}, f32[4,16]{1,0:T(4,128)S(1)}, u32[]{:S(2)}, u32[]{:S(2)}) collective-permute-start(f32[4,16]{1,0:T(4,128)S(1)} %get-tuple-element.65), channel_id=1, source_target_pairs={{0,1},{1,0},{2,3},{3,2},{4,5},{5,4},{6,7},{7,6},{8,9},{9,8},{10,11... | collective-permute-start | bytes 776 | tf_op jit(solution)/shard_map/ppermute | solution.py:354
  (49 shorter events, 5.9 us)
Async XLA Ops:
  0.6 2.9 %collective-permute-start.1 = (bf16[16,4096]{1,0:T(8,128)(2,1)}, bf16[16,4096]{1,0:T(8,128)(2,1)S(1)}, u32[]{:S(2)}, u32[]{:S(2)}) collective-permute-start(bf16[16,4096]{1,0:T(8,128)(2,1)} %refs_1_.3), channel_id=1, source_target_pairs={{0,1},{1,0},{2,3},{3,2},{4,5},{5,4},{6,7},{7,6},{8,9},{9,8},{10,11... | collective-permute-start | bytes 393224 | tf_op jit(solution)/shard_map/ppermute | solution.py:354
  2.1 1.4 %collective-permute-start = (s32[4,16]{1,0:T(4,128)}, s32[4,16]{1,0:T(4,128)S(1)}, u32[]{:S(2)}, u32[]{:S(2)}) collective-permute-start(s32[4,16]{1,0:T(4,128)} %bitcast.15), channel_id=1, source_target_pairs={{0,1},{1,0},{2,3},{3,2},{4,5},{5,4},{6,7},{7,6},{8,9},{9,8},{10,11... | collective-permute-start | bytes 776 | tf_op jit(solution)/shard_map/ppermute | solution.py:354
  3.5 14.4 %copy-start.18 = (bf16[16,4096]{1,0:T(8,128)(2,1)S(1)}, bf16[16,4096]{1,0:T(8,128)(2,1)}, u32[]{:S(2)}) copy-start(bf16[16,4096]{1,0:T(8,128)(2,1)} %refs_4_) | copy-start | bytes 393220
  3.5 15.0 %copy-start.19 = (f32[16,4]{0,1:T(4,128)S(1)}, f32[16,4]{0,1:T(4,128)}, u32[]{:S(2)}) copy-start(f32[16,4]{0,1:T(4,128)} %param.9) | copy-start | bytes 772
  3.5 16.1 %copy-start.20 = (s32[16,4]{0,1:T(4,128)S(1)}, s32[16,4]{0,1:T(4,128)}, u32[]{:S(2)}) copy-start(s32[16,4]{0,1:T(4,128)} %param.10) | copy-start | bytes 772
  3.5 19.8 %copy-start = (bf16[1,4096,384]{2,1,0:T(8,128)(2,1)S(1)}, bf16[1,4096,384]{2,1,0:T(8,128)(2,1)}, u32[]{:S(2)}) copy-start(bf16[1,4096,384]{2,1,0:T(8,128)(2,1)} %gate_ref.1) | copy-start | bytes 9437188
  6.4 39.2 %all-to-all-start = ((bf16[64,8,2048]{2,1,0:T(8,128)(2,1)}), bf16[64,8,2048]{2,1,0:T(8,128)(2,1)}, u32[]{:S(2)}, u32[]{:S(2)}) async-start(bf16[64,8,2048]{2,1,0:T(8,128)(2,1)} %bitcast.19), calls=%async_computation | async-start | bytes 4194304 | tf_op jit(solution)/shard_map/all_to_all | solution.py:357
  17.9 1.7 %collective-permute-start.3 = (bf16[16,4096]{1,0:T(8,128)(2,1)S(1)}, bf16[16,4096]{1,0:T(8,128)(2,1)S(1)}, u32[]{:S(2)}, u32[]{:S(2)}) collective-permute-start(bf16[16,4096]{1,0:T(8,128)(2,1)S(1)} %copy-done.18), channel_id=1, source_target_pairs={{0,1},{1,0},{2,3},{3,2},{4,5},{5,4},{6,7},{7,6},{8,9},{9,8},{10,11... | collective-permute-start | bytes 393224 | tf_op jit(solution)/shard_map/ppermute | solution.py:354
  18.5 1.2 collective-permute-start.2
  23.4 1.9 %copy-start.1 = (bf16[1,4096,384]{2,1,0:T(8,128)(2,1)S(1)}, bf16[1,4096,384]{2,1,0:T(8,128)(2,1)}, u32[]{:S(2)}) copy-start(bf16[1,4096,384]{2,1,0:T(8,128)(2,1)} %up_ref.1) | copy-start | bytes 9437188
  25.8 1.7 %copy-start.12 = (bf16[2048,768]{1,0:T(8,128)(2,1)}, bf16[2048,768]{1,0:T(8,128)(2,1)S(1)}, u32[]{:S(2)}) copy-start(bf16[2048,768]{1,0:T(8,128)(2,1)S(1)} %lend.1) | copy-start | bytes 9437188
  45.6 21.5 %collective-permute-start.5 = (bf16[2048,768]{1,0:T(8,128)(2,1)}, bf16[2048,768]{1,0:T(8,128)(2,1)}, u32[]{:S(2)}, u32[]{:S(2)}) collective-permute-start(bf16[2048,768]{1,0:T(8,128)(2,1)} %copy-done.12), channel_id=1, source_target_pairs={{0,1},{1,0},{2,3},{3,2},{4,5},{5,4},{6,7},{7,6},{8,9},{9,8},{10,11... | collective-permute-start | bytes 9437192 | tf_op jit(solution)/shard_map/ppermute | solution.py:354
  48.4 8.6 %collective-permute-start.4 = (bf16[512,2048]{1,0:T(8,128)(2,1)}, bf16[512,2048]{1,0:T(8,128)(2,1)}, u32[]{:S(2)}, u32[]{:S(2)}) collective-permute-start(bf16[512,2048]{1,0:T(8,128)(2,1)} %bitcast.3.refs_2_.refs_0_), channel_id=1, source_target_pairs={{0,1},{1,0},{2,3},{3,2},{4,5},{5,4},{6,7},{7,6},{8,9},{9,8},{10,11... | collective-permute-start | bytes 6291464 | tf_op jit(solution)/shard_map/ppermute | solution.py:354
  48.4 33.0 %all-to-all-start.1 = ((bf16[64,8,2048]{2,1,0:T(8,128)(2,1)}), bf16[64,8,2048]{2,1,0:T(8,128)(2,1)}, u32[]{:S(2)}, u32[]{:S(2)}) async-start(bf16[64,8,2048]{2,1,0:T(8,128)(2,1)} %bitcast.20), calls=%async_computation.1 | async-start | bytes 4194304 | tf_op jit(solution)/shard_map/all_to_all | solution.py:357
  57.0 1.9 %copy-start.2 = (bf16[1,4096,384]{2,1,0:T(8,128)(2,1)S(1)}, bf16[1,4096,384]{2,1,0:T(8,128)(2,1)}, u32[]{:S(2)}) copy-start(bf16[1,4096,384]{2,1,0:T(8,128)(2,1)} %up_ref.1) | copy-start | bytes 9437188
  58.9 8.2 %copy-start.11 = (bf16[1,384,4096]{2,1,0:T(8,128)(2,1)S(1)}, bf16[1,384,4096]{2,1,0:T(8,128)(2,1)}, u32[]{:S(2)}) copy-start(bf16[1,384,4096]{2,1,0:T(8,128)(2,1)} %down_ref.1) | copy-start | bytes 9437188
  65.8 1.2 copy-start.13
  71.5 1.7 %copy-start.3 = (bf16[4096,384]{1,0:T(8,128)(2,1)}, bf16[4096,384]{1,0:T(8,128)(2,1)S(1)}, u32[]{:S(2)}) copy-start(bf16[4096,384]{1,0:T(8,128)(2,1)S(1)} %get-tuple-element.49.refs_0_.back_ref) | copy-start | bytes 9437188
  73.2 1.7 %copy-start.7 = (bf16[768,2048]{1,0:T(8,128)(2,1)}, bf16[768,2048]{1,0:T(8,128)(2,1)S(1)}, u32[]{:S(2)}) copy-start(bf16[768,2048]{1,0:T(8,128)(2,1)S(1)} %get-tuple-element.48.turned_ref) | copy-start | bytes 9437188
  74.9 1.7 %copy-start.9 = (bf16[768,2048]{1,0:T(8,128)(2,1)}, bf16[768,2048]{1,0:T(8,128)(2,1)S(1)}, u32[]{:S(2)}) copy-start(bf16[768,2048]{1,0:T(8,128)(2,1)S(1)} %get-tuple-element.56.turned_ref) | copy-start | bytes 9437188
  76.5 11.9 %copy-start.14 = (f32[512,768]{1,0:T(8,128)S(1)}, f32[512,768]{1,0:T(8,128)}, u32[]{:S(2)}) copy-start(f32[512,768]{1,0:T(8,128)} %copy-done.13) | copy-start | bytes 4718596
  81.4 7.0 %copy-start.4 = (bf16[4096,384]{1,0:T(8,128)(2,1)S(1)}, bf16[4096,384]{1,0:T(8,128)(2,1)}, u32[]{:S(2)}) copy-start(bf16[4096,384]{1,0:T(8,128)(2,1)} %copy-done.3) | copy-start | bytes 9437188
  81.4 7.0 %collective-permute-start.6 = (bf16[512,2048]{1,0:T(8,128)(2,1)}, bf16[512,2048]{1,0:T(8,128)(2,1)S(1)}, u32[]{:S(2)}, u32[]{:S(2)}) collective-permute-start(bf16[512,2048]{1,0:T(8,128)(2,1)} %bitcast.6.refs_1_.refs_2_), channel_id=1, source_target_pairs={{0,1},{1,0},{2,3},{3,2},{4,5},{5,4},{6,7},{7,6},{8,9},{9,8},{10,11... | collective-permute-start | bytes 6291464 | tf_op jit(solution)/shard_map/ppermute | solution.py:354
  87.8 2.6 %copy-start.10 = (bf16[768,2048]{1,0:T(8,128)(2,1)S(1)}, bf16[768,2048]{1,0:T(8,128)(2,1)}, u32[]{:S(2)}) copy-start(bf16[768,2048]{1,0:T(8,128)(2,1)} %copy-done.9) | copy-start | bytes 9437188
  88.4 1.4 %copy-start.5 = (bf16[512,2048]{1,0:T(8,128)(2,1)}, bf16[512,2048]{1,0:T(8,128)(2,1)S(1)}, u32[]{:S(2)}) copy-start(bf16[512,2048]{1,0:T(8,128)(2,1)S(1)} %collective-permute-done.6.other_ref.refs_3_) | copy-start | bytes 6291460
  89.8 2.4 %copy-start.8 = (bf16[768,2048]{1,0:T(8,128)(2,1)S(1)}, bf16[768,2048]{1,0:T(8,128)(2,1)}, u32[]{:S(2)}) copy-start(bf16[768,2048]{1,0:T(8,128)(2,1)} %copy-done.7) | copy-start | bytes 9437188
  89.8 2.4 %collective-permute-start.7 = (bf16[512,768]{1,0:T(8,128)(2,1)S(1)}, bf16[512,768]{1,0:T(8,128)(2,1)S(1)}, u32[]{:S(2)}, u32[]{:S(2)}) collective-permute-start(bf16[512,768]{1,0:T(8,128)(2,1)S(1)} %get-tuple-element.55.deltas_ref.refs_4_), channel_id=1, source_target_pairs={{0,1},{1,0},{2,3},{3,2},{4,5},{5,4},{6,7},{7,6},{8,9},{9,8},{10,11... | collective-permute-start | bytes 2359304 | tf_op jit(solution)/shard_map/ppermute | solution.py:354
  95.0 34.1 %all-to-all-start.2 = ((bf16[64,8,2176]{2,1,0:T(8,128)(2,1)}), bf16[64,8,2176]{2,1,0:T(8,128)(2,1)S(1)}, u32[]{:S(2)}, u32[]{:S(2)}) async-start(bf16[64,8,2176]{2,1,0:T(8,128)(2,1)} %bitcast.18), calls=%async_computation.2 | async-start | bytes 4456448 | tf_op jit(solution)/shard_map/all_to_all | solution.py:357
  100.3 1.6 %copy-start.6 = (bf16[512,2048]{1,0:T(8,128)(2,1)S(1)}, bf16[512,2048]{1,0:T(8,128)(2,1)}, u32[]{:S(2)}) copy-start(bf16[512,2048]{1,0:T(8,128)(2,1)} %copy-done.5) | copy-start | bytes 6291460
  129.1 0.9 copy-start.16
  130.6 3.9 %collective-permute-start.9 = (f32[4,16]{1,0:T(4,128)S(1)}, f32[4,16]{1,0:T(4,128)S(1)}, u32[]{:S(2)}, u32[]{:S(2)}) collective-permute-start(f32[4,16]{1,0:T(4,128)S(1)} %get-tuple-element.65), channel_id=1, source_target_pairs={{0,1},{1,0},{2,3},{3,2},{4,5},{5,4},{6,7},{7,6},{8,9},{9,8},{10,11... | collective-permute-start | bytes 776 | tf_op jit(solution)/shard_map/ppermute | solution.py:354
  133.7 1.4 %collective-permute-start.8 = (bf16[16,2048]{1,0:T(8,128)(2,1)S(1)}, bf16[16,2048]{1,0:T(8,128)(2,1)S(1)}, u32[]{:S(2)}, u32[]{:S(2)}) collective-permute-start(bf16[16,2048]{1,0:T(8,128)(2,1)S(1)} %get-tuple-element.63), channel_id=1, source_target_pairs={{0,1},{1,0},{2,3},{3,2},{4,5},{5,4},{6,7},{7,6},{8,9},{9,8},{10,11... | collective-permute-start | bytes 196616 | tf_op jit(solution)/shard_map/ppermute | solution.py:354
  (2 other events, 1.6 us)
